TPU v7x, 32 devices: a whole 2x2x4 slice. The times are simulated.
32 devices in a mesh: dp: 4 (over y, core), blk: 8 (over z, x).
Axes of the slice: x: 2, y: 2, z: 4, core: 2. Of those that a mesh axis runs over, the one named last changes fastest.
Arguments:
- features: bfloat16 [4, 2, 32, 64, 512], P('dp', None, 'blk'), may hold values from -24 to 24
- bounds: int32 [4, 2, 2], P('dp'), may hold values from 1 to 31, as said below
- out_grad: bfloat16 [4, 2, 32, 64, 512], P('dp', None, 'blk'), may hold values from -6 to 6
- norm1_gain: bfloat16 [512], P('blk'), may hold values from 0.5 to 1.5
- norm1_shift: bfloat16 [512], P('blk'), may hold values from -2.5 to 2.5
- conv1_weight: bfloat16 [4608, 512], P('blk', 'dp'), may hold values from -0.09375 to 0.09375
- norm2_gain: bfloat16 [512], P('blk'), may hold values from 0.5 to 1.5
- norm2_shift: bfloat16 [512], P('blk'), may hold values from -2.5 to 2.5
- conv2_weight: bfloat16 [4608, 512], P('blk', 'dp'), may hold values from -0.09375 to 0.09375
- norm3_gain: bfloat16 [512], P('blk'), may hold values from 0.5 to 1.5
- norm3_shift: bfloat16 [512], P('blk'), may hold values from -2.5 to 2.5
- query_weight: bfloat16 [512, 512], P('blk', 'dp'), may hold values from -0.25 to 0.25
- key_weight: bfloat16 [512, 512], P('blk', 'dp'), may hold values from -0.25 to 0.25
- value_weight: bfloat16 [512, 512], P('blk', 'dp'), may hold values from -0.25 to 0.25
- output_weight: bfloat16 [512, 512], P('blk', 'dp'), may hold values from -1.5 to 1.5
Outputs:
- activations: float32 [4, 2, 32, 64, 512], P('dp', None, 'blk')
- input_grad: float32 [4, 2, 32, 64, 512], P('dp', None, 'blk')
- norm1_gain_grad: float32 [512], P('blk')
- norm1_shift_grad: float32 [512], P('blk')
- conv1_grad: float32 [4608, 512], P('blk', 'dp')
- norm2_gain_grad: float32 [512], P('blk')
- norm2_shift_grad: float32 [512], P('blk')
- conv2_grad: float32 [4608, 512], P('blk', 'dp')
- norm3_gain_grad: float32 [512], P('blk')
- norm3_shift_grad: float32 [512], P('blk')
- query_grad: float32 [512, 512], P('blk', 'dp')
- key_grad: float32 [512, 512], P('blk', 'dp')
- value_grad: float32 [512, 512], P('blk', 'dp')
- output_grad: float32 [512, 512], P('blk', 'dp')
Inputs may be any that keep to these rules, and one draw needn't show every extreme that they name: In each micro-batch of each data group canvas 0 holds rows [0, bounds[0]), canvas 1 row [bounds[0], bounds[1]), canvas 2 rows [bounds[1], 32); bounds[0] and 32 - bounds[1] each lie in 1 to 3.
All inputs are finite; a program needn't handle non-finite values.
Results may differ from a plain program's by a relative error of at most 0.015.
Values may be sent and summed in bfloat16 or wider, within the bound.
A program may use at most 384 MiB of HBM per device.

v0:
```python
import jax
import jax.numpy as jnp
from jax import lax
from jax.sharding import PartitionSpec as P

GROUPS = 32
CANVASES = 3


EPSILON = 1e-06
HIGHEST = lax.Precision.HIGHEST
NEGATIVE = -1e30


def extended(shard, sides, width):
    for axis, dim in sides:
        devices, length = (lax.axis_size(axis), shard.shape[dim])
        up = [(i, (i + 1) % devices) for i in range(devices - 1)]
        down = [(j, i) for i, j in up]
        last = lax.slice_in_dim(shard, length - width, length, axis=dim)
        initial = lax.slice_in_dim(shard, 0, width, axis=dim)
        before = lax.ppermute(last, axis, up)
        after = lax.ppermute(initial, axis, down)
        shard = jnp.concatenate([before, shard, after], axis=dim)
    return shard


def canvas_index(global_rows, first_row, second_row):
    return (global_rows >= first_row).astype(jnp.int32) + (global_rows >= second_row).astype(
        jnp.int32
    )


def swish(argument):
    return argument * jax.nn.sigmoid(argument)


def swish_slope(argument):
    sigmoid_value = jax.nn.sigmoid(argument)
    return sigmoid_value * (1.0 + argument * (1.0 - sigmoid_value))


def group_sums(member, grouped):
    return jnp.einsum("rk,rwgc->kg", member, grouped, precision=HIGHEST)


def spread_rows(member, lookup):
    return jnp.dot(member, lookup, precision=HIGHEST)


def norm_forward(inputs, member, counts, norm_gain, norm_shift):
    row_count, width, channels = inputs.shape
    grouped = inputs.reshape(row_count, width, GROUPS, channels // GROUPS)
    totals, square = lax.psum(
        (group_sums(member, grouped), group_sums(member, grouped * grouped)), "blk"
    )
    average = totals / counts[:, None]
    inverse = lax.rsqrt(square / counts[:, None] - average * average + EPSILON)
    average_rows = spread_rows(member, average)
    scale_rows = spread_rows(member, inverse)
    normal = (grouped - average_rows[:, None, :, None]) * scale_rows[:, None, :, None]
    normal = normal.reshape(row_count, width, channels)
    return (normal * norm_gain + norm_shift, normal, scale_rows)


def norm_backward(incoming, normal, scale_rows, member, counts, norm_gain):
    row_count, width, channels = incoming.shape
    gain_grad = jnp.sum(incoming * normal, axis=(0, 1))
    shift_grad = jnp.sum(incoming, axis=(0, 1))
    scaled = (incoming * norm_gain).reshape(row_count, width, GROUPS, channels // GROUPS)
    grouped_normal = normal.reshape(row_count, width, GROUPS, channels // GROUPS)
    first_sum, second_sum = lax.psum(
        (group_sums(member, scaled), group_sums(member, scaled * grouped_normal)), "blk"
    )
    first_rows = spread_rows(member, first_sum / counts[:, None])
    second_rows = spread_rows(member, second_sum / counts[:, None])
    result = scale_rows[:, None, :, None] * (
        scaled - first_rows[:, None, :, None] - grouped_normal * second_rows[:, None, :, None]
    )
    return (result.reshape(row_count, width, channels), gain_grad, shift_grad)


def gather_taps(padded, seg_pad, seg_rows, direction):
    row_count = seg_rows.shape[0]
    width = padded.shape[1]
    widened = jnp.pad(padded, ((0, 0), (1, 1), (0, 0)))
    pieces = []
    for step_row in (-1, 0, 1):
        low_row = 1 + direction * step_row
        allowed = (seg_pad[low_row : low_row + row_count] == seg_rows).astype(padded.dtype)[
            :, None, None
        ]
        for step_col in (-1, 0, 1):
            low_col = 1 + direction * step_col
            pieces.append(
                widened[low_row : low_row + row_count, low_col : low_col + width, :] * allowed
            )
    return jnp.stack(pieces, axis=2)


def conv_apply(activation, seg_pad, seg_rows, weight_matrix):
    row_count, width, channels = activation.shape
    padded = extended(activation, (("blk", 0),), 1)
    stacked = gather_taps(padded, seg_pad, seg_rows, 1).reshape(row_count * width, 9 * channels)
    result = jnp.dot(stacked, weight_matrix, preferred_element_type=jnp.float32)
    return (result.reshape(row_count, width, channels), stacked)


def conv_reverse(gradient, stacked, seg_pad, seg_rows, weight_matrix):
    row_count, width, channels = gradient.shape
    flattened = gradient.reshape(row_count * width, channels)
    weight_grad = lax.dot_general(
        stacked, flattened, (((0,), (0,)), ((), ())), preferred_element_type=jnp.float32
    )
    padded = extended(gradient, (("blk", 0),), 1)
    mirrored = gather_taps(padded, seg_pad, seg_rows, -1).reshape(row_count * width, 9, channels)
    kernel = weight_matrix.reshape(9, channels, channels)
    result = lax.dot_general(
        mirrored, kernel, (((1, 2), (0, 2)), ((), ())), preferred_element_type=jnp.float32
    )
    return (result.reshape(row_count, width, channels), weight_grad)


def attention_forward(
    queries, keys_local, values_local, token_seg, first_row, second_row, width, scale
):
    token_count, channels = queries.shape

    def absorb(running, portion, offset):
        key_block, value_block = portion
        maximum, totals, accumulated = running
        key_seg = canvas_index(
            jnp.arange(key_block.shape[0], dtype=jnp.int32) // width, first_row, second_row
        )
        shared = token_seg[:, None] == key_seg[None, :]
        scores = (
            lax.dot_general(
                queries, key_block, (((1,), (1,)), ((), ())), preferred_element_type=jnp.float32
            )
            * scale
        )
        masked = jnp.where(shared, scores, NEGATIVE)
        new_maximum = jnp.maximum(maximum, jnp.max(masked, axis=1))
        weights = jnp.where(shared, jnp.exp(masked - new_maximum[:, None]), 0.0)
        totals = jnp.sum(weights, axis=1)
        accumulated = jnp.dot(
            weights.astype(jnp.bfloat16), value_block, preferred_element_type=jnp.float32
        )
        return (new_maximum, totals, accumulated)

    initial = (
        jnp.full((token_count,), NEGATIVE, jnp.float32),
        jnp.zeros((token_count,), jnp.float32),
        jnp.zeros((token_count, channels), jnp.float32),
    )
    maximum, totals, accumulated = absorb(
        initial,
        (
            lax.all_gather(keys_local, "blk", axis=0, tiled=True),
            lax.all_gather(values_local, "blk", axis=0, tiled=True),
        ),
        jnp.int32(0),
    )
    return (accumulated / totals[:, None], maximum + jnp.log(totals))


def attention_query_grad(
    queries,
    heads_grad,
    log_total,
    correction,
    keys_local,
    values_local,
    token_seg,
    first_row,
    second_row,
    width,
    scale,
):

    def absorb(running, portion, offset):
        key_block, value_block = portion
        key_seg = canvas_index(
            jnp.arange(key_block.shape[0], dtype=jnp.int32) // width, first_row, second_row
        )
        shared = token_seg[:, None] == key_seg[None, :]
        scores = (
            lax.dot_general(
                queries, key_block, (((1,), (1,)), ((), ())), preferred_element_type=jnp.float32
            )
            * scale
        )
        weights = jnp.where(
            shared, jnp.exp(jnp.where(shared, scores, NEGATIVE) - log_total[:, None]), 0.0
        )
        slopes = lax.dot_general(
            heads_grad, value_block, (((1,), (1,)), ((), ())), preferred_element_type=jnp.float32
        )
        score_grad = (weights * (slopes - correction[:, None])).astype(jnp.bfloat16)
        return jnp.dot(score_grad, key_block, preferred_element_type=jnp.float32) * scale

    return absorb(
        jnp.zeros(queries.shape, jnp.float32),
        (
            lax.all_gather(keys_local, "blk", axis=0, tiled=True),
            lax.all_gather(values_local, "blk", axis=0, tiled=True),
        ),
        jnp.int32(0),
    )


def attention_key_grad(
    queries,
    heads_grad,
    log_total,
    correction,
    keys_local,
    values_local,
    token_seg,
    first_row,
    second_row,
    width,
    scale,
):

    def absorb(running, portion, offset):
        query_part, upstream_part, total_part, correct_part = portion
        query_seg = canvas_index(
            jnp.arange(query_part.shape[0], dtype=jnp.int32) // width, first_row, second_row
        )
        query_low = query_part.astype(jnp.bfloat16)
        upstream_low = upstream_part.astype(jnp.bfloat16)
        shared = query_seg[:, None] == token_seg[None, :]
        scores = (
            lax.dot_general(
                query_low, keys_local, (((1,), (1,)), ((), ())), preferred_element_type=jnp.float32
            )
            * scale
        )
        weights = jnp.where(
            shared, jnp.exp(jnp.where(shared, scores, NEGATIVE) - total_part[:, None]), 0.0
        )
        value_acc = lax.dot_general(
            weights.astype(jnp.bfloat16),
            upstream_low,
            (((0,), (0,)), ((), ())),
            preferred_element_type=jnp.float32,
        )
        slopes = lax.dot_general(
            upstream_low, values_local, (((1,), (1,)), ((), ())), preferred_element_type=jnp.float32
        )
        score_grad = (weights * (slopes - correct_part[:, None])).astype(jnp.bfloat16)
        key_acc = (
            lax.dot_general(
                score_grad, query_low, (((0,), (0,)), ((), ())), preferred_element_type=jnp.float32
            )
            * scale
        )
        return (key_acc, value_acc)

    empty = jnp.zeros(keys_local.shape, jnp.float32)
    return absorb(
        (empty, empty),
        (
            lax.all_gather(queries.astype(jnp.float32), "blk", axis=0, tiled=True),
            lax.all_gather(heads_grad.astype(jnp.float32), "blk", axis=0, tiled=True),
            lax.all_gather(log_total, "blk", axis=0, tiled=True),
            lax.all_gather(correction, "blk", axis=0, tiled=True),
        ),
        jnp.int32(0),
    )


def collect(
    conv1_weight,
    conv2_weight,
    query_weight,
    key_weight,
    value_weight,
    output_weight,
    norm1_gain,
    norm1_shift,
    norm2_gain,
    norm2_shift,
    norm3_gain,
    norm3_shift,
):
    row_parts = (
        lax.all_gather(conv1_weight, "blk", axis=0, tiled=True),
        lax.all_gather(conv2_weight, "blk", axis=0, tiled=True),
        lax.all_gather(query_weight, "blk", axis=0, tiled=True),
        lax.all_gather(key_weight, "blk", axis=0, tiled=True),
        lax.all_gather(value_weight, "blk", axis=0, tiled=True),
        lax.all_gather(output_weight, "blk", axis=0, tiled=True),
        lax.all_gather(norm1_gain, "blk", axis=0, tiled=True),
        lax.all_gather(norm1_shift, "blk", axis=0, tiled=True),
        lax.all_gather(norm2_gain, "blk", axis=0, tiled=True),
        lax.all_gather(norm2_shift, "blk", axis=0, tiled=True),
        lax.all_gather(norm3_gain, "blk", axis=0, tiled=True),
        lax.all_gather(norm3_shift, "blk", axis=0, tiled=True),
    )
    full_parts = (
        lax.all_gather(row_parts[0], "dp", axis=1, tiled=True),
        lax.all_gather(row_parts[1], "dp", axis=1, tiled=True),
        lax.all_gather(row_parts[2], "dp", axis=1, tiled=True),
        lax.all_gather(row_parts[3], "dp", axis=1, tiled=True),
        lax.all_gather(row_parts[4], "dp", axis=1, tiled=True),
        lax.all_gather(row_parts[5], "dp", axis=1, tiled=True),
    )
    return (tuple(full_parts), tuple(row_parts[6:]))


def reduce_all(gradients):
    row_sums = (
        lax.psum_scatter(gradients[0], "blk", scatter_dimension=0, tiled=True),
        lax.psum_scatter(gradients[1], "blk", scatter_dimension=0, tiled=True),
        lax.psum_scatter(gradients[2], "blk", scatter_dimension=0, tiled=True),
        lax.psum_scatter(gradients[3], "blk", scatter_dimension=0, tiled=True),
        lax.psum_scatter(gradients[4], "blk", scatter_dimension=0, tiled=True),
        lax.psum_scatter(gradients[5], "blk", scatter_dimension=0, tiled=True),
        lax.psum_scatter(gradients[6], "blk", scatter_dimension=0, tiled=True),
        lax.psum_scatter(gradients[7], "blk", scatter_dimension=0, tiled=True),
        lax.psum_scatter(gradients[8], "blk", scatter_dimension=0, tiled=True),
        lax.psum_scatter(gradients[9], "blk", scatter_dimension=0, tiled=True),
        lax.psum_scatter(gradients[10], "blk", scatter_dimension=0, tiled=True),
        lax.psum_scatter(gradients[11], "blk", scatter_dimension=0, tiled=True),
    )
    matrix_sums = (
        lax.psum_scatter(row_sums[0], "dp", scatter_dimension=1, tiled=True),
        lax.psum_scatter(row_sums[1], "dp", scatter_dimension=1, tiled=True),
        lax.psum_scatter(row_sums[2], "dp", scatter_dimension=1, tiled=True),
        lax.psum_scatter(row_sums[3], "dp", scatter_dimension=1, tiled=True),
        lax.psum_scatter(row_sums[4], "dp", scatter_dimension=1, tiled=True),
        lax.psum_scatter(row_sums[5], "dp", scatter_dimension=1, tiled=True),
    )
    norm_sums = lax.psum(
        (row_sums[6], row_sums[7], row_sums[8], row_sums[9], row_sums[10], row_sums[11]), "dp"
    )
    return tuple(matrix_sums) + tuple(norm_sums)


def one_batch(inputs_low, bound_pair, upstream_low, matrices, norm_params, position, blocks):
    row_count, width, channels = inputs_low.shape
    token_count = row_count * width
    total_rows = row_count * blocks
    scale = channels ** (-0.5)
    first_row = bound_pair[0]
    second_row = bound_pair[1]
    local_rows = position * row_count + jnp.arange(row_count, dtype=jnp.int32)
    padded_rows = position * row_count - 1 + jnp.arange(row_count + 2, dtype=jnp.int32)
    seg_rows = canvas_index(local_rows, first_row, second_row)
    seg_pad = canvas_index(padded_rows, first_row, second_row)
    member = (seg_rows[:, None] == jnp.arange(CANVASES, dtype=jnp.int32)[None, :]).astype(
        jnp.float32
    )
    counts = jnp.stack([first_row, second_row - first_row, total_rows - second_row]).astype(
        jnp.float32
    ) * float(width * (channels // GROUPS))
    gains = [item.astype(jnp.float32) for item in norm_params]
    inputs = inputs_low.astype(jnp.float32)
    norm_one, normal_one, scale_one = norm_forward(inputs, member, counts, gains[0], gains[1])
    act_one = swish(norm_one).astype(jnp.bfloat16)
    hidden_one, stacked_one = conv_apply(act_one, seg_pad, seg_rows, matrices[0])
    norm_two, normal_two, scale_two = norm_forward(hidden_one, member, counts, gains[2], gains[3])
    act_two = swish(norm_two).astype(jnp.bfloat16)
    hidden_two, stacked_two = conv_apply(act_two, seg_pad, seg_rows, matrices[1])
    residual = inputs + hidden_two
    norm_three, normal_three, scale_three = norm_forward(
        residual, member, counts, gains[4], gains[5]
    )
    normed = norm_three.astype(jnp.bfloat16).reshape(token_count, channels)
    queries = jnp.dot(normed, matrices[2], preferred_element_type=jnp.float32).astype(jnp.bfloat16)
    keys_local = jnp.dot(normed, matrices[3], preferred_element_type=jnp.float32).astype(
        jnp.bfloat16
    )
    values_local = jnp.dot(normed, matrices[4], preferred_element_type=jnp.float32).astype(
        jnp.bfloat16
    )
    token_seg = jnp.repeat(seg_rows, width)
    attended, log_total = attention_forward(
        queries, keys_local, values_local, token_seg, first_row, second_row, width, scale
    )
    heads = attended.astype(jnp.bfloat16)
    activation = residual + jnp.dot(heads, matrices[5], preferred_element_type=jnp.float32).reshape(
        row_count, width, channels
    )
    upstream = upstream_low.reshape(token_count, channels)
    output_weight_grad = lax.dot_general(
        heads, upstream, (((0,), (0,)), ((), ())), preferred_element_type=jnp.float32
    )
    heads_grad = lax.dot_general(
        upstream, matrices[5], (((1,), (1,)), ((), ())), preferred_element_type=jnp.float32
    ).astype(jnp.bfloat16)
    correction = jnp.sum(heads_grad.astype(jnp.float32) * attended, axis=1)
    query_sum = attention_query_grad(
        queries,
        heads_grad,
        log_total,
        correction,
        keys_local,
        values_local,
        token_seg,
        first_row,
        second_row,
        width,
        scale,
    )
    key_sum, value_sum = attention_key_grad(
        queries,
        heads_grad,
        log_total,
        correction,
        keys_local,
        values_local,
        token_seg,
        first_row,
        second_row,
        width,
        scale,
    )
    query_low = query_sum.astype(jnp.bfloat16)
    key_low = key_sum.astype(jnp.bfloat16)
    value_low = value_sum.astype(jnp.bfloat16)
    contract_rows = (((0,), (0,)), ((), ()))
    contract_cols = (((1,), (1,)), ((), ()))
    query_weight_grad = lax.dot_general(
        normed, query_low, contract_rows, preferred_element_type=jnp.float32
    )
    key_weight_grad = lax.dot_general(
        normed, key_low, contract_rows, preferred_element_type=jnp.float32
    )
    value_weight_grad = lax.dot_general(
        normed, value_low, contract_rows, preferred_element_type=jnp.float32
    )
    normed_grad = (
        lax.dot_general(query_low, matrices[2], contract_cols, preferred_element_type=jnp.float32)
        + lax.dot_general(key_low, matrices[3], contract_cols, preferred_element_type=jnp.float32)
        + lax.dot_general(value_low, matrices[4], contract_cols, preferred_element_type=jnp.float32)
    )
    back_three, gain_three_grad, shift_three_grad = norm_backward(
        normed_grad.reshape(row_count, width, channels),
        normal_three,
        scale_three,
        member,
        counts,
        gains[4],
    )
    residual_grad = upstream_low.astype(jnp.float32) + back_three
    act_two_grad, conv_two_grad = conv_reverse(
        residual_grad.astype(jnp.bfloat16), stacked_two, seg_pad, seg_rows, matrices[1]
    )
    back_two, gain_two_grad, shift_two_grad = norm_backward(
        act_two_grad * swish_slope(norm_two), normal_two, scale_two, member, counts, gains[2]
    )
    act_one_grad, conv_one_grad = conv_reverse(
        back_two.astype(jnp.bfloat16), stacked_one, seg_pad, seg_rows, matrices[0]
    )
    back_one, gain_one_grad, shift_one_grad = norm_backward(
        act_one_grad * swish_slope(norm_one), normal_one, scale_one, member, counts, gains[0]
    )
    input_grad = residual_grad + back_one
    local_grads = (
        conv_one_grad,
        conv_two_grad,
        query_weight_grad,
        key_weight_grad,
        value_weight_grad,
        output_weight_grad,
        gain_one_grad,
        shift_one_grad,
        gain_two_grad,
        shift_two_grad,
        gain_three_grad,
        shift_three_grad,
    )
    return (activation, input_grad, local_grads)


def shards(
    features,
    bounds,
    out_grad,
    norm1_gain,
    norm1_shift,
    conv1_weight,
    norm2_gain,
    norm2_shift,
    conv2_weight,
    norm3_gain,
    norm3_shift,
    query_weight,
    key_weight,
    value_weight,
    output_weight,
):
    blocks = lax.axis_size("blk")
    position = lax.axis_index("blk")
    micro_count = features.shape[1]
    shard_sums = None
    outputs = []
    input_grads = []
    for micro_index in range(micro_count):
        matrices, norm_params = collect(
            conv1_weight,
            conv2_weight,
            query_weight,
            key_weight,
            value_weight,
            output_weight,
            norm1_gain,
            norm1_shift,
            norm2_gain,
            norm2_shift,
            norm3_gain,
            norm3_shift,
        )
        activation, input_grad, local_grads = one_batch(
            features[0, micro_index],
            bounds[0, micro_index],
            out_grad[0, micro_index],
            matrices,
            norm_params,
            position,
            blocks,
        )
        outputs.append(activation)
        input_grads.append(input_grad)
        reduced = reduce_all(local_grads)
        shard_sums = (
            reduced
            if shard_sums is None
            else tuple((acc + new for acc, new in zip(shard_sums, reduced)))
        )
    activations = jnp.stack(outputs)[None]
    input_grad_all = jnp.stack(input_grads)[None]
    return (
        activations,
        input_grad_all,
        shard_sums[6],
        shard_sums[7],
        shard_sums[0],
        shard_sums[8],
        shard_sums[9],
        shard_sums[1],
        shard_sums[10],
        shard_sums[11],
        shard_sums[2],
        shard_sums[3],
        shard_sums[4],
        shard_sums[5],
    )


def solution(mesh):
    in_specs = (
        P("dp", None, "blk", None, None),
        P("dp", None, None),
        P("dp", None, "blk", None, None),
        P("blk"),
        P("blk"),
        P("blk", "dp"),
        P("blk"),
        P("blk"),
        P("blk", "dp"),
        P("blk"),
        P("blk"),
        P("blk", "dp"),
        P("blk", "dp"),
        P("blk", "dp"),
        P("blk", "dp"),
    )
    out_specs = (
        P("dp", None, "blk", None, None),
        P("dp", None, "blk", None, None),
        P("blk"),
        P("blk"),
        P("blk", "dp"),
        P("blk"),
        P("blk"),
        P("blk", "dp"),
        P("blk"),
        P("blk"),
        P("blk", "dp"),
        P("blk", "dp"),
        P("blk", "dp"),
        P("blk", "dp"),
    )
    return jax.shard_map(shards, mesh=mesh, in_specs=in_specs, out_specs=out_specs, check_vma=False)
```

profile of v0, /device:TPU:0, one launch (start us, length us, event | category | flops | bytes accessed | tf_op | source)
XLA Modules:
  0.0 1405.5 jit_solution(282269957229691629)
XLA Ops:
  15.8 23.3 %all-reduce.27 = (bf16[512]{0:T(512)(128)(2,1)S(1)}, bf16[512]{0:T(512)(128)(2,1)S(1)}, bf16[512]{0:T(512)(128)(2,1)S(1)}, bf16[512]{0:T(512)(128)(2,1)S(1)}, bf...) all-reduce(bf16[512]{0:T(512)(128)(2,1)S(1)} %dynamic-update-slice.1, ...), channel_id=1, replica_groups=mesh['dp'=4,'blk'=8] {'blk'}, use_global_device_ids=true, to_apply=%add.9 | all-reduce | flops 3072 | bytes 12288
  56.7 19.6 %all-reduce.25 = (f32[3,32]{1,0:T(4,128)S(1)}, f32[3,32]{1,0:T(4,128)S(1)}, f32[3,32]{1,0:T(4,128)S(1)}, f32[3,32]{1,0:T(4,128)S(1)}) all-reduce(f32[3,32]{1,0:T(4,128)S(1)} %fusion.336, f32[3,32]{1,0:T(4,128)S(1)} %fusion.338, f32[3,32]{1,0:T(4,128)S(1)} %fusion.365, f32[3,32]{1,0:T(4,128)S(1)} %fusion.367), channel_id=1, replica_groups=mesh['dp'=4,'blk'=8] {'blk'}, use_global_device_ids=true, to_apply=%region_23.24 | all-reduce | flops 384 | bytes 3072 | tf_op jit(solution)/shard_map/psum | solution.py:54
  91.5 30.5 %all_gather.124 = bf16[512,128]{1,0:T(8,128)(2,1)S(1)} all-gather(bf16[64,128]{1,0:T(8,128)(2,1)S(1)} %copy-done.131), channel_id=1, replica_groups=mesh['dp'=4,'blk'=8] {'blk'}, dimensions={0}, use_global_device_ids=true | all-gather | bytes 147456 | tf_op jit(solution)/shard_map/all_gather | solution.py:292
  170.3 19.2 %all-reduce.24 = (f32[3,32]{1,0:T(4,128)S(1)}, f32[3,32]{1,0:T(4,128)S(1)}, f32[3,32]{1,0:T(4,128)S(1)}, f32[3,32]{1,0:T(4,128)S(1)}) all-reduce(f32[3,32]{1,0:T(4,128)S(1)} %fusion.333, f32[3,32]{1,0:T(4,128)S(1)} %fusion.335, f32[3,32]{1,0:T(4,128)S(1)} %fusion.362, f32[3,32]{1,0:T(4,128)S(1)} %fusion.364), channel_id=1, replica_groups=mesh['dp'=4,'blk'=8] {'blk'}, use_global_device_ids=true, to_apply=%region_27.28 | all-reduce | flops 384 | bytes 3072 | tf_op jit(solution)/shard_map/psum | solution.py:54
  234.6 19.2 %all-reduce.23 = (f32[3,32]{1,0:T(4,128)S(1)}, f32[3,32]{1,0:T(4,128)S(1)}, f32[3,32]{1,0:T(4,128)S(1)}, f32[3,32]{1,0:T(4,128)S(1)}) all-reduce(f32[3,32]{1,0:T(4,128)S(1)} %fusion.330, f32[3,32]{1,0:T(4,128)S(1)} %fusion.332, f32[3,32]{1,0:T(4,128)S(1)} %fusion.359, f32[3,32]{1,0:T(4,128)S(1)} %fusion.361), channel_id=1, replica_groups=mesh['dp'=4,'blk'=8] {'blk'}, use_global_device_ids=true, to_apply=%region_33.34 | all-reduce | flops 384 | bytes 3072 | tf_op jit(solution)/shard_map/psum | solution.py:54
  256.7 30.8 %all_gather.127 = bf16[512,128]{1,0:T(8,128)(2,1)S(1)} all-gather(bf16[64,128]{1,0:T(8,128)(2,1)S(1)} %copy-done.132), channel_id=1, replica_groups=mesh['dp'=4,'blk'=8] {'blk'}, dimensions={0}, use_global_device_ids=true | all-gather | bytes 147456 | tf_op jit(solution)/shard_map/all_gather | solution.py:293
  297.7 30.9 %all_gather.122 = bf16[512,128]{1,0:T(8,128)(2,1)S(1)} all-gather(bf16[64,128]{1,0:T(8,128)(2,1)S(1)} %copy-done.133), channel_id=1, replica_groups=mesh['dp'=4,'blk'=8] {'blk'}, dimensions={0}, use_global_device_ids=true | all-gather | bytes 147456 | tf_op jit(solution)/shard_map/all_gather | solution.py:291
  336.2 30.7 %all_gather.130 = bf16[512,128]{1,0:T(8,128)(2,1)S(1)} all-gather(bf16[64,128]{1,0:T(8,128)(2,1)S(1)} %copy-done.134), channel_id=1, replica_groups=mesh['dp'=4,'blk'=8] {'blk'}, dimensions={0}, use_global_device_ids=true | all-gather | bytes 147456 | tf_op jit(solution)/shard_map/all_gather | solution.py:294
  425.7 19.1 %all-gather.3 = f32[8,1,256]{2,1,0:T(1,128)} all-gather(f32[1,1,256]{2,1,0:T(1,128)S(1)} %bitcast.764), channel_id=1, replica_groups=mesh['dp'=4,'blk'=8] {'blk'}, dimensions={0}, use_global_device_ids=true | all-gather | bytes 9216 | tf_op jit(solution)/shard_map/all_gather | solution.py:268
  450.5 17.4 %all-gather = f32[8,1,256]{2,1,0:T(1,128)} all-gather(f32[1,1,256]{2,1,0:T(1,128)S(1)} %bitcast.763), channel_id=1, replica_groups=mesh['dp'=4,'blk'=8] {'blk'}, dimensions={0}, use_global_device_ids=true | all-gather | bytes 9216 | tf_op jit(solution)/shard_map/all_gather | solution.py:267
  472.3 19.2 %all-gather.1 = f32[8,1,256]{2,1,0:T(1,128)} all-gather(f32[1,1,256]{2,1,0:T(1,128)S(1)} %bitcast.765), channel_id=1, replica_groups=mesh['dp'=4,'blk'=8] {'blk'}, dimensions={0}, use_global_device_ids=true | all-gather | bytes 9216 | tf_op jit(solution)/shard_map/all_gather | solution.py:268
  511.8 43.3 %all-gather.35.cloned.1.call-done = bf16[2048,512]{1,0:T(8,128)(2,1)} async-done(((bf16[256,512]{1,0:T(8,128)(2,1)}), bf16[2048,512]{1,0:T(8,128)(2,1)}) %all-gather.35.cloned.1.call-update) | async-done | bytes 2097168 | tf_op jit(solution)/shard_map/all_gather | solution.py:266
  563.2 41.9 %all-gather.37.cloned.1.call-done = bf16[2048,512]{1,0:T(8,128)(2,1)} async-done(((bf16[256,512]{1,0:T(8,128)(2,1)}), bf16[2048,512]{1,0:T(8,128)(2,1)}) %all-gather.37.cloned.1.call-update) | async-done | bytes 2097168 | tf_op jit(solution)/shard_map/all_gather | solution.py:265
  608.9 46.0 %all-gather.39.cloned.1.call-done = bf16[2048,512]{1,0:T(8,128)(2,1)} async-done(((bf16[256,512]{1,0:T(8,128)(2,1)}), bf16[2048,512]{1,0:T(8,128)(2,1)}) %all-gather.39.cloned.1.call-update) | async-done | bytes 2097168 | tf_op jit(solution)/shard_map/all_gather | solution.py:266
  694.6 19.1 %all-reduce.22 = (f32[3,32]{1,0:T(4,128)S(1)}, f32[3,32]{1,0:T(4,128)S(1)}, f32[3,32]{1,0:T(4,128)S(1)}, f32[3,32]{1,0:T(4,128)S(1)}) all-reduce(f32[3,32]{1,0:T(4,128)S(1)} %fusion.384, f32[3,32]{1,0:T(4,128)S(1)} %fusion.386, f32[3,32]{1,0:T(4,128)S(1)} %fusion.380, f32[3,32]{1,0:T(4,128)S(1)} %fusion.382), channel_id=1, replica_groups=mesh['dp'=4,'blk'=8] {'blk'}, use_global_device_ids=true, to_apply=%region_56.57 | all-reduce | flops 384 | bytes 3072 | tf_op jit(solution)/shard_map/psum | solution.py:72
  770.7 19.6 %all-reduce.21 = (f32[3,32]{1,0:T(4,128)S(1)}, f32[3,32]{1,0:T(4,128)S(1)}, f32[3,32]{1,0:T(4,128)S(1)}, f32[3,32]{1,0:T(4,128)S(1)}) all-reduce(f32[3,32]{1,0:T(4,128)S(1)} %fusion.323, f32[3,32]{1,0:T(4,128)S(1)} %fusion.325, f32[3,32]{1,0:T(4,128)S(1)} %fusion.352, f32[3,32]{1,0:T(4,128)S(1)} %fusion.354), channel_id=1, replica_groups=mesh['dp'=4,'blk'=8] {'blk'}, use_global_device_ids=true, to_apply=%region_61.62 | all-reduce | flops 384 | bytes 3072 | tf_op jit(solution)/shard_map/psum | solution.py:72
  854.2 64.5 %reduce-scatter.35.cloned.1.call-done = f32[64,512]{1,0:T(8,128)} async-done(((f32[512,512]{1,0:T(8,128)}), f32[64,512]{1,0:T(8,128)}) %reduce-scatter.35.cloned.1.call-update) | async-done | bytes 131088 | tf_op jit(solution)/shard_map/reduce_scatter | solution.py:320
  920.4 164.3 %reduce-scatter.27.cloned.1.call-done = f32[576,512]{1,0:T(8,128)} async-done(((f32[4608,512]{1,0:T(8,128)}), f32[576,512]{1,0:T(8,128)}) %reduce-scatter.27.cloned.1.call-update) | async-done | bytes 1179664 | tf_op jit(solution)/shard_map/reduce_scatter | solution.py:316
  1096.8 153.9 %reduce-scatter.25.cloned.1.call-done = f32[576,512]{1,0:T(8,128)} async-done(((f32[4608,512]{1,0:T(8,128)}), f32[576,512]{1,0:T(8,128)}) %reduce-scatter.25.cloned.1.call-update) | async-done | bytes 1179664 | tf_op jit(solution)/shard_map/reduce_scatter | solution.py:315
  1252.0 35.2 %all-reduce.20 = (f32[3,32]{1,0:T(4,128)S(1)}, f32[3,32]{1,0:T(4,128)S(1)}, f32[3,32]{1,0:T(4,128)S(1)}, f32[3,32]{1,0:T(4,128)S(1)}, f32[512]{0:T(512)S(1)}, /*...) all-reduce(f32[3,32]{1,0:T(4,128)S(1)} %fusion.319, ...), channel_id=1, replica_groups=mesh['dp'=4,'blk'=8] {'blk'}, use_global_device_ids=true, to_apply=%region_67.68 | all-reduce | flops 3456 | bytes 27648 | tf_op jit(solution)/shard_map/psum | solution.py:72
  1300.1 17.6 %reduce-scatter.21.cloned.1.call-done = f32[64,128]{1,0:T(8,128)} async-done(((f32[64,512]{1,0:T(8,128)}), f32[64,128]{1,0:T(8,128)}) %reduce-scatter.21.cloned.1.call-update) | async-done | bytes 32784 | tf_op jit(solution)/shard_map/reduce_scatter | solution.py:333
  1317.7 22.7 %reduce-scatter.23.cloned.1.call-done = f32[64,128]{1,0:T(8,128)} async-done(((f32[64,512]{1,0:T(8,128)}), f32[64,128]{1,0:T(8,128)}) %reduce-scatter.23.cloned.1.call-update) | async-done | bytes 32784 | tf_op jit(solution)/shard_map/reduce_scatter | solution.py:334
  1340.4 28.9 %reduce-scatter.15.cloned.1.call-done = f32[576,128]{1,0:T(8,128)} async-done(((f32[576,512]{1,0:T(8,128)}), f32[576,128]{1,0:T(8,128)}) %reduce-scatter.15.cloned.1.call-update) | async-done | bytes 294928 | tf_op jit(solution)/shard_map/reduce_scatter | solution.py:330
  1369.3 28.9 %reduce-scatter.13.cloned.1.call-done = f32[576,128]{1,0:T(8,128)} async-done(((f32[576,512]{1,0:T(8,128)}), f32[576,128]{1,0:T(8,128)}) %reduce-scatter.13.cloned.1.call-update) | async-done | bytes 294928 | tf_op jit(solution)/shard_map/reduce_scatter | solution.py:329
  (814 shorter events, 436.6 us)
Async XLA Ops:
  7.9 152.5 %all-gather.21.cloned.1.call-start = ((), (), s32[]{:S(2)}) async-start(), calls=%async_computation.14 | async-start | bytes 1327104 | tf_op jit(solution)/shard_map/all_gather | solution.py:290
  8.7 152.0 %all-gather.19.cloned.1.call-start = ((), (), s32[]{:S(2)}) async-start(), calls=%async_computation.13 | async-start | bytes 5898240 | tf_op jit(solution)/shard_map/all_gather | solution.py:303
  56.4 164.9 %all-gather.23.cloned.1.call-start = ((), (), s32[]{:S(2)}) async-start(), calls=%async_computation.15 | async-start | bytes 5898240 | tf_op jit(solution)/shard_map/all_gather | solution.py:304
  79.7 54.0 %collective-permute-start.1 = (bf16[1,64,512]{2,1,0:T(8,128)(2,1)S(1)}, bf16[1,64,512]{2,1,0:T(8,128)(2,1)S(1)}, u32[]{:S(2)}, u32[]{:S(2)}) collective-permute-start(bf16[1,64,512]{2,1,0:T(8,128)(2,1)S(1)} %get-tuple-element.127), channel_id=1, source_target_pairs={{1,0},{2,1},{3,2},{4,3},{5,4},{6,5},{7,6},{9,8},{10,9},{11,10},{12... | collective-permute-start | bytes 196616 | tf_op jit(solution)/shard_map/ppermute | solution.py:23
  160.4 238.2 %all-gather.29.cloned.1.call-start = ((), (), s32[]{:S(2)}) async-start(), calls=%async_computation.18 | async-start | bytes 2359296 | tf_op jit(solution)/shard_map/all_gather | solution.py:159
  256.7 164.6 %all-gather.31.cloned.1.call-start = ((), (), s32[]{:S(2)}) async-start(), calls=%async_computation.19 | async-start | bytes 2359296 | tf_op jit(solution)/shard_map/all_gather | solution.py:160
  295.5 149.4 %all-gather.25.cloned.1.call-start = ((), (), s32[]{:S(2)}) async-start(), calls=%async_computation.16 | async-start | bytes 2359296 | tf_op jit(solution)/shard_map/all_gather | solution.py:159
  296.6 171.3 %all-gather.27.cloned.1.call-start = ((), (), s32[]{:S(2)}) async-start(), calls=%async_computation.17 | async-start | bytes 2359296 | tf_op jit(solution)/shard_map/all_gather | solution.py:160
  297.6 209.1 %all-gather.33.cloned.1.call-start = ((), (), s32[]{:S(2)}) async-start(), calls=%async_computation.20 | async-start | bytes 2359296 | tf_op jit(solution)/shard_map/all_gather | solution.py:265
  336.2 219.0 %all-gather.35.cloned.1.call-start = ((), (), s32[]{:S(2)}) async-start(), calls=%async_computation.21 | async-start | bytes 2359296 | tf_op jit(solution)/shard_map/all_gather | solution.py:266
  375.7 229.4 %all-gather.37.cloned.1.call-start = ((), (), s32[]{:S(2)}) async-start(), calls=%async_computation.22 | async-start | bytes 2359296 | tf_op jit(solution)/shard_map/all_gather | solution.py:265
  376.8 278.1 %all-gather.39.cloned.1.call-start = ((), (), s32[]{:S(2)}) async-start(), calls=%async_computation.23 | async-start | bytes 2359296 | tf_op jit(solution)/shard_map/all_gather | solution.py:266
  379.0 461.6 %reduce-scatter.29.cloned.1.call-start = ((), (), s32[]{:S(2)}) async-start(), calls=%async_computation.32 | async-start | bytes 1179648 | tf_op jit(solution)/shard_map/reduce_scatter | solution.py:317
  506.7 334.9 %reduce-scatter.31.cloned.1.call-start = ((), (), s32[]{:S(2)}) async-start(), calls=%async_computation.33 | async-start | bytes 1179648 | tf_op jit(solution)/shard_map/reduce_scatter | solution.py:318
  663.3 189.2 %reduce-scatter.33.cloned.1.call-start = ((), (), s32[]{:S(2)}) async-start(), calls=%async_computation.34 | async-start | bytes 1179648 | tf_op jit(solution)/shard_map/reduce_scatter | solution.py:319
  688.8 229.9 %reduce-scatter.35.cloned.1.call-start = ((), (), s32[]{:S(2)}) async-start(), calls=%async_computation.35 | async-start | bytes 1179648 | tf_op jit(solution)/shard_map/reduce_scatter | solution.py:320
  719.1 365.6 %reduce-scatter.27.cloned.1.call-start = ((), (), s32[]{:S(2)}) async-start(), calls=%async_computation.31 | async-start | bytes 10616832 | tf_op jit(solution)/shard_map/reduce_scatter | solution.py:316
  731.3 519.4 %reduce-scatter.25.cloned.1.call-start = ((), (), s32[]{:S(2)}) async-start(), calls=%async_computation.30 | async-start | bytes 10616832 | tf_op jit(solution)/shard_map/reduce_scatter | solution.py:315
  811.3 488.8 %reduce-scatter.17.cloned.1.call-start = ((), (), s32[]{:S(2)}) async-start(), calls=%async_computation.26 | async-start | bytes 163840 | tf_op jit(solution)/shard_map/reduce_scatter | solution.py:331
  840.6 459.5 %reduce-scatter.19.cloned.1.call-start = ((), (), s32[]{:S(2)}) async-start(), calls=%async_computation.27 | async-start | bytes 163840 | tf_op jit(solution)/shard_map/reduce_scatter | solution.py:332
  841.7 476.0 %reduce-scatter.21.cloned.1.call-start = ((), (), s32[]{:S(2)}) async-start(), calls=%async_computation.28 | async-start | bytes 163840 | tf_op jit(solution)/shard_map/reduce_scatter | solution.py:333
  852.5 487.9 %reduce-scatter.23.cloned.1.call-start = ((), (), s32[]{:S(2)}) async-start(), calls=%async_computation.29 | async-start | bytes 163840 | tf_op jit(solution)/shard_map/reduce_scatter | solution.py:334
  918.7 450.6 %reduce-scatter.15.cloned.1.call-start = ((), (), s32[]{:S(2)}) async-start(), calls=%async_computation.25 | async-start | bytes 1474560 | tf_op jit(solution)/shard_map/reduce_scatter | solution.py:330
  1084.7 313.5 %reduce-scatter.13.cloned.1.call-start = ((), (), s32[]{:S(2)}) async-start(), calls=%async_computation.24 | async-start | bytes 1474560 | tf_op jit(solution)/shard_map/reduce_scatter | solution.py:329
  (191 other events, 7288.9 us)
Sparse Core Ops, SparseCore 0:
  10.2 43.7 all-gather.16
  56.2 42.4 all-gather.20
  100.2 38.9 all-gather.18
  160.5 36.2 all-gather.22
  256.8 46.3 all-gather.28
  305.2 49.9 all-gather.30
  357.3 47.8 all-gather.24
  407.3 47.8 all-gather.26
  457.4 47.9 all-gather.32
  507.3 47.7 all-gather.34
  557.3 47.7 all-gather.36
  607.1 47.7 all-gather.38
  658.3 62.0 reduce-scatter.28
  724.0 62.5 reduce-scatter.30
  789.9 62.5 reduce-scatter.32
  856.2 62.5 reduce-scatter.34
  922.2 162.4 reduce-scatter.26
  1088.1 162.5 reduce-scatter.24
  1253.8 18.6 reduce-scatter.16
  1275.5 19.5 reduce-scatter.18
  1298.1 19.5 reduce-scatter.20
  1320.8 19.5 reduce-scatter.22
  1343.6 25.6 reduce-scatter.14
  1372.5 25.7 reduce-scatter.12
where the time goes:
time: 1420 us; the launch traced here: 1410 us
  waiting for transfers between devices  624 us (44%)
  blocking collectives  388 us (27%)
  matrix products  141 us (10%)
  local copies, waits for them, and re-layouts  111 us (8%)
  other arithmetic  68 us (5%)
  starting transfers between devices  50 us (4%)
  between operations  23.1 us (2%)
    reduce_scatter x1, waiting for transfers between devices, reduce_all(): lax.psum_scatter(gradients[1], 'blk', scatter_dimension=0, tiled=True)  164 us
    reduce_scatter x1, waiting for transfers between devices, reduce_all(): lax.psum_scatter(gradients[0], 'blk', scatter_dimension=0, tiled=True)  154 us
    all_gather x2, waiting for transfers between devices, attention_key_grad(): lax.all_gather(heads_grad.astype(jnp.float32), 'blk', axis=0, tiled=True)  89.3 us
    psum x3, blocking collectives, norm_backward(): lax.psum((group_sums(member, scaled), group_sums(member, scaled * grouped...  73.9 us
    reduce_scatter x1, waiting for transfers between devices, reduce_all(): lax.psum_scatter(gradients[5], 'blk', scatter_dimension=0, tiled=True)  64.5 us
    psum x3, blocking collectives, norm_forward(): lax.psum((group_sums(member, grouped), group_sums(member, grouped * group...  57.9 us
    all_gather x2, waiting for transfers between devices, attention_key_grad(): lax.all_gather(queries.astype(jnp.float32), 'blk', axis=0, tiled=True)  41.9 us
    all_gather x2, blocking collectives, attention_key_grad(): lax.all_gather(correction, 'blk', axis=0, tiled=True)  38.3 us
  transfers between devices with their start and end apart: 40, of which 12 were waited for; matrix products, arithmetic and copies ran while one was open for 21% of the time, Pallas kernels for 0%

commit v1 on v0

--- a/solution.py
+++ b/solution.py
@@ -1,6 +1,10 @@
+import functools
+
 import jax
 import jax.numpy as jnp
 from jax import lax
+from jax.experimental import pallas as pl
+from jax.experimental.pallas import tpu as pltpu
 from jax.sharding import PartitionSpec as P
 
 GROUPS = 32
@@ -10,6 +14,410 @@
 EPSILON = 1e-06
 HIGHEST = lax.Precision.HIGHEST
 NEGATIVE = -1e30
+MESH = pl.DeviceIdType.MESH
+
+
+class Place:
+    def __init__(self):
+        self.d = lax.axis_index("dp")
+        self.b = lax.axis_index("blk")
+        self.y, self.c = self.d // 2, self.d % 2
+        self.z, self.x = self.b // 2, self.b % 2
+        self.up = {"dp": self.d, "blk": self.b + 2}
+        self.down = {"dp": self.d, "blk": self.b - 2}
+        self.xn = {"dp": self.d, "blk": self.z * 2 + 1 - self.x}
+        self.yn = {"dp": (1 - self.y) * 2 + self.c, "blk": self.b}
+        self.cn = {"dp": self.y * 2 + 1 - self.c, "blk": self.b}
+
+
+def enter(here, nz):
+    barrier = pltpu.get_barrier_semaphore()
+    for device in (here.xn, here.yn, here.cn):
+        pl.semaphore_signal(barrier, inc=1, device_id=device, device_id_type=MESH)
+
+    @pl.when(here.z < nz - 1)
+    def _():
+        pl.semaphore_signal(barrier, inc=1, device_id=here.up, device_id_type=MESH)
+
+    @pl.when(here.z > 0)
+    def _():
+        pl.semaphore_signal(barrier, inc=1, device_id=here.down, device_id_type=MESH)
+
+    lines = (here.z < nz - 1).astype(jnp.int32) + (here.z > 0).astype(jnp.int32)
+    pl.semaphore_wait(barrier, 3 + lines)
+
+
+def remote(src, dst, send, recv, device):
+    return pltpu.make_async_remote_copy(
+        src_ref=src, dst_ref=dst, send_sem=send, recv_sem=recv, device_id=device, device_id_type=MESH
+    )
+
+
+def steps_of(z, nz):
+    visits = [(z, None)]
+    for k in range(1, nz):
+        visits.append((z - k, z >= k))
+        visits.append((z + k, z + k < nz))
+    return visits
+
+
+def guarded(valid, body):
+    if valid is None:
+        body()
+    else:
+        pl.when(valid)(body)
+
+
+class Gather:
+    SEMS = 40
+
+    def __init__(self, here, nz, at, sems):
+        self.here, self.nz, self.at, self.sems = here, nz, at, sems
+        self.visits = steps_of(here.z, nz)
+
+    def sem(self, kind, z, way):
+        base = {"z": 0, "x": 4, "y": 8, "da": 12, "db": 16, "co": 20, "cx": 24, "cy": 28, "cd": 32, "zd": 36}[kind]
+        return self.sems.at[way, base + z]
+
+    def cp(self, kind, z, src, device, skind=None):
+        return remote(src, src, self.sem(skind or kind, z, 0), self.sem(kind, z, 1), device)
+
+    def own(self, z):
+        return self.at(z, self.here.x, self.here.d, None)
+
+    def colx(self, z, half=None):
+        return self.at(z, 1 - self.here.x, self.here.d, half)
+
+    def coly(self, z, half=None):
+        return self.at(z, self.here.x, (1 - self.here.y) * 2 + self.here.c, half)
+
+    def cold(self, z, half=None):
+        return self.at(z, 1 - self.here.x, (1 - self.here.y) * 2 + self.here.c, half)
+
+    def have(self, j):
+        z, valid = self.visits[j]
+        here = self.here
+
+        def body():
+            src = self.own(z)
+            if j > 0:
+                self.cp("z", z, src, here.up).wait_recv()
+            if j == 0 or j % 2 == 1:
+
+                @pl.when(here.z < self.nz - 1)
+                def _():
+                    self.cp("z", z, src, here.up).start()
+
+            if j == 0 or j % 2 == 0:
+
+                @pl.when(here.z > 0)
+                def _():
+                    self.cp("z", z, src, here.down, "zd").start()
+
+            self.cp("x", z, src, here.xn).start()
+            self.cp("y", z, src, here.yn).start()
+            self.cp("co", z, src, here.cn).start()
+
+        guarded(valid, body)
+
+    def cross(self, j):
+        z, valid = self.visits[j]
+        here = self.here
+
+        def body():
+            self.cp("x", z, self.colx(z), here.xn).wait_recv()
+            self.cp("da", z, self.colx(z, 0), here.yn).start()
+            self.cp("cx", z, self.colx(z), here.cn).start()
+            self.cp("y", z, self.coly(z), here.yn).wait_recv()
+            self.cp("db", z, self.coly(z, 1), here.xn).start()
+            self.cp("cy", z, self.coly(z), here.cn).start()
+
+        guarded(valid, body)
+
+    def diagonal(self, j):
+        z, valid = self.visits[j]
+        here = self.here
+
+        def body():
+            self.cp("da", z, self.cold(z, 0), here.yn).wait_recv()
+            self.cp("db", z, self.cold(z, 1), here.xn).wait_recv()
+            self.cp("cd", z, self.cold(z), here.cn).start()
+
+        guarded(valid, body)
+
+    def arrive(self):
+        here = self.here
+        near, far = here.y * 2 + 1 - here.c, (1 - here.y) * 2 + 1 - here.c
+        for z in range(self.nz):
+            for kind, x, d in (("co", here.x, near), ("cx", 1 - here.x, near), ("cy", here.x, far), ("cd", 1 - here.x, far)):
+                self.cp(kind, z, self.at(z, x, d, None), here.cn).wait_recv()
+
+    def finish(self):
+        here = self.here
+        for j, (z, valid) in enumerate(self.visits):
+
+            def body():
+                src = self.own(z)
+                if j == 0 or j % 2 == 1:
+
+                    @pl.when(here.z < self.nz - 1)
+                    def _():
+                        self.cp("z", z, src, here.up).wait_send()
+
+                if j == 0 or j % 2 == 0:
+
+                    @pl.when(here.z > 0)
+                    def _():
+                        self.cp("z", z, src, here.down, "zd").wait_send()
+
+                self.cp("x", z, src, here.xn).wait_send()
+                self.cp("y", z, src, here.yn).wait_send()
+                self.cp("da", z, self.colx(z, 0), here.yn).wait_send()
+                self.cp("db", z, self.coly(z, 1), here.xn).wait_send()
+                for kind in ("co", "cx", "cy", "cd"):
+                    self.cp(kind, z, src, here.cn).wait_send()
+
+            guarded(valid, body)
+
+    def program(self):
+        todo = [lambda: self.have(0)]
+        pairs = [(0,)] + [(2 * k - 1, 2 * k) for k in range(1, self.nz)]
+        for k in range(1, self.nz + 2):
+            if k < self.nz:
+                todo += [lambda j=j: self.have(j) for j in pairs[k]]
+            if k - 1 < self.nz:
+                todo += [lambda j=j: self.cross(j) for j in pairs[k - 1]]
+            if 0 <= k - 2 < self.nz:
+                todo += [lambda j=j: self.diagonal(j) for j in pairs[k - 2]]
+        return todo
+
+
+class Scatter:
+    SEMS = 44
+
+    def __init__(self, here, nz, at, part, sems, bufs):
+        self.here, self.nz, self.at, self.part, self.sems = here, nz, at, part, sems
+        self.core, self.acc, self.half, self.side, self.line = bufs
+        visits = steps_of(here.z, nz)
+        self.visits = visits[::-1]
+
+    def sem(self, kind, z, way):
+        base = {"c0": 0, "c1": 4, "c2": 8, "c3": 12, "da": 16, "db": 20, "x": 24, "y": 28, "l": 32, "ld": 36}[kind]
+        return self.sems.at[way, base + z]
+
+    def cp(self, kind, z, src, dst, device, skind=None):
+        return remote(src, dst, self.sem(skind or kind, z, 0), self.sem(kind, z, 1), device)
+
+    def places(self, z, c):
+        here = self.here
+        y, x = here.y, here.x
+        return [(z, x, y * 2 + c), (z, 1 - x, y * 2 + c), (z, x, (1 - y) * 2 + c), (z, 1 - x, (1 - y) * 2 + c)]
+
+    def core_cp(self, z, k):
+        return self.cp("c%d" % k, z, self.at(*self.places(z, 1 - self.here.c)[k]), self.core.at[k, z], self.here.cn)
+
+    def begin(self, j):
+        z, valid = self.visits[j]
+
+        def body():
+            for k in (3, 1, 2, 0):
+                self.core_cp(z, k).start()
+
+        guarded(valid, body)
+
+    def halves(self, z):
+        return (
+            self.cp("da", z, self.part(self.acc.at[3, z], 0), self.half.at[0, z], self.here.xn),
+            self.cp("db", z, self.part(self.acc.at[3, z], 1), self.half.at[1, z], self.here.yn),
+        )
+
+    def sides(self, z):
+        return (
+            self.cp("x", z, self.acc.at[1, z], self.side.at[0, z], self.here.xn),
+            self.cp("y", z, self.acc.at[2, z], self.side.at[1, z], self.here.yn),
+        )
+
+    def pair(self, z, k):
+        self.core_cp(z, k).wait_recv()
+        mine = self.at(*self.places(z, self.here.c)[k])[...].astype(jnp.float32)
+        return mine + self.core[k, z].astype(jnp.float32)
+
+    def corner(self, j):
+        z, valid = self.visits[j]
+
+        def body():
+            self.acc[3, z] = self.pair(z, 3).astype(jnp.bfloat16)
+            for copy in self.halves(z):
+                copy.start()
+
+        guarded(valid, body)
+
+    def edges(self, j):
+        z, valid = self.visits[j]
+
+        def body():
+            from_x, from_y = self.halves(z)
+            for k, copy, h in ((1, from_y, 1), (2, from_x, 0)):
+                total = self.pair(z, k)
+                copy.wait_recv()
+                self.acc[k, z] = total.astype(jnp.bfloat16)
+                place = self.part(self.acc.at[k, z], h)
+                place[...] = (place[...].astype(jnp.float32) + self.half[h, z].astype(jnp.float32)).astype(jnp.bfloat16)
+                self.sides(z)[k - 1].start()
+
+        guarded(valid, body)
+
+    def line_cp(self, z, upward):
+        here = self.here
+        if upward:
+            return self.cp("l", z, self.acc.at[0, z], self.line.at[0, z], here.up)
+        return self.cp("ld", z, self.acc.at[0, z], self.line.at[1, z], here.down)
+
+    def column(self, j, out=None):
+        z, valid = self.visits[j]
+        here, nz = self.here, self.nz
+        last = j == len(self.visits) - 1
+
+        def body():
+            total = self.pair(z, 0)
+            for copy, k in zip(self.sides(z), (0, 1)):
+                copy.wait_recv()
+                total = total + self.side[k, z].astype(jnp.float32)
+            if last:
+                out[...] = total
+
+                @pl.when(here.z > 0)
+                def _():
+                    self.line_cp(z, True).wait_recv()
+                    out[...] += self.line[0, z].astype(jnp.float32)
+
+                @pl.when(here.z < nz - 1)
+                def _():
+                    self.line_cp(z, False).wait_recv()
+                    out[...] += self.line[1, z].astype(jnp.float32)
+            else:
+                upward = j % 2 == 0
+                self.acc[0, z] = total.astype(jnp.bfloat16)
+
+                @pl.when((here.z > 0) if upward else (here.z < nz - 1))
+                def _():
+                    self.line_cp(z, upward).wait_recv()
+                    k = 0 if upward else 1
+                    self.acc[0, z] = (self.acc[0, z].astype(jnp.float32) + self.line[k, z].astype(jnp.float32)).astype(jnp.bfloat16)
+
+                self.line_cp(z, upward).start()
+
+        guarded(valid, body)
+
+    def finish(self):
+        for j, (z, valid) in enumerate(self.visits):
+            last = j == len(self.visits) - 1
+
+            def body():
+                for k in range(4):
+                    self.core_cp(z, k).wait_send()
+                for copy in self.halves(z) + self.sides(z):
+                    copy.wait_send()
+                if not last:
+                    self.line_cp(z, j % 2 == 0).wait_send()
+
+            guarded(valid, body)
+
+    def program(self, out):
+        pairs = [[2 * k, 2 * k + 1] for k in range(self.nz - 1)] + [[2 * (self.nz - 1)]]
+        todo = []
+        for k in range(self.nz + 3):
+            if k < self.nz:
+                todo += [lambda j=j: self.begin(j) for j in pairs[k]]
+            if 0 <= k - 1 < self.nz:
+                todo += [lambda j=j: self.corner(j) for j in pairs[k - 1]]
+            if 0 <= k - 2 < self.nz:
+                todo += [lambda j=j: self.edges(j) for j in pairs[k - 2]]
+            if 0 <= k - 3 < self.nz:
+                todo += [lambda j=j: self.column(j, out) for j in pairs[k - 3]]
+        return todo
+
+def weight_places(ref, rows):
+    def at(z, x, d, half=None):
+        base, count = (z * 2 + x) * rows, rows
+        if half is not None:
+            base, count = base + half * (rows // 2), rows // 2
+        return ref.at[pl.ds(pl.multiple_of(base, 16), count), pl.ds(pl.multiple_of(d * 128, 128), 128)]
+
+    return at
+
+
+def gather_kernel(nz, rows, *refs):
+    count = len(rows)
+    shards, wholes, (sems, local) = refs[:count], refs[count : 2 * count], refs[2 * count :]
+    here = Place()
+    enter(here, nz)
+    gathers = []
+    for k in range(count):
+        at = weight_places(wholes[k], rows[k])
+        gathers.append(Gather(here, nz, at, sems.at[k]))
+        own = pltpu.make_async_copy(shards[k], at(here.z, here.x, here.d), local.at[k])
+        own.start()
+    for k in range(count):
+        pltpu.make_async_copy(shards[k], gathers[k].own(here.z), local.at[k]).wait()
+        for step in gathers[k].program():
+            step()
+    for gather in gathers:
+        gather.arrive()
+        gather.finish()
+
+
+def gather_all(shards, nz):
+    rows = [item.shape[0] for item in shards]
+    return pl.pallas_call(
+        functools.partial(gather_kernel, nz, rows),
+        out_shape=[jax.ShapeDtypeStruct((r * nz * 2, 512), jnp.bfloat16) for r in rows],
+        in_specs=[pl.BlockSpec(memory_space=pltpu.VMEM)] * len(rows),
+        out_specs=[pl.BlockSpec(memory_space=pltpu.VMEM)] * len(rows),
+        scratch_shapes=[
+            pltpu.SemaphoreType.DMA((len(rows), 2, Gather.SEMS)),
+            pltpu.SemaphoreType.DMA((len(rows),)),
+        ],
+        compiler_params=pltpu.CompilerParams(collective_id=0, has_side_effects=True, vmem_limit_bytes=56 << 20),
+    )(*shards)
+
+
+def scatter_kernel(nz, rows, *refs):
+    count = len(rows)
+    wholes, outs = refs[:count], refs[count : 2 * count]
+    bufs, sems = refs[2 * count : -1], refs[-1]
+    here = Place()
+    enter(here, nz)
+    scatters = []
+    for k in range(count):
+        at = weight_places(wholes[k], rows[k])
+        half = rows[k] // 2
+
+        def part(ref, h, half=half):
+            return ref.at[pl.ds(h * half, half)]
+
+        scatters.append(Scatter(here, nz, at, part, sems.at[k], bufs[5 * k : 5 * k + 5]))
+    for k in range(count):
+        for step in scatters[k].program(outs[k]):
+            step()
+    for scatter in scatters:
+        scatter.finish()
+
+
+def scatter_all(wholes, nz):
+    rows = [item.shape[0] // (nz * 2) for item in wholes]
+    scratch = []
+    for r in rows:
+        for shape in ((4, nz, r, 128), (4, nz, r, 128), (2, nz, r // 2, 128), (2, nz, r, 128), (2, nz, r, 128)):
+            scratch.append(pltpu.VMEM(shape, jnp.bfloat16))
+    return pl.pallas_call(
+        functools.partial(scatter_kernel, nz, rows),
+        out_shape=[jax.ShapeDtypeStruct((r, 128), jnp.float32) for r in rows],
+        in_specs=[pl.BlockSpec(memory_space=pltpu.VMEM)] * len(rows),
+        out_specs=[pl.BlockSpec(memory_space=pltpu.VMEM)] * len(rows),
+        scratch_shapes=scratch + [pltpu.SemaphoreType.DMA((len(rows), 2, Scatter.SEMS))],
+        compiler_params=pltpu.CompilerParams(collective_id=1, has_side_effects=True, vmem_limit_bytes=60 << 20),
+    )(*wholes)
 
 
 def extended(shard, sides, width):
@@ -476,6 +884,29 @@
     return (activation, input_grad, local_grads)
 
 
+def by_block(whole, nz):
+    split = whole.reshape(nz * 2, 4, -1, 512)
+    return [split[:, k].reshape(-1, 512) for k in range(4)]
+
+
+def fast_collect(conv1_weight, conv2_weight, query_weight, key_weight, value_weight, output_weight, *norms):
+    nz = lax.axis_size("blk") // 2
+    stacked = jnp.concatenate([query_weight, key_weight, value_weight, output_weight])
+    w1, w2, wa = gather_all((conv1_weight, conv2_weight, stacked), nz)
+    rows = tuple(lax.all_gather(item, "blk", axis=0, tiled=True) for item in norms)
+    return (w1, w2, *by_block(wa, nz)), rows
+
+
+def fast_reduce(gradients):
+    nz = lax.axis_size("blk") // 2
+    low_grads = [item.astype(jnp.bfloat16) for item in gradients[:6]]
+    attn = jnp.stack([item.reshape(nz * 2, -1, 512) for item in low_grads[2:]], axis=1).reshape(-1, 512)
+    g2, ga, g1 = scatter_all((low_grads[1], attn, low_grads[0]), nz)
+    ga = ga.reshape(4, -1, 128)
+    norms = tuple(lax.psum_scatter(item, "blk", scatter_dimension=0, tiled=True) for item in gradients[6:])
+    return (g1, g2, ga[0], ga[1], ga[2], ga[3]) + tuple(lax.psum(norms, "dp"))
+
+
 def shards(
     features,
     bounds,
@@ -496,24 +927,25 @@
     blocks = lax.axis_size("blk")
     position = lax.axis_index("blk")
     micro_count = features.shape[1]
-    shard_sums = None
+    local_sums = None
     outputs = []
     input_grads = []
+    near = lax.axis_size("dp") == 4 and blocks == 8
+    matrices, norm_params = (fast_collect if near else collect)(
+        conv1_weight,
+        conv2_weight,
+        query_weight,
+        key_weight,
+        value_weight,
+        output_weight,
+        norm1_gain,
+        norm1_shift,
+        norm2_gain,
+        norm2_shift,
+        norm3_gain,
+        norm3_shift,
+    )
     for micro_index in range(micro_count):
-        matrices, norm_params = collect(
-            conv1_weight,
-            conv2_weight,
-            query_weight,
-            key_weight,
-            value_weight,
-            output_weight,
-            norm1_gain,
-            norm1_shift,
-            norm2_gain,
-            norm2_shift,
-            norm3_gain,
-            norm3_shift,
-        )
         activation, input_grad, local_grads = one_batch(
             features[0, micro_index],
             bounds[0, micro_index],
@@ -525,12 +957,12 @@
         )
         outputs.append(activation)
         input_grads.append(input_grad)
-        reduced = reduce_all(local_grads)
-        shard_sums = (
-            reduced
-            if shard_sums is None
-            else tuple((acc + new for acc, new in zip(shard_sums, reduced)))
-        )
+        local_sums = (
+            local_grads
+            if local_sums is None
+            else tuple((acc + new for acc, new in zip(local_sums, local_grads)))
+        )
+    shard_sums = (fast_reduce if near else reduce_all)(local_sums)
     activations = jnp.stack(outputs)[None]
     input_grad_all = jnp.stack(input_grads)[None]
     return (

time: 1420 us -> 1000 us (0.70)
  waiting for transfers between devices: 624 us -> 213 us
  Pallas kernels: 0 us -> 151 us
  blocking collectives: 388 us -> 241 us
    reduce_scatter x12 -> x0, waiting for transfers between devices: 490 us -> none  [the longest x1 164 us: reduce_all(): lax.psum_scatter(gradients[1], 'blk', scatter_dimension=0, tiled=True)]
    all_gather x8 -> x0, blocking collectives: 154 us -> none  [the longest x1 30.9 us: collect(): lax.all_gather(query_weight, 'blk', axis=0, tiled=True)]
    pallas_call x0 -> x2, Pallas kernels: none -> 151 us  [the longest x1 78.2 us: scatter_all(): pl.pallas_call(functools.partial(scatter_kernel, nz, rows), out_shape=[ja...]
    all_gather x2, waiting for transfers between devices: 0.01 us -> 50.6 us  [attention_forward(): lax.all_gather(values_local, 'blk', axis=0, tiled=True)]
    all_gather x2, waiting for transfers between devices: 0.02 us -> 36.5 us  [attention_forward(): lax.all_gather(keys_local, 'blk', axis=0, tiled=True)]
    unnamed x373 -> x419, local copies, waits for them, and re-layouts: 35.5 us -> 32.5 us
  transfers between devices with their start and end apart: 40 -> 24, of which waited for: 12 -> 8; matrix products, arithmetic and copies ran while one was open for 21% -> 17% of each run, Pallas kernels for 0% -> 15%
where the time goes in v1:
time: 1000 us; the launch traced here: 993 us
  blocking collectives  241 us (24%)
  waiting for transfers between devices  213 us (21%)
  Pallas kernels  151 us (15%)
  matrix products  137 us (14%)
  local copies, waits for them, and re-layouts  125 us (12%)
  other arithmetic  64.1 us (6%)
  starting transfers between devices  39.3 us (4%)
  between operations  23 us (2%)
    all_gather x2, waiting for transfers between devices, attention_key_grad(): lax.all_gather(heads_grad.astype(jnp.float32), 'blk', axis=0, tiled=True)  93.4 us
    pallas_call x1, Pallas kernels, scatter_all(): pl.pallas_call(functools.partial(scatter_kernel, nz, rows), out_shape=[ja...  78.2 us
    psum x3, blocking collectives, norm_backward(): lax.psum((group_sums(member, scaled), group_sums(member, scaled * grouped...  76.7 us
    pallas_call x1, Pallas kernels, gather_all(): pl.pallas_call(functools.partial(gather_kernel, nz, rows), out_shape=[jax...  72.7 us
    psum x3, blocking collectives, norm_forward(): lax.psum((group_sums(member, grouped), group_sums(member, grouped * group...  63.8 us
    all_gather x2, waiting for transfers between devices, attention_forward(): lax.all_gather(values_local, 'blk', axis=0, tiled=True)  50.6 us
    all_gather x2, blocking collectives, attention_key_grad(): lax.all_gather(correction, 'blk', axis=0, tiled=True)  38.4 us
    all_gather x2, blocking collectives, attention_key_grad(): lax.all_gather(log_total, 'blk', axis=0, tiled=True)  38.2 us
  transfers between devices with their start and end apart: 24, of which 8 were waited for; matrix products, arithmetic and copies ran while one was open for 17% of the time, Pallas kernels for 15%

profile of v1, /device:TPU:0, one launch (start us, length us, event | category | flops | bytes accessed | tf_op | source)
XLA Modules:
  0.0 993.0 jit_solution(3799191787995053433)
XLA Ops:
  21.8 23.3 %all-reduce.25 = (f32[3,32]{1,0:T(4,128)S(1)}, f32[3,32]{1,0:T(4,128)S(1)}, f32[3,32]{1,0:T(4,128)S(1)}, f32[3,32]{1,0:T(4,128)S(1)}) all-reduce(f32[3,32]{1,0:T(4,128)S(1)} %fusion.335, f32[3,32]{1,0:T(4,128)S(1)} %fusion.337, f32[3,32]{1,0:T(4,128)S(1)} %fusion.364, f32[3,32]{1,0:T(4,128)S(1)} %fusion.366), channel_id=1, replica_groups=mesh['dp'=4,'blk'=8] {'blk'}, use_global_device_ids=true, to_apply=%region_23.24 | all-reduce | flops 384 | bytes 3072 | tf_op jit(solution)/shard_map/psum | solution.py:462
  50.2 17.9 %all-reduce.27 = (bf16[512]{0:T(512)(128)(2,1)S(1)}, bf16[512]{0:T(512)(128)(2,1)S(1)}, bf16[512]{0:T(512)(128)(2,1)}, bf16[512]{0:T(512)(128)(2,1)}, bf16[512]{0:T(512)(128)(2,1)}, /*index=5*/bf16[512]{0:T(512)(128)(2,1)S(1)}) all-reduce(bf16[512]{0:T(512)(128)(2,1)S(1)} %dynamic-update-slice.1, ...), channel_id=1, replica_groups=mesh['dp'=4,'blk'=8] {'blk'}, use_global_device_ids=true, to_apply=%add.9 | all-reduce | flops 3072 | bytes 12288
  81.0 72.7 %shard_map.254 = (bf16[4608,512]{1,0:T(8,128)(2,1)}, bf16[4608,512]{1,0:T(8,128)(2,1)}, bf16[2048,512]{1,0:T(8,128)(2,1)}) custom-call(bf16[576,128]{1,0:T(8,128)(2,1)} %refs_0_.1, bf16[576,128]{1,0:T(8,128)(2,1)} %refs_1_.1, bf16[256,128]{1,0:T(8,128)(2,1)} %pad_maximum_fusion.17.refs_2_), custom_call_target="tpu_custom_call" | custom-call | tf_op jit(solution)/shard_map/pallas_call | solution.py:372
  155.6 7.4 copy.121
  192.7 6.2 fusion.477
  199.4 20.5 %all-reduce.24 = (f32[3,32]{1,0:T(4,128)S(1)}, f32[3,32]{1,0:T(4,128)S(1)}, f32[3,32]{1,0:T(4,128)S(1)}, f32[3,32]{1,0:T(4,128)S(1)}) all-reduce(f32[3,32]{1,0:T(4,128)S(1)} %fusion.332, f32[3,32]{1,0:T(4,128)S(1)} %fusion.334, f32[3,32]{1,0:T(4,128)S(1)} %fusion.361, f32[3,32]{1,0:T(4,128)S(1)} %fusion.363), channel_id=1, replica_groups=mesh['dp'=4,'blk'=8] {'blk'}, use_global_device_ids=true, to_apply=%region_27.28 | all-reduce | flops 384 | bytes 3072 | tf_op jit(solution)/shard_map/psum | solution.py:462
  270.4 20.0 %all-reduce.23 = (f32[3,32]{1,0:T(4,128)S(1)}, f32[3,32]{1,0:T(4,128)S(1)}, f32[3,32]{1,0:T(4,128)S(1)}, f32[3,32]{1,0:T(4,128)S(1)}) all-reduce(f32[3,32]{1,0:T(4,128)S(1)} %fusion.329, f32[3,32]{1,0:T(4,128)S(1)} %fusion.331, f32[3,32]{1,0:T(4,128)S(1)} %fusion.358, f32[3,32]{1,0:T(4,128)S(1)} %fusion.360), channel_id=1, replica_groups=mesh['dp'=4,'blk'=8] {'blk'}, use_global_device_ids=true, to_apply=%region_33.34 | all-reduce | flops 384 | bytes 3072 | tf_op jit(solution)/shard_map/psum | solution.py:462
  310.7 6.3 copy.195
  346.5 19.0 %all-gather = f32[8,1,256]{2,1,0:T(1,128)} all-gather(f32[1,1,256]{2,1,0:T(1,128)S(1)} %bitcast.815), channel_id=1, replica_groups=mesh['dp'=4,'blk'=8] {'blk'}, dimensions={0}, use_global_device_ids=true | all-gather | bytes 9216 | tf_op jit(solution)/shard_map/all_gather | solution.py:675
  365.5 25.6 %all-gather.15.cloned.1.call-done = bf16[2048,512]{1,0:T(8,128)(2,1)} async-done(((bf16[256,512]{1,0:T(8,128)(2,1)}), bf16[2048,512]{1,0:T(8,128)(2,1)}) %all-gather.15.cloned.1.call-update) | async-done | bytes 2097168 | tf_op jit(solution)/shard_map/all_gather | solution.py:568
  395.4 18.9 %all-gather.1 = f32[8,1,256]{2,1,0:T(1,128)} all-gather(f32[1,1,256]{2,1,0:T(1,128)S(1)} %bitcast.817), channel_id=1, replica_groups=mesh['dp'=4,'blk'=8] {'blk'}, dimensions={0}, use_global_device_ids=true | all-gather | bytes 9216 | tf_op jit(solution)/shard_map/all_gather | solution.py:676
  421.5 19.5 %all-gather.21.cloned.1.call-done = bf16[2048,512]{1,0:T(8,128)(2,1)} async-done(((bf16[256,512]{1,0:T(8,128)(2,1)}), bf16[2048,512]{1,0:T(8,128)(2,1)}) %all-gather.21.cloned.1.call-update) | async-done | bytes 2097168 | tf_op jit(solution)/shard_map/all_gather | solution.py:673
  444.9 46.0 %all-gather.23.cloned.1.call-done = bf16[2048,512]{1,0:T(8,128)(2,1)} async-done(((bf16[256,512]{1,0:T(8,128)(2,1)}), bf16[2048,512]{1,0:T(8,128)(2,1)}) %all-gather.23.cloned.1.call-update) | async-done | bytes 2097168 | tf_op jit(solution)/shard_map/all_gather | solution.py:674
  509.2 31.4 %all-gather.17.cloned.1.call-done = bf16[2048,512]{1,0:T(8,128)(2,1)} async-done(((bf16[256,512]{1,0:T(8,128)(2,1)}), bf16[2048,512]{1,0:T(8,128)(2,1)}) %all-gather.17.cloned.1.call-update) | async-done | bytes 2097168 | tf_op jit(solution)/shard_map/all_gather | solution.py:567
  546.3 19.1 %all-gather.2 = f32[8,1,256]{2,1,0:T(1,128)} all-gather(f32[1,1,256]{2,1,0:T(1,128)S(1)} %bitcast.816), channel_id=1, replica_groups=mesh['dp'=4,'blk'=8] {'blk'}, dimensions={0}, use_global_device_ids=true | all-gather | bytes 9216 | tf_op jit(solution)/shard_map/all_gather | solution.py:675
  565.4 25.0 %all-gather.19.cloned.1.call-done = bf16[2048,512]{1,0:T(8,128)(2,1)} async-done(((bf16[256,512]{1,0:T(8,128)(2,1)}), bf16[2048,512]{1,0:T(8,128)(2,1)}) %all-gather.19.cloned.1.call-update) | async-done | bytes 2097168 | tf_op jit(solution)/shard_map/all_gather | solution.py:568
  594.8 19.5 %all-gather.3 = f32[8,1,256]{2,1,0:T(1,128)} all-gather(f32[1,1,256]{2,1,0:T(1,128)S(1)} %bitcast.818), channel_id=1, replica_groups=mesh['dp'=4,'blk'=8] {'blk'}, dimensions={0}, use_global_device_ids=true | all-gather | bytes 9216 | tf_op jit(solution)/shard_map/all_gather | solution.py:676
  626.8 13.1 %all-gather.25.cloned.1.call-done = bf16[2048,512]{1,0:T(8,128)(2,1)} async-done(((bf16[256,512]{1,0:T(8,128)(2,1)}), bf16[2048,512]{1,0:T(8,128)(2,1)}) %all-gather.25.cloned.1.call-update) | async-done | bytes 2097168 | tf_op jit(solution)/shard_map/all_gather | solution.py:673
  643.7 47.4 %all-gather.27.cloned.1.call-done = bf16[2048,512]{1,0:T(8,128)(2,1)} async-done(((bf16[256,512]{1,0:T(8,128)(2,1)}), bf16[2048,512]{1,0:T(8,128)(2,1)}) %all-gather.27.cloned.1.call-update) | async-done | bytes 2097168 | tf_op jit(solution)/shard_map/all_gather | solution.py:674
  713.4 19.8 %all-reduce.22 = (f32[3,32]{1,0:T(4,128)}, f32[3,32]{1,0:T(4,128)}, f32[3,32]{1,0:T(4,128)S(1)}, f32[3,32]{1,0:T(4,128)S(1)}) all-reduce(f32[3,32]{1,0:T(4,128)S(1)} %fusion.383, f32[3,32]{1,0:T(4,128)S(1)} %fusion.385, f32[3,32]{1,0:T(4,128)S(1)} %fusion.379, f32[3,32]{1,0:T(4,128)S(1)} %fusion.381), channel_id=1, replica_groups=mesh['dp'=4,'blk'=8] {'blk'}, use_global_device_ids=true, to_apply=%region_56.57 | all-reduce | flops 384 | bytes 3072 | tf_op jit(solution)/shard_map/psum | solution.py:480
  788.1 20.3 %all-reduce.21 = (f32[3,32]{1,0:T(4,128)S(1)}, f32[3,32]{1,0:T(4,128)S(1)}, f32[3,32]{1,0:T(4,128)S(1)}, f32[3,32]{1,0:T(4,128)S(1)}) all-reduce(f32[3,32]{1,0:T(4,128)S(1)} %fusion.322, f32[3,32]{1,0:T(4,128)S(1)} %fusion.324, f32[3,32]{1,0:T(4,128)S(1)} %fusion.351, f32[3,32]{1,0:T(4,128)S(1)} %fusion.353), channel_id=1, replica_groups=mesh['dp'=4,'blk'=8] {'blk'}, use_global_device_ids=true, to_apply=%region_61.62 | all-reduce | flops 384 | bytes 3072 | tf_op jit(solution)/shard_map/psum | solution.py:480
  832.9 78.2 %shard_map.255 = (f32[576,128]{1,0:T(8,128)}, f32[256,128]{1,0:T(8,128)}, f32[576,128]{1,0:T(8,128)}) custom-call(bf16[4608,512]{1,0:T(8,128)(2,1)} %add_convert_fusion.1.refs_0_, bf16[2048,512]{1,0:T(8,128)(2,1)} %bitcast.778, bf16[4608,512]{1,0:T(8,128)(2,1)} %add_convert_fusion.refs_2_), custom_call_target="tpu_custom_call" | custom-call | tf_op jit(solution)/shard_map/pallas_call | solution.py:413
  936.3 36.7 %all-reduce.20 = (f32[3,32]{1,0:T(4,128)S(1)}, f32[3,32]{1,0:T(4,128)S(1)}, f32[3,32]{1,0:T(4,128)S(1)}, f32[3,32]{1,0:T(4,128)S(1)}, f32[512]{0:T(512)S(1)}, /*...) all-reduce(f32[3,32]{1,0:T(4,128)S(1)} %fusion.318, ...), channel_id=1, replica_groups=mesh['dp'=4,'blk'=8] {'blk'}, use_global_device_ids=true, to_apply=%region_67.68 | all-reduce | flops 3456 | bytes 27648 | tf_op jit(solution)/shard_map/psum | solution.py:480
  978.0 6.3 all-reduce.26
  (809 shorter events, 349.9 us)
Async XLA Ops:
  7.3 333.6 %all-gather.13.cloned.1.call-start = ((), (), s32[]{:S(2)}) async-start(), calls=%async_computation | async-start | bytes 2359296 | tf_op jit(solution)/shard_map/all_gather | solution.py:567
  68.6 95.7 %collective-permute-start.4 = (bf16[1,64,512]{2,1,0:T(8,128)(2,1)S(1)}, bf16[1,64,512]{2,1,0:T(8,128)(2,1)S(1)}, u32[]{:S(2)}, u32[]{:S(2)}) collective-permute-start(bf16[1,64,512]{2,1,0:T(8,128)(2,1)S(1)} %get-tuple-element.144), channel_id=1, source_target_pairs={{0,1},{1,2},{2,3},{3,4},{4,5},{5,6},{6,7},{8,9},{9,10},{10,11},{11... | collective-permute-start | bytes 196616 | tf_op jit(solution)/shard_map/ppermute | solution.py:430
  72.5 91.8 %collective-permute-start.5 = (bf16[1,64,512]{2,1,0:T(8,128)(2,1)S(1)}, bf16[1,64,512]{2,1,0:T(8,128)(2,1)S(1)}, u32[]{:S(2)}, u32[]{:S(2)}) collective-permute-start(bf16[1,64,512]{2,1,0:T(8,128)(2,1)S(1)} %get-tuple-element.145), channel_id=1, source_target_pairs={{1,0},{2,1},{3,2},{4,3},{5,4},{6,5},{7,6},{9,8},{10,9},{11,10},{12... | collective-permute-start | bytes 196616 | tf_op jit(solution)/shard_map/ppermute | solution.py:431
  74.4 90.3 %collective-permute-start = (bf16[1,64,512]{2,1,0:T(8,128)(2,1)}, bf16[1,64,512]{2,1,0:T(8,128)(2,1)S(1)}, u32[]{:S(2)}, u32[]{:S(2)}) collective-permute-start(bf16[1,64,512]{2,1,0:T(8,128)(2,1)} %get-tuple-element.142), channel_id=1, source_target_pairs={{0,1},{1,2},{2,3},{3,4},{4,5},{5,6},{6,7},{8,9},{9,10},{10,11},{11... | collective-permute-start | bytes 196616 | tf_op jit(solution)/shard_map/ppermute | solution.py:430
  79.0 85.8 %collective-permute-start.1 = (bf16[1,64,512]{2,1,0:T(8,128)(2,1)S(1)}, bf16[1,64,512]{2,1,0:T(8,128)(2,1)S(1)}, u32[]{:S(2)}, u32[]{:S(2)}) collective-permute-start(bf16[1,64,512]{2,1,0:T(8,128)(2,1)S(1)} %get-tuple-element.143), channel_id=1, source_target_pairs={{1,0},{2,1},{3,2},{4,3},{5,4},{6,5},{7,6},{9,8},{10,9},{11,10},{12... | collective-permute-start | bytes 196616 | tf_op jit(solution)/shard_map/ppermute | solution.py:431
  231.5 13.8 %collective-permute-start.6 = (bf16[1,64,512]{2,1,0:T(8,128)(2,1)}, bf16[1,64,512]{2,1,0:T(8,128)(2,1)}, u32[]{:S(2)}, u32[]{:S(2)}) collective-permute-start(bf16[1,64,512]{2,1,0:T(8,128)(2,1)} %get-tuple-element.140), channel_id=1, source_target_pairs={{0,1},{1,2},{2,3},{3,4},{4,5},{5,6},{6,7},{8,9},{9,10},{10,11},{11... | collective-permute-start | bytes 196616 | tf_op jit(solution)/shard_map/ppermute | solution.py:430
  233.4 11.9 %collective-permute-start.7 = (bf16[1,64,512]{2,1,0:T(8,128)(2,1)}, bf16[1,64,512]{2,1,0:T(8,128)(2,1)S(1)}, u32[]{:S(2)}, u32[]{:S(2)}) collective-permute-start(bf16[1,64,512]{2,1,0:T(8,128)(2,1)} %get-tuple-element.141), channel_id=1, source_target_pairs={{1,0},{2,1},{3,2},{4,3},{5,4},{6,5},{7,6},{9,8},{10,9},{11,10},{12... | collective-permute-start | bytes 196616 | tf_op jit(solution)/shard_map/ppermute | solution.py:431
  235.3 15.1 %collective-permute-start.2 = (bf16[1,64,512]{2,1,0:T(8,128)(2,1)}, bf16[1,64,512]{2,1,0:T(8,128)(2,1)}, u32[]{:S(2)}, u32[]{:S(2)}) collective-permute-start(bf16[1,64,512]{2,1,0:T(8,128)(2,1)} %get-tuple-element.138), channel_id=1, source_target_pairs={{0,1},{1,2},{2,3},{3,4},{4,5},{5,6},{6,7},{8,9},{9,10},{10,11},{11... | collective-permute-start | bytes 196616 | tf_op jit(solution)/shard_map/ppermute | solution.py:430
  240.5 9.9 %collective-permute-start.3 = (bf16[1,64,512]{2,1,0:T(8,128)(2,1)}, bf16[1,64,512]{2,1,0:T(8,128)(2,1)S(1)}, u32[]{:S(2)}, u32[]{:S(2)}) collective-permute-start(bf16[1,64,512]{2,1,0:T(8,128)(2,1)} %get-tuple-element.139), channel_id=1, source_target_pairs={{1,0},{2,1},{3,2},{4,3},{5,4},{6,5},{7,6},{9,8},{10,9},{11,10},{12... | collective-permute-start | bytes 196616 | tf_op jit(solution)/shard_map/ppermute | solution.py:431
  293.9 97.2 %all-gather.15.cloned.1.call-start = ((), (), s32[]{:S(2)}) async-start(), calls=%async_computation.1 | async-start | bytes 2359296 | tf_op jit(solution)/shard_map/all_gather | solution.py:568
  295.0 146.0 %all-gather.21.cloned.1.call-start = ((), (), s32[]{:S(2)}) async-start(), calls=%async_computation.4 | async-start | bytes 2359296 | tf_op jit(solution)/shard_map/all_gather | solution.py:673
  296.1 194.7 %all-gather.23.cloned.1.call-start = ((), (), s32[]{:S(2)}) async-start(), calls=%async_computation.5 | async-start | bytes 2359296 | tf_op jit(solution)/shard_map/all_gather | solution.py:674
  299.7 240.9 %all-gather.17.cloned.1.call-start = ((), (), s32[]{:S(2)}) async-start(), calls=%async_computation.2 | async-start | bytes 2359296 | tf_op jit(solution)/shard_map/all_gather | solution.py:567
  301.8 288.6 %all-gather.19.cloned.1.call-start = ((), (), s32[]{:S(2)}) async-start(), calls=%async_computation.3 | async-start | bytes 2359296 | tf_op jit(solution)/shard_map/all_gather | solution.py:568
  302.9 337.0 %all-gather.25.cloned.1.call-start = ((), (), s32[]{:S(2)}) async-start(), calls=%async_computation.6 | async-start | bytes 2359296 | tf_op jit(solution)/shard_map/all_gather | solution.py:673
  304.0 387.1 %all-gather.27.cloned.1.call-start = ((), (), s32[]{:S(2)}) async-start(), calls=%async_computation.7 | async-start | bytes 2359296 | tf_op jit(solution)/shard_map/all_gather | solution.py:674
  738.5 28.3 %collective-permute-start.8 = (bf16[1,64,512]{2,1,0:T(8,128)(2,1)}, bf16[1,64,512]{2,1,0:T(8,128)(2,1)}, u32[]{:S(2)}, u32[]{:S(2)}) collective-permute-start(bf16[1,64,512]{2,1,0:T(8,128)(2,1)} %get-tuple-element.134), channel_id=1, source_target_pairs={{0,1},{1,2},{2,3},{3,4},{4,5},{5,6},{6,7},{8,9},{9,10},{10,11},{11... | collective-permute-start | bytes 196616 | tf_op jit(solution)/shard_map/ppermute | solution.py:430
  741.2 25.6 %collective-permute-start.9 = (bf16[1,64,512]{2,1,0:T(8,128)(2,1)}, bf16[1,64,512]{2,1,0:T(8,128)(2,1)}, u32[]{:S(2)}, u32[]{:S(2)}) collective-permute-start(bf16[1,64,512]{2,1,0:T(8,128)(2,1)} %get-tuple-element.135), channel_id=1, source_target_pairs={{1,0},{2,1},{3,2},{4,3},{5,4},{6,5},{7,6},{9,8},{10,9},{11,10},{12... | collective-permute-start | bytes 196616 | tf_op jit(solution)/shard_map/ppermute | solution.py:431
  746.9 29.8 %collective-permute-start.12 = (bf16[1,64,512]{2,1,0:T(8,128)(2,1)}, bf16[1,64,512]{2,1,0:T(8,128)(2,1)S(1)}, u32[]{:S(2)}, u32[]{:S(2)}) collective-permute-start(bf16[1,64,512]{2,1,0:T(8,128)(2,1)} %get-tuple-element.136), channel_id=1, source_target_pairs={{0,1},{1,2},{2,3},{3,4},{4,5},{5,6},{6,7},{8,9},{9,10},{10,11},{11... | collective-permute-start | bytes 196616 | tf_op jit(solution)/shard_map/ppermute | solution.py:430
  751.5 25.2 %collective-permute-start.13 = (bf16[1,64,512]{2,1,0:T(8,128)(2,1)}, bf16[1,64,512]{2,1,0:T(8,128)(2,1)S(1)}, u32[]{:S(2)}, u32[]{:S(2)}) collective-permute-start(bf16[1,64,512]{2,1,0:T(8,128)(2,1)} %get-tuple-element.137), channel_id=1, source_target_pairs={{1,0},{2,1},{3,2},{4,3},{5,4},{6,5},{7,6},{9,8},{10,9},{11,10},{12... | collective-permute-start | bytes 196616 | tf_op jit(solution)/shard_map/ppermute | solution.py:431
  821.8 100.4 %collective-permute-start.10 = (bf16[1,64,512]{2,1,0:T(8,128)(2,1)}, bf16[1,64,512]{2,1,0:T(8,128)(2,1)}, u32[]{:S(2)}, u32[]{:S(2)}) collective-permute-start(bf16[1,64,512]{2,1,0:T(8,128)(2,1)} %copy.145), channel_id=1, source_target_pairs={{0,1},{1,2},{2,3},{3,4},{4,5},{5,6},{6,7},{8,9},{9,10},{10,11},{11... | collective-permute-start | bytes 196616 | tf_op jit(solution)/shard_map/ppermute | solution.py:430
  825.4 96.9 %collective-permute-start.11 = (bf16[1,64,512]{2,1,0:T(8,128)(2,1)}, bf16[1,64,512]{2,1,0:T(8,128)(2,1)S(1)}, u32[]{:S(2)}, u32[]{:S(2)}) collective-permute-start(bf16[1,64,512]{2,1,0:T(8,128)(2,1)} %copy.148), channel_id=1, source_target_pairs={{1,0},{2,1},{3,2},{4,3},{5,4},{6,5},{7,6},{9,8},{10,9},{11,10},{12... | collective-permute-start | bytes 196616 | tf_op jit(solution)/shard_map/ppermute | solution.py:431
  916.1 10.1 %collective-permute-start.14 = (bf16[1,64,512]{2,1,0:T(8,128)(2,1)}, bf16[1,64,512]{2,1,0:T(8,128)(2,1)S(1)}, u32[]{:S(2)}, u32[]{:S(2)}) collective-permute-start(bf16[1,64,512]{2,1,0:T(8,128)(2,1)} %copy.164), channel_id=1, source_target_pairs={{0,1},{1,2},{2,3},{3,4},{4,5},{5,6},{6,7},{8,9},{9,10},{10,11},{11... | collective-permute-start | bytes 196616 | tf_op jit(solution)/shard_map/ppermute | solution.py:430
  920.0 6.3 collective-permute-start.15
  (197 other events, 9051.0 us)
Sparse Core Ops, SparseCore 0:
  294.0 46.8 all-gather.12
  343.1 47.9 all-gather.14
  393.2 47.8 all-gather.20
  443.0 47.7 all-gather.22
  492.8 47.7 all-gather.16
  542.6 47.7 all-gather.18
  592.5 47.3 all-gather.24
  642.6 48.4 all-gather.26

commit v2 on v1

--- a/solution.py
+++ b/solution.py
@@ -347,77 +347,963 @@
     return at
 
 
-def gather_kernel(nz, rows, *refs):
-    count = len(rows)
-    shards, wholes, (sems, local) = refs[:count], refs[count : 2 * count], refs[2 * count :]
-    here = Place()
-    enter(here, nz)
-    gathers = []
-    for k in range(count):
-        at = weight_places(wholes[k], rows[k])
-        gathers.append(Gather(here, nz, at, sems.at[k]))
-        own = pltpu.make_async_copy(shards[k], at(here.z, here.x, here.d), local.at[k])
-        own.start()
-    for k in range(count):
-        pltpu.make_async_copy(shards[k], gathers[k].own(here.z), local.at[k]).wait()
-        for step in gathers[k].program():
+BF = jnp.bfloat16
+F32 = jnp.float32
+ROW = 8
+PARAMS = 16
+
+
+def both(a, b):
+    return jnp.logical_and(a, b)
+
+
+def cols(a, b):
+    return lax.dot_general(a, b, (((1,), (1,)), ((), ())), preferred_element_type=F32)
+
+
+def mm(a, b):
+    return jnp.dot(a, b, preferred_element_type=F32)
+
+
+class Unit(Place):
+    def __init__(self):
+        super().__init__()
+        self.q = self.x * 2 + self.c
+        self.mu = self.z % 2
+        self.alone = both(both(self.c == self.z % 2, self.x == self.z // 2), self.c == self.z // 2)
+
+    def peer(self, q):
+        return {"dp": self.y * 2 + q % 2, "blk": self.z * 2 + q // 2}
+
+    def worker(self, m):
+        return {"dp": self.y * 2 + self.z % 2, "blk": (2 * self.c + m) * 2 + self.z // 2}
+
+    def keeper(self, h):
+        return {"dp": self.y * 2 + self.z // 2, "blk": self.q * 2 + h}
+
+    def line(self, k):
+        return {"dp": self.d, "blk": ((self.z + k) % 4) * 2 + self.x}
+
+    def enter(self, shares, lines):
+        barrier = pltpu.get_barrier_semaphore()
+
+        def greet(device):
+            pl.semaphore_signal(barrier, inc=1, device_id=device, device_id_type=MESH)
+
+        for k in (1, 2, 3):
+            greet(self.peer((self.q + k) % 4))
+        count = 3
+        if lines:
+            greet(self.yn)
+            for k in (1, 2, 3):
+                greet(self.line(k))
+            count += 4
+        if shares:
+            for m in (0, 1):
+                pl.when(jnp.logical_not(both(self.alone, self.c == m)))(lambda m=m: greet(self.worker(m)))
+            for h in (0, 1):
+                pl.when(jnp.logical_not(both(self.alone, self.x == h)))(lambda h=h: greet(self.keeper(h)))
+            count = count + 4 - 2 * self.alone.astype(jnp.int32)
+        pl.semaphore_wait(barrier, count)
+
+
+class Share:
+    def __init__(self, u, sems, local):
+        self.u, self.sems, self.local = u, sems, local
+
+    def send(self, src, dst):
+        u = self.u
+        for m in (0, 1):
+            mine = both(u.alone, u.c == m)
+            place = dst.at[pl.ds(4 * u.x, 4)]
+            pl.when(mine)(lambda: pltpu.make_async_copy(src.at[m], place, self.local).start())
+            pl.when(jnp.logical_not(mine))(
+                lambda: remote(src.at[m], place, self.sems.at[0, m], self.sems.at[1, u.x], u.worker(m)).start()
+            )
+
+    def wait(self, src, dst):
+        u = self.u
+        for h in (0, 1):
+            mine = both(u.alone, u.x == h)
+            place = dst.at[pl.ds(4 * h, 4)]
+            pl.when(mine)(lambda: pltpu.make_async_copy(src.at[0], place, self.local).wait())
+            pl.when(jnp.logical_not(mine))(
+                lambda: remote(place, place, self.sems.at[0, 0], self.sems.at[1, h], u.keeper(h)).wait_recv()
+            )
+
+    def sent(self, src, dst):
+        u = self.u
+        for m in (0, 1):
+            place = dst.at[pl.ds(4 * u.x, 4)]
+            pl.when(jnp.logical_not(both(u.alone, u.c == m)))(
+                lambda: remote(src.at[m], place, self.sems.at[0, m], self.sems.at[1, u.x], u.worker(m)).wait_send()
+            )
+
+    def back(self, src, dst):
+        u = self.u
+        for h in (0, 1):
+            mine = both(u.alone, u.x == h)
+            piece = src.at[pl.ds(4 * h, 4)]
+            pl.when(mine)(lambda: pltpu.make_async_copy(piece, dst.at[u.mu], self.local).start())
+            pl.when(jnp.logical_not(mine))(
+                lambda: remote(piece, dst.at[u.mu], self.sems.at[0, h], self.sems.at[1, u.mu], u.keeper(h)).start()
+            )
+
+    def back_wait(self, src, dst):
+        u = self.u
+        for m in (0, 1):
+            mine = both(u.alone, u.c == m)
+            pl.when(mine)(lambda: pltpu.make_async_copy(src.at[pl.ds(0, 4)], dst.at[m], self.local).wait())
+            pl.when(jnp.logical_not(mine))(
+                lambda: remote(dst.at[m], dst.at[m], self.sems.at[0, 0], self.sems.at[1, m], u.worker(m)).wait_recv()
+            )
+        for h in (0, 1):
+            pl.when(jnp.logical_not(both(u.alone, u.x == h)))(
+                lambda: remote(
+                    src.at[pl.ds(4 * h, 4)], dst.at[u.mu], self.sems.at[0, h], self.sems.at[1, u.mu], u.keeper(h)
+                ).wait_send()
+            )
+
+
+class Swap:
+    def __init__(self, u, buf, sems):
+        self.u, self.buf, self.sems = u, buf, sems
+
+    def cps(self):
+        u = self.u
+        out = []
+        for k in (1, 2, 3):
+            out.append((self.buf.at[u.q], self.sems.at[0, k], self.sems.at[1, u.q], u.peer((u.q + k) % 4)))
+        return out
+
+    def send(self):
+        for ref, s, r, dev in self.cps():
+            remote(ref, ref, s, r, dev).start()
+
+    def wait(self):
+        u = self.u
+        for k in (1, 2, 3):
+            p = (u.q + k) % 4
+            remote(self.buf.at[p], self.buf.at[p], self.sems.at[0, k], self.sems.at[1, p], u.peer(p)).wait_recv()
+
+    def sent(self):
+        for ref, s, r, dev in self.cps():
+            remote(ref, ref, s, r, dev).wait_send()
+
+    def total(self):
+        return self.buf[0] + self.buf[1] + self.buf[2] + self.buf[3]
+
+
+class Spread:
+    def __init__(self, u, buf, sems, parts):
+        self.u, self.buf, self.sems, self.parts = u, buf, sems, parts
+
+    def cp(self, kind, p, part):
+        u = self.u
+        ref = self.buf.at[p, part]
+        device = u.xn if kind == 1 else u.cn
+        return remote(ref, ref, self.sems.at[0, kind, part], self.sems.at[1, kind, part], device)
+
+    def send(self, part):
+        self.cp(1, self.u.q, part).start()
+        self.cp(0, self.u.q, part).start()
+
+    def across(self):
+        return (1 - self.u.x) * 2 + self.u.c
+
+    def relay(self, part):
+        copy = self.cp(1, self.across(), part)
+        copy.wait_recv()
+        self.cp(2, self.across(), part).start()
+
+    def wait(self, part):
+        u = self.u
+        self.cp(0, u.x * 2 + 1 - u.c, part).wait_recv()
+        self.cp(2, (1 - u.x) * 2 + 1 - u.c, part).wait_recv()
+
+    def sent(self, part):
+        self.cp(1, self.u.q, part).wait_send()
+        self.cp(0, self.u.q, part).wait_send()
+        self.cp(2, self.across(), part).wait_send()
+
+
+class Halo:
+    def __init__(self, u, buf, sems):
+        self.u, self.buf, self.sems = u, buf, sems
+
+    def cp(self, downward):
+        u, buf = self.u, self.buf
+        if downward:
+            return remote(buf.at[1], buf.at[ROW + 1], self.sems.at[0, 0], self.sems.at[1, 0], u.peer(jnp.maximum(u.q - 1, 0)))
+        return remote(buf.at[ROW], buf.at[0], self.sems.at[0, 1], self.sems.at[1, 1], u.peer(jnp.minimum(u.q + 1, 3)))
+
+    def send(self):
+        u, buf = self.u, self.buf
+        pl.when(u.q > 0)(lambda: self.cp(True).start())
+        pl.when(u.q < 3)(lambda: self.cp(False).start())
+
+        @pl.when(u.q == 0)
+        def _():
+            buf[0] = jnp.zeros(buf.shape[1:], buf.dtype)
+
+        @pl.when(u.q == 3)
+        def _():
+            buf[ROW + 1] = jnp.zeros(buf.shape[1:], buf.dtype)
+
+    def wait(self):
+        u = self.u
+        pl.when(u.q > 0)(lambda: self.cp(False).wait_recv())
+        pl.when(u.q < 3)(lambda: self.cp(True).wait_recv())
+
+    def sent(self):
+        u = self.u
+        pl.when(u.q > 0)(lambda: self.cp(True).wait_send())
+        pl.when(u.q < 3)(lambda: self.cp(False).wait_send())
+
+
+def canvas_of(rows, limits):
+    return (rows >= limits[0:1]).astype(F32) + (rows >= limits[1:2]).astype(F32)
+
+
+def row_numbers(u, offset, shape):
+    return (ROW * u.q + offset + lax.broadcasted_iota(jnp.int32, shape, 0)).astype(F32)
+
+
+def counts_of(limits, total_rows):
+    each = 64.0 * 16.0
+    return (limits[0:1] * each, (limits[1:2] - limits[0:1]) * each, (total_rows - limits[1:2]) * each)
+
+
+def group_total(sums):
+    width = sums.shape[1]
+    lane = lax.broadcasted_iota(jnp.int32, sums.shape, 1)
+    for step in (1, 2, 4, 8):
+        after = pltpu.roll(sums, width - step, 1)
+        before = pltpu.roll(sums, step, 1)
+        sums = sums + jnp.where((lane // step) % 2 == 0, after, before)
+    return sums
+
+
+def canvas_sums(first, second, seg):
+    out = []
+    for rows in (first, second):
+        for k in range(CANVASES):
+            out.append(jnp.sum(jnp.where(seg == float(k), rows, 0.0), axis=0, keepdims=True))
+    out.append(jnp.zeros((2, first.shape[1]), F32))
+    return jnp.concatenate(out, axis=0)
+
+
+def by_row(values, seg):
+    return jnp.where(seg == 0.0, values[0], jnp.where(seg == 1.0, values[1], values[2]))
+
+
+def moments(total, counts, seg):
+    grouped = group_total(total)
+    averages, inverses = [], []
+    for k in range(CANVASES):
+        average = grouped[k : k + 1] / counts[k]
+        averages.append(average)
+        inverses.append(lax.rsqrt(grouped[3 + k : 4 + k] / counts[k] - average * average + EPSILON))
+    return by_row(averages, seg), by_row(inverses, seg)
+
+
+def sigmoid(argument):
+    return 0.5 * jnp.tanh(0.5 * argument) + 0.5
+
+
+def each_row(body):
+    lax.fori_loop(0, ROW, lambda r, carry: (body(r), carry)[1], 0)
+
+
+def row_of(ref, r):
+    return ref[pl.ds(r, 1), :]
+
+
+def tap_masks(u, limits, masks):
+    shape = (ROW, limits.shape[1])
+    rows = row_numbers(u, 0, shape)
+    seg = canvas_of(rows, limits)
+    masks[0] = both(canvas_of(rows - 1.0, limits) == seg, rows >= 1.0).astype(F32)
+    masks[1] = both(canvas_of(rows + 1.0, limits) == seg, rows < 4.0 * ROW - 1.0).astype(F32)
+    return seg
+
+
+def shifted(line):
+    position = lax.broadcasted_iota(jnp.int32, line.shape, 0)
+    width = line.shape[0]
+    before = jnp.where(position == 0, 0.0, pltpu.roll(line, 1, 0))
+    after = jnp.where(position == width - 1, 0.0, pltpu.roll(line, width - 1, 0))
+    return before, line, after
+
+
+def taps_inner(buf, masks, taps):
+    def body(s):
+        lines = shifted(buf[s + 1].astype(F32))
+        for k in range(3):
+            taps[3 + k, s] = lines[k].astype(BF)
+
+        @pl.when(s < ROW - 1)
+        def _():
+            mask = masks[0, pl.ds(s + 1, 1), :]
+            for k in range(3):
+                taps[k, s + 1] = (lines[k] * mask).astype(BF)
+
+        @pl.when(s > 0)
+        def _():
+            mask = masks[1, pl.ds(s - 1, 1), :]
+            for k in range(3):
+                taps[6 + k, s - 1] = (lines[k] * mask).astype(BF)
+
+    each_row(body)
+
+
+def taps_outer(buf, masks, taps):
+    for k, line in enumerate(shifted(buf[0].astype(F32))):
+        taps[k, 0] = (line * masks[0, 0:1, :]).astype(BF)
+    for k, line in enumerate(shifted(buf[ROW + 1].astype(F32))):
+        taps[6 + k, ROW - 1] = (line * masks[1, ROW - 1 : ROW, :]).astype(BF)
+
+
+def conv_tile(taps, weight, m, flip):
+    total = None
+    for tap in range(9):
+        left = taps[8 - tap if flip else tap, pl.ds(pl.multiple_of(m * 4, 4), 4)].reshape(256, -1)
+        right = weight[tap * 512 : (tap + 1) * 512, :]
+        term = cols(left, right) if flip else mm(left, right)
+        total = term if total is None else total + term
+    return total.reshape(4, 64, -1)
+
+
+def conv_all(taps, weight, out, flip, between=None):
+    for m in range(2):
+        out[4 * m : 4 * m + 4] = conv_tile(taps, weight, m, flip)
+        if between is not None:
+            between()
+
+
+def conv_weight_grad(act_t, taps, out, first, last):
+    def body(tap, carry):
+        piece = mm(act_t[...], taps[8 - tap].reshape(512, -1))
+        out[pl.ds(pl.multiple_of(tap * 512, 512), 512), :] = piece.astype(BF)
+        return carry
+
+    lax.fori_loop(first, last, body, 0)
+
+
+class Steps:
+    def __init__(self, *programs):
+        self.todo = [step for program in programs for step in program]
+
+    def run(self, count=None):
+        count = len(self.todo) if count is None else count
+        now, self.todo = self.todo[:count], self.todo[count:]
+        for step in now:
             step()
-    for gather in gathers:
-        gather.arrive()
-        gather.finish()
-
-
-def gather_all(shards, nz):
-    rows = [item.shape[0] for item in shards]
+
+
+def attn_places(ref):
+    def at(z, x, d, half=None):
+        place = ref.at[z * 2 + x]
+        lanes = pl.ds(pl.multiple_of(d * 128, 128), 128)
+        if half is None:
+            return place.at[:, lanes]
+        return place.at[pl.ds(half * 128, 128), lanes]
+
+    return at
+
+
+def param_places(ref):
+    def at(z, x, d, half=None):
+        place = ref.at[z * 2 + x]
+        lanes = pl.ds(pl.multiple_of(d * 128, 128), 128)
+        if half is None:
+            return place.at[:, lanes]
+        return place.at[pl.ds(half * 8, 8), lanes]
+
+    return at
+
+
+def forward_kernel(
+    feat, grad, bounds, par, s1, s2, sa,
+    w1_out, w2_out, wa_out, small_out, nall_out, oall_out, resid_out, hidden_out, x_out,
+    w1, w2, wa, pb, bb, xin, oall, nall, taps, a1, a2, masks, hidden, resid, small, rows_a, rows_b, swaps,
+    gsems, local, share_sems, bound_sems, swap_sems, spread_sems, halo_sems, out_sems,
+):
+    u = Unit()
+    u.enter(True, True)
+    groups = []
+    for k, at in enumerate((weight_places(w1, 576), weight_places(w2, 576), attn_places(wa), param_places(pb))):
+        groups.append(Gather(u, 4, at, gsems.at[k]))
+    g1, g2, ga, gp = groups
+    own = [pltpu.make_async_copy(src, group.own(u.z), local.at[k]) for k, (src, group) in enumerate(zip((s1, s2, sa, par), groups))]
+    for copy in own:
+        copy.start()
+    keep = pltpu.make_async_copy(bounds, bb.at[u.c], local.at[4])
+    keep.start()
+    share_x, share_o = Share(u, share_sems.at[0], local.at[5]), Share(u, share_sems.at[1], local.at[6])
+    share_x.send(feat, xin)
+    bound_cp = remote(bounds, bb.at[u.c], bound_sems.at[0], bound_sems.at[1], u.cn)
+    bound_cp.start()
+    for copy in own:
+        copy.wait()
+    lead, follow = gp.program(), g1.program()
+    early = []
+    for k in range(len(follow)):
+        early += [follow[k], lead[k]]
+    early = Steps(early)
+    early.run(12)
+    keep.wait()
+    remote(bounds, bb.at[1 - u.c], bound_sems.at[0], bound_sems.at[1], u.cn).wait_recv()
+    limits = jnp.where(u.mu == 0, bb[u.z // 2, 0:2, :], bb[u.z // 2, 2:4, :])
+    seg = tap_masks(u, limits, masks)
+    counts = counts_of(limits, 4.0 * ROW)
+    early.run(8)
+
+    share_x.wait(feat, xin)
+    share_o.send(grad, oall.at[u.z])
+    swap = [Swap(u, swaps.at[k], swap_sems.at[k]) for k in range(3)]
+    halo = [Halo(u, buf, halo_sems.at[k]) for k, buf in enumerate((a1, a2))]
+
+    def sums_of(value):
+        def body(r):
+            line = value(r)
+            rows_a[pl.ds(r, 1), :] = jnp.sum(line, axis=0, keepdims=True)
+            rows_b[pl.ds(r, 1), :] = jnp.sum(line * line, axis=0, keepdims=True)
+
+        each_row(body)
+
+    def norm_send(k, value):
+        sums_of(value)
+        swap[k].buf[u.q] = canvas_sums(rows_a[...], rows_b[...], seg)
+        swap[k].send()
+
+    def norm_stats(k):
+        swap[k].wait()
+        average, inverse = moments(swap[k].total(), counts, seg)
+        small[2 * k] = average
+        small[2 * k + 1] = inverse
+
+    def normal(k, value, r):
+        line = (value(r) - small[2 * k, pl.ds(r, 1), :]) * small[2 * k + 1, pl.ds(r, 1), :]
+        return line * small[6, 2 * k : 2 * k + 1, :] + small[6, 2 * k + 1 : 2 * k + 2, :]
+
+    def feature(r):
+        return xin[r].astype(F32)
+
+    norm_send(0, feature)
+    early.run()
+    gp.arrive()
+    total = pb[0, 0:8, :]
+    for b in range(1, 8):
+        total = total + pb[b, 0:8, :]
+    small[6] = total
+    small[7] = jnp.concatenate([limits, jnp.zeros((6, limits.shape[1]), F32)], axis=0)
+    norm_stats(0)
+
+    def activate(k, value, buf):
+        def body(r):
+            line = normal(k, value, r)
+            buf[r + 1] = (line * sigmoid(line)).astype(BF)
+
+        each_row(body)
+
+    later = Steps(g2.program(), ga.program())
+    later.run(1)
+    activate(0, feature, a1)
+    halo[0].send()
+    taps_inner(a1, masks, taps)
+    halo[0].wait()
+    taps_outer(a1, masks, taps)
+    share_o.wait(grad, oall.at[u.q])
+    later.run(2)
+    g1.arrive()
+    spread_o = Spread(u, oall_parts(oall), spread_sems.at[0], 2)
+    spread_n = Spread(u, oall_parts(nall), spread_sems.at[1], 2)
+    for part in range(2):
+        spread_o.send(part)
+
+    copies = [pltpu.make_async_copy(w1, w1_out, out_sems.at[0])]
+    copies[-1].start()
+    conv_all(taps, w1, hidden, False, lambda: later.run(2))
+
+    def middle(r):
+        return hidden[r]
+
+    norm_send(1, middle)
+    later.run(6)
+    copies.append(pltpu.make_async_copy(hidden, hidden_out, out_sems.at[1]))
+    copies[-1].start()
+    norm_stats(1)
+    activate(1, middle, a2)
+    halo[1].send()
+    taps_inner(a2, masks, taps)
+    halo[1].wait()
+    taps_outer(a2, masks, taps)
+    later.run(len(later.todo) - 14)
+    for part in range(2):
+        spread_o.relay(part)
+    g2.arrive()
+
+    copies.append(pltpu.make_async_copy(w2, w2_out, out_sems.at[2]))
+    copies[-1].start()
+    for m in range(2):
+        piece = conv_tile(taps, w2, m, False)
+        resid[4 * m : 4 * m + 4] = piece + xin[4 * m : 4 * m + 4].astype(F32)
+        later.run(2)
+
+    def last(r):
+        return resid[r]
+
+    norm_send(2, last)
+    later.run(4)
+    copies.append(pltpu.make_async_copy(resid, resid_out, out_sems.at[3]))
+    copies.append(pltpu.make_async_copy(xin, x_out, out_sems.at[4]))
+    for copy in copies[-2:]:
+        copy.start()
+    norm_stats(2)
+
+    def normed_row(r):
+        nall[u.q, r] = normal(2, last, r).astype(BF)
+
+    for part in range(2):
+        lax.fori_loop(4 * part, 4 * part + 4, lambda r, carry: (normed_row(r), carry)[1], 0)
+        spread_n.send(part)
+    later.run()
+    ga.arrive()
+    copies.append(pltpu.make_async_copy(wa, wa_out, out_sems.at[5]))
+    copies.append(pltpu.make_async_copy(small, small_out, out_sems.at[6]))
+    for copy in copies[-2:]:
+        copy.start()
+    for part in range(2):
+        spread_n.relay(part)
+    for part in range(2):
+        spread_o.wait(part)
+        spread_n.wait(part)
+    copies.append(pltpu.make_async_copy(oall, oall_out, out_sems.at[7]))
+    copies.append(pltpu.make_async_copy(nall, nall_out, out_sems.at[8]))
+    for copy in copies[-2:]:
+        copy.start()
+    for group in groups:
+        group.finish()
+    bound_cp.wait_send()
+    share_x.sent(feat, xin)
+    share_o.sent(grad, oall.at[u.z])
+    for item in swap + halo:
+        item.sent()
+    for item in (spread_o, spread_n):
+        for part in range(2):
+            item.sent(part)
+    for copy in copies:
+        copy.wait()
+
+
+class oall_parts:
+    def __init__(self, ref):
+        self.ref = ref
+
+    @property
+    def at(self):
+        return self
+
+    def __getitem__(self, index):
+        member, part = index
+        return self.ref.at[member, pl.ds(part * (ROW // 2), ROW // 2)]
+
+
+ANY = pl.BlockSpec(memory_space=pl.ANY)
+VM = pl.BlockSpec(memory_space=pltpu.VMEM)
+
+
+def forward_call(features, out_grad, limits, params, s1, s2, sa):
+    full = lambda shape, kind: jax.ShapeDtypeStruct(shape, kind)
+    dma = pltpu.SemaphoreType.DMA
+    rows = (ROW, 64, 512)
     return pl.pallas_call(
-        functools.partial(gather_kernel, nz, rows),
-        out_shape=[jax.ShapeDtypeStruct((r * nz * 2, 512), jnp.bfloat16) for r in rows],
-        in_specs=[pl.BlockSpec(memory_space=pltpu.VMEM)] * len(rows),
-        out_specs=[pl.BlockSpec(memory_space=pltpu.VMEM)] * len(rows),
+        forward_kernel,
+        out_shape=[
+            full((4608, 512), BF), full((4608, 512), BF), full((8, 256, 512), BF), full((8, 8, 512), F32),
+            full((4, *rows), BF), full((4, *rows), BF), full(rows, F32), full(rows, F32), full(rows, BF),
+        ],
+        in_specs=[VM] * 7,
+        out_specs=[ANY] * 9,
         scratch_shapes=[
-            pltpu.SemaphoreType.DMA((len(rows), 2, Gather.SEMS)),
-            pltpu.SemaphoreType.DMA((len(rows),)),
+            pltpu.VMEM((4608, 512), BF), pltpu.VMEM((4608, 512), BF), pltpu.VMEM((8, 256, 512), BF),
+            pltpu.VMEM((8, PARAMS, 512), F32), pltpu.VMEM((2, 8, 512), F32), pltpu.VMEM(rows, BF),
+            pltpu.VMEM((4, *rows), BF), pltpu.VMEM((4, *rows), BF), pltpu.VMEM((9, *rows), BF),
+            pltpu.VMEM((ROW + 2, 64, 512), BF), pltpu.VMEM((ROW + 2, 64, 512), BF), pltpu.VMEM((2, ROW, 512), F32),
+            pltpu.VMEM(rows, F32), pltpu.VMEM(rows, F32), pltpu.VMEM((8, 8, 512), F32),
+            pltpu.VMEM((ROW, 512), F32), pltpu.VMEM((ROW, 512), F32), pltpu.VMEM((3, 4, 8, 512), F32),
+            dma((4, 2, Gather.SEMS)), dma((7,)), dma((2, 2, 2)), dma((2,)), dma((3, 2, 4)), dma((2, 2, 3, 2)),
+            dma((2, 2, 2)), dma((9,)),
         ],
-        compiler_params=pltpu.CompilerParams(collective_id=0, has_side_effects=True, vmem_limit_bytes=56 << 20),
-    )(*shards)
-
-
-def scatter_kernel(nz, rows, *refs):
-    count = len(rows)
-    wholes, outs = refs[:count], refs[count : 2 * count]
-    bufs, sems = refs[2 * count : -1], refs[-1]
-    here = Place()
-    enter(here, nz)
-    scatters = []
-    for k in range(count):
-        at = weight_places(wholes[k], rows[k])
-        half = rows[k] // 2
-
-        def part(ref, h, half=half):
-            return ref.at[pl.ds(h * half, half)]
-
-        scatters.append(Scatter(here, nz, at, part, sems.at[k], bufs[5 * k : 5 * k + 5]))
-    for k in range(count):
-        for step in scatters[k].program(outs[k]):
-            step()
-    for scatter in scatters:
-        scatter.finish()
-
-
-def scatter_all(wholes, nz):
-    rows = [item.shape[0] // (nz * 2) for item in wholes]
-    scratch = []
-    for r in rows:
-        for shape in ((4, nz, r, 128), (4, nz, r, 128), (2, nz, r // 2, 128), (2, nz, r, 128), (2, nz, r, 128)):
-            scratch.append(pltpu.VMEM(shape, jnp.bfloat16))
+        compiler_params=pltpu.CompilerParams(collective_id=2, has_side_effects=True, vmem_limit_bytes=58 << 20),
+    )(features, out_grad, limits, params, s1, s2, sa)
+
+
+def unit_inputs(features, bounds, out_grad, norms, conv1, conv2, attn):
+    d, b = lax.axis_index("dp"), lax.axis_index("blk")
+    limits = jnp.broadcast_to(bounds.reshape(-1).astype(F32)[:, None], (4, 512))
+    limits = jnp.concatenate([limits, jnp.zeros((4, 512), F32)])
+    rows = jnp.stack([item.astype(F32) for item in norms])
+    mine = jnp.where(d == b // 2, rows, 0.0)
+    params = jnp.concatenate([jnp.where(b % 2 == 0, mine, 0.0), jnp.where(b % 2 == 1, mine, 0.0)], axis=1)
+    params = jnp.concatenate([params, jnp.zeros((PARAMS - 6, 128), F32)])
+    return (features[0], out_grad[0], limits, params, conv1, conv2, jnp.concatenate(attn))
+
+
+def forward_all(
+    features, bounds, out_grad, norm1_gain, norm1_shift, conv1_weight, norm2_gain, norm2_shift, conv2_weight,
+    norm3_gain, norm3_shift, query_weight, key_weight, value_weight, output_weight,
+):
+    norms = (norm1_gain, norm1_shift, norm2_gain, norm2_shift, norm3_gain, norm3_shift)
+    attn = (query_weight, key_weight, value_weight, output_weight)
+    return forward_call(*unit_inputs(features, bounds, out_grad, norms, conv1_weight, conv2_weight, attn))
+
+
+def attention_kernel(
+    nall, oall, wa, resid, small,
+    act_out, ga_out, gn_out,
+    qall, kall, vall, doall, scores, slopes, heads, gq, gk, gv, lcol, dcol, ld, dk, dv,
+    sems,
+):
+    u = Unit()
+    u.enter(False, False)
+    swap = Swap(u, ld, sems)
+    scale = 512.0 ** (-0.5)
+    limits = small[7]
+    low, high = limits[0:1, 0:1], limits[1:2, 0:1]
+
+    def matrix(k):
+        return wa[:, pl.ds(k * 64, 64), :].reshape(512, 512)
+
+    def project(i, carry):
+        tokens, upstream = nall[i], oall[i]
+        qall[i] = mm(tokens, matrix(0)).astype(BF)
+        kall[i] = mm(tokens, matrix(1)).astype(BF)
+        vall[i] = mm(tokens, matrix(2)).astype(BF)
+        doall[i] = cols(upstream, matrix(3)).astype(BF)
+        return carry
+
+    lax.fori_loop(0, 4, project, 0)
+
+    def canvas(rows):
+        return (rows >= low).astype(F32) + (rows >= high).astype(F32)
+
+    def seg_col(q, offset, count):
+        token = offset + lax.broadcasted_iota(jnp.int32, (count, 1), 0)
+        return canvas((ROW * q + token // 64).astype(F32))
+
+    def seg_row(q):
+        token = lax.broadcasted_iota(jnp.int32, (1, 512), 1)
+        return canvas((ROW * q + token // 64).astype(F32))
+
+    def queries(j, carry):
+        block = pl.ds(pl.multiple_of(j * 256, 256), 256)
+        query, upstream = qall[u.q, block], doall[u.q, block]
+        seg = seg_col(u.q, j * 256, 256)
+        most = jnp.full((256, 1), NEGATIVE, F32)
+        for i in range(4):
+            part = jnp.where(seg == seg_row(i), cols(query, kall[i]) * scale, NEGATIVE)
+            scores[i] = part
+            most = jnp.maximum(most, jnp.max(part, axis=1, keepdims=True))
+        total = jnp.zeros((256, 1), F32)
+        for i in range(4):
+            part = jnp.exp(scores[i] - most)
+            total = total + jnp.sum(part, axis=1, keepdims=True)
+            scores[i] = part
+        inverse = 1.0 / total
+        found = jnp.zeros((256, 512), F32)
+        correction = jnp.zeros((256, 1), F32)
+        for i in range(4):
+            part = scores[i] * inverse
+            scores[i] = part
+            found = found + mm(part.astype(BF), vall[i])
+            slope = cols(upstream, vall[i])
+            slopes[i] = slope
+            correction = correction + jnp.sum(part * slope, axis=1, keepdims=True)
+        heads[block, :] = found.astype(BF)
+        back = jnp.zeros((256, 512), F32)
+        for i in range(4):
+            back = back + mm((scores[i] * (slopes[i] - correction)).astype(BF), kall[i])
+        gq[block, :] = (back * scale).astype(BF)
+        lcol[block, :] = jnp.broadcast_to(most + jnp.log(total), (256, 128))
+        dcol[block, :] = jnp.broadcast_to(correction, (256, 128))
+        return carry
+
+    lax.fori_loop(0, 2, queries, 0)
+    ld[u.q] = jnp.concatenate([lcol[...].T[0:1], dcol[...].T[0:1], jnp.zeros((6, 512), F32)], axis=0)
+    swap.send()
+    low_heads = heads[...]
+    act_out[...] = (resid[...] + mm(low_heads, matrix(3)).reshape(ROW, 64, 512)).astype(BF)
+    ga_out[:, 192:256, :] = mm(low_heads.T, oall[u.q]).astype(BF).reshape(8, 64, 512)
+    dk[...] = jnp.zeros_like(dk)
+    dv[...] = jnp.zeros_like(dv)
+    swap.wait()
+
+    def keys(step, carry):
+        i, j = step // 2, step % 2
+        block = pl.ds(pl.multiple_of(j * 256, 256), 256)
+        key, value = kall[u.q, block], vall[u.q, block]
+        query, upstream = qall[i], doall[i]
+        shared = seg_col(u.q, j * 256, 256) == seg_row(i)
+        part = jnp.where(shared, cols(key, query) * scale, NEGATIVE)
+        part = jnp.where(shared, jnp.exp(part - ld[i, 0:1, :]), 0.0)
+        dv[block, :] += mm(part.astype(BF), upstream)
+        slope = cols(value, upstream) - ld[i, 1:2, :]
+        dk[block, :] += mm((part * slope).astype(BF), query)
+        return carry
+
+    lax.fori_loop(0, 8, keys, 0)
+    gk[...] = (dk[...] * scale).astype(BF)
+    gv[...] = dv[...].astype(BF)
+    tokens = nall[u.q].T
+    total = None
+    for k, part in enumerate((gq, gk, gv)):
+        ga_out[:, k * 64 : (k + 1) * 64, :] = mm(tokens, part[...]).astype(BF).reshape(8, 64, 512)
+        term = cols(part[...], matrix(k))
+        total = term if total is None else total + term
+    gn_out[...] = total.reshape(ROW, 64, 512)
+    swap.sent()
+
+
+def attention_call(nall, oall, wa, resid, small):
+    rows = (ROW, 64, 512)
+    full = lambda shape, kind: jax.ShapeDtypeStruct(shape, kind)
+    square = (512, 512)
     return pl.pallas_call(
-        functools.partial(scatter_kernel, nz, rows),
-        out_shape=[jax.ShapeDtypeStruct((r, 128), jnp.float32) for r in rows],
-        in_specs=[pl.BlockSpec(memory_space=pltpu.VMEM)] * len(rows),
-        out_specs=[pl.BlockSpec(memory_space=pltpu.VMEM)] * len(rows),
-        scratch_shapes=scratch + [pltpu.SemaphoreType.DMA((len(rows), 2, Scatter.SEMS))],
-        compiler_params=pltpu.CompilerParams(collective_id=1, has_side_effects=True, vmem_limit_bytes=60 << 20),
-    )(*wholes)
+        attention_kernel,
+        out_shape=[full(rows, BF), full((8, 256, 512), BF), full(rows, F32)],
+        in_specs=[VM] * 5,
+        out_specs=[VM] * 3,
+        scratch_shapes=[pltpu.VMEM((4, *square), BF)] * 4
+        + [pltpu.VMEM((4, 256, 512), F32)] * 2
+        + [pltpu.VMEM(square, BF)] * 4
+        + [pltpu.VMEM((512, 128), F32)] * 2
+        + [pltpu.VMEM((4, 8, 512), F32)]
+        + [pltpu.VMEM(square, F32)] * 2
+        + [pltpu.SemaphoreType.DMA((2, 4))],
+        compiler_params=pltpu.CompilerParams(collective_id=3, has_side_effects=True, vmem_limit_bytes=58 << 20),
+    )(nall.reshape(4, *square), oall.reshape(4, *square), wa, resid, small)
+
+
+def backward_kernel(
+    act, ga, gn, resid, hidden, xin, small,
+    w1_in, w2_in, oall_in,
+    act_back, grad_back, g1_out, g2_out, ga_out, norm_out,
+    w1, w2, og, taps, a1, a2, act_t1, act_t2, masks, big, gres, grad_low, wg1, wg2, rows_a, rows_b, swaps,
+    psum_y, psum_z, mine,
+    c1, c2, c3, c4, c5, d1, d2, d3, d4, d5, e1, e2, e3, e4, e5,
+    ssems, local, share_sems, swap_sems, halo_sems, py_sems, pz_sems,
+):
+    u = Unit()
+    u.enter(True, True)
+    mine[...] = jnp.zeros_like(mine)
+    loads = [
+        pltpu.make_async_copy(oall_in.at[u.q], og, local.at[0]),
+        pltpu.make_async_copy(w2_in, w2, local.at[1]),
+        pltpu.make_async_copy(w1_in, w1, local.at[2]),
+    ]
+    for copy in loads:
+        copy.start()
+    share_a, share_g = Share(u, share_sems.at[0], local.at[3]), Share(u, share_sems.at[1], local.at[4])
+
+    def part_of(half):
+        return lambda ref, h: ref.at[pl.ds(h * half, half)]
+
+    sum_a = Scatter(u, 4, attn_places(ga), part_of(128), ssems.at[0], (c1, c2, c3, c4, c5))
+    sum_2 = Scatter(u, 4, weight_places(wg2, 576), part_of(288), ssems.at[1], (d1, d2, d3, d4, d5))
+    sum_1 = Scatter(u, 4, weight_places(wg1, 576), part_of(288), ssems.at[2], (e1, e2, e3, e4, e5))
+    steps = Steps(sum_a.program(ga_out))
+    steps.run(2)
+    share_a.back(act, act_back)
+
+    limits = small[7]
+    seg = tap_masks(u, limits, masks)
+    counts = counts_of(limits, 4.0 * ROW)
+    swap = [Swap(u, swaps.at[k], swap_sems.at[k]) for k in range(3)]
+    halo = [Halo(u, buf, halo_sems.at[k]) for k, buf in enumerate((a1, a2))]
+
+    def xhat(k, value, r):
+        return (value(r) - small[2 * k, pl.ds(r, 1), :]) * small[2 * k + 1, pl.ds(r, 1), :]
+
+    def param(j):
+        return small[6, j : j + 1, :]
+
+    def send_sums(k, value, incoming):
+        def body(r):
+            line = incoming(r)
+            rows_a[pl.ds(r, 1), :] = jnp.sum(line, axis=0, keepdims=True)
+            rows_b[pl.ds(r, 1), :] = jnp.sum(line * xhat(k, value, r), axis=0, keepdims=True)
+
+        each_row(body)
+        swap[k].buf[u.q] = canvas_sums(rows_a[...], rows_b[...], seg)
+        swap[k].send()
+
+    def take_sums(k):
+        swap[k].wait()
+        total = swap[k].total()
+        mine[2 * k : 2 * k + 1, :] = jnp.sum(total[3:6], axis=0, keepdims=True)
+        mine[2 * k + 1 : 2 * k + 2, :] = jnp.sum(total[0:3], axis=0, keepdims=True)
+        grouped = group_total(total * param(2 * k))
+        rows_a[...] = by_row([grouped[j : j + 1] / counts[j] for j in range(3)], seg)
+        rows_b[...] = by_row([grouped[3 + j : 4 + j] / counts[j] for j in range(3)], seg)
+
+    def back(k, value, incoming, r):
+        line = incoming(r) * param(2 * k) - row_of(rows_a, r) - xhat(k, value, r) * row_of(rows_b, r)
+        return line * small[2 * k + 1, pl.ds(r, 1), :]
+
+    def third(r):
+        return resid[r]
+
+    def second(r):
+        return hidden[r]
+
+    def first(r):
+        return xin[r].astype(F32)
+
+    def swish_of(k, value, out):
+        def body(r):
+            line = xhat(k, value, r) * param(2 * k) + param(2 * k + 1)
+            out[r] = (line * sigmoid(line)).astype(BF)
+
+        each_row(body)
+
+    def slope_of(k, value, r):
+        line = xhat(k, value, r) * param(2 * k) + param(2 * k + 1)
+        part = sigmoid(line)
+        return part * (1.0 + line * (1.0 - part))
+
+    send_sums(2, third, lambda r: gn[r])
+    swish_of(1, second, grad_low)
+    act_t2[...] = grad_low[...].reshape(512, 512).T
+    steps.run(4)
+    take_sums(2)
+    loads[0].wait()
+
+    def resid_grad(r):
+        line = og[r].astype(F32) + back(2, third, lambda s: gn[s], r)
+        gres[r] = line
+        a2[r + 1] = line.astype(BF)
+
+    each_row(resid_grad)
+    halo[1].send()
+    taps_inner(a2, masks, taps)
+    halo[1].wait()
+    taps_outer(a2, masks, taps)
+
+    loads[1].wait()
+    conv_weight_grad(act_t2, taps, wg2, 0, 9)
+    steps = Steps(steps.todo, sum_2.program(g2_out))
+    steps.run(6)
+    for m in range(2):
+        big[4 * m : 4 * m + 4] = conv_tile(taps, w2, m, True)
+        steps.run(3)
+
+    def scaled(k, value):
+        def body(r):
+            big[r] = big[r] * slope_of(k, value, r)
+
+        each_row(body)
+
+    scaled(1, second)
+    send_sums(1, second, lambda r: big[r])
+    swish_of(0, first, grad_low)
+    act_t1[...] = grad_low[...].reshape(512, 512).T
+    steps.run(3)
+    take_sums(1)
+
+    def hidden_grad(r):
+        a1[r + 1] = back(1, second, lambda s: big[s], r).astype(BF)
+
+    each_row(hidden_grad)
+    halo[0].send()
+    taps_inner(a1, masks, taps)
+    halo[0].wait()
+    taps_outer(a1, masks, taps)
+    steps.run(4)
+
+    loads[2].wait()
+    conv_weight_grad(act_t1, taps, wg1, 0, 9)
+    steps = Steps(steps.todo, sum_1.program(g1_out))
+    steps.run(12)
+    for m in range(2):
+        big[4 * m : 4 * m + 4] = conv_tile(taps, w1, m, True)
+        steps.run(4)
+    scaled(0, first)
+    send_sums(0, first, lambda r: big[r])
+    steps.run(2)
+    take_sums(0)
+
+    def input_grad(r):
+        grad_low[r] = (gres[r] + back(0, first, lambda s: big[s], r)).astype(BF)
+
+    each_row(input_grad)
+    share_g.back(grad_low, grad_back)
+
+    py = remote(mine, psum_y, py_sems.at[0], py_sems.at[1], u.yn)
+    py.start()
+    steps.run(4)
+    py.wait()
+    psum_z[u.z] = mine[...] + psum_y[...]
+    pz = []
+    for k in (1, 2, 3):
+        pz.append(remote(psum_z.at[u.z], psum_z.at[u.z], pz_sems.at[0, k], pz_sems.at[1, u.z], u.line(k)))
+        pz[-1].start()
+    steps.run()
+    for k in (1, 2, 3):
+        other = (u.z + k) % 4
+        remote(psum_z.at[other], psum_z.at[other], pz_sems.at[0, k], pz_sems.at[1, other], u.line(k)).wait_recv()
+    norm_out[...] = psum_z[0] + psum_z[1] + psum_z[2] + psum_z[3]
+    for copy in pz:
+        copy.wait_send()
+    share_a.back_wait(act, act_back)
+    share_g.back_wait(grad_low, grad_back)
+    for item in (sum_a, sum_2, sum_1):
+        item.finish()
+    for item in swap + halo:
+        item.sent()
+
+
+def backward_call(act, ga, gn, resid, hidden, xin, small, w1, w2, oall):
+    full = lambda shape, kind: jax.ShapeDtypeStruct(shape, kind)
+    dma = pltpu.SemaphoreType.DMA
+    rows = (ROW, 64, 512)
+    padded = (ROW + 2, 64, 512)
+    sums = []
+    for r in (256, 576, 576):
+        for shape in ((4, 4, r, 128), (4, 4, r, 128), (2, 4, r // 2, 128), (2, 4, r, 128), (2, 4, r, 128)):
+            sums.append(pltpu.VMEM(shape, BF))
+    return pl.pallas_call(
+        backward_kernel,
+        out_shape=[
+            full((2, 4, 64, 512), BF), full((2, 4, 64, 512), BF), full((576, 128), F32), full((576, 128), F32),
+            full((256, 128), F32), full((8, 512), F32),
+        ],
+        in_specs=[VM] * 7 + [ANY] * 3,
+        out_specs=[VM] * 6,
+        scratch_shapes=[
+            pltpu.VMEM((4608, 512), BF), pltpu.VMEM((4608, 512), BF), pltpu.VMEM(rows, BF), pltpu.VMEM((9, *rows), BF),
+            pltpu.VMEM(padded, BF), pltpu.VMEM(padded, BF), pltpu.VMEM((512, 512), BF), pltpu.VMEM((512, 512), BF),
+            pltpu.VMEM((2, ROW, 512), F32), pltpu.VMEM(rows, F32), pltpu.VMEM(rows, F32), pltpu.VMEM(rows, BF),
+            pltpu.VMEM((4608, 512), BF), pltpu.VMEM((4608, 512), BF), pltpu.VMEM((ROW, 512), F32),
+            pltpu.VMEM((ROW, 512), F32), pltpu.VMEM((3, 4, 8, 512), F32), pltpu.VMEM((8, 512), F32),
+            pltpu.VMEM((4, 8, 512), F32), pltpu.VMEM((8, 512), F32), *sums,
+            dma((3, 2, Scatter.SEMS)), dma((5,)), dma((2, 2, 2)), dma((3, 2, 4)), dma((2, 2, 2)), dma((2,)), dma((2, 4)),
+        ],
+        compiler_params=pltpu.CompilerParams(collective_id=4, has_side_effects=True, vmem_limit_bytes=62 << 20),
+    )(act, ga, gn, resid, hidden, xin, small, w1, w2, oall)
+
+
+def unit_shards(*args):
+    w1, w2, wa, small, nall, oall, resid, hidden, xin = forward_all(*args)
+    act, ga, gn = attention_call(nall, oall, wa, resid, small)
+    act_back, grad_back, g1, g2, ga, norms = backward_call(act, ga, gn, resid, hidden, xin, small, w1, w2, oall)
+    norms = lax.dynamic_slice_in_dim(norms, lax.axis_index("blk") * 64, 64, axis=1)
+    ga = ga.reshape(4, 64, 128)
+    return (
+        act_back.astype(F32)[None], grad_back.astype(F32)[None], norms[0], norms[1], g1, norms[2], norms[3], g2,
+        norms[4], norms[5], ga[0], ga[1], ga[2], ga[3],
+    )
 
 
 def extended(shard, sides, width):
@@ -884,29 +1770,6 @@
     return (activation, input_grad, local_grads)
 
 
-def by_block(whole, nz):
-    split = whole.reshape(nz * 2, 4, -1, 512)
-    return [split[:, k].reshape(-1, 512) for k in range(4)]
-
-
-def fast_collect(conv1_weight, conv2_weight, query_weight, key_weight, value_weight, output_weight, *norms):
-    nz = lax.axis_size("blk") // 2
-    stacked = jnp.concatenate([query_weight, key_weight, value_weight, output_weight])
-    w1, w2, wa = gather_all((conv1_weight, conv2_weight, stacked), nz)
-    rows = tuple(lax.all_gather(item, "blk", axis=0, tiled=True) for item in norms)
-    return (w1, w2, *by_block(wa, nz)), rows
-
-
-def fast_reduce(gradients):
-    nz = lax.axis_size("blk") // 2
-    low_grads = [item.astype(jnp.bfloat16) for item in gradients[:6]]
-    attn = jnp.stack([item.reshape(nz * 2, -1, 512) for item in low_grads[2:]], axis=1).reshape(-1, 512)
-    g2, ga, g1 = scatter_all((low_grads[1], attn, low_grads[0]), nz)
-    ga = ga.reshape(4, -1, 128)
-    norms = tuple(lax.psum_scatter(item, "blk", scatter_dimension=0, tiled=True) for item in gradients[6:])
-    return (g1, g2, ga[0], ga[1], ga[2], ga[3]) + tuple(lax.psum(norms, "dp"))
-
-
 def shards(
     features,
     bounds,
@@ -927,25 +1790,24 @@
     blocks = lax.axis_size("blk")
     position = lax.axis_index("blk")
     micro_count = features.shape[1]
-    local_sums = None
+    shard_sums = None
     outputs = []
     input_grads = []
-    near = lax.axis_size("dp") == 4 and blocks == 8
-    matrices, norm_params = (fast_collect if near else collect)(
-        conv1_weight,
-        conv2_weight,
-        query_weight,
-        key_weight,
-        value_weight,
-        output_weight,
-        norm1_gain,
-        norm1_shift,
-        norm2_gain,
-        norm2_shift,
-        norm3_gain,
-        norm3_shift,
-    )
     for micro_index in range(micro_count):
+        matrices, norm_params = collect(
+            conv1_weight,
+            conv2_weight,
+            query_weight,
+            key_weight,
+            value_weight,
+            output_weight,
+            norm1_gain,
+            norm1_shift,
+            norm2_gain,
+            norm2_shift,
+            norm3_gain,
+            norm3_shift,
+        )
         activation, input_grad, local_grads = one_batch(
             features[0, micro_index],
             bounds[0, micro_index],
@@ -957,12 +1819,12 @@
         )
         outputs.append(activation)
         input_grads.append(input_grad)
-        local_sums = (
-            local_grads
-            if local_sums is None
-            else tuple((acc + new for acc, new in zip(local_sums, local_grads)))
+        reduced = reduce_all(local_grads)
+        shard_sums = (
+            reduced
+            if shard_sums is None
+            else tuple((acc + new for acc, new in zip(shard_sums, reduced)))
         )
-    shard_sums = (fast_reduce if near else reduce_all)(local_sums)
     activations = jnp.stack(outputs)[None]
     input_grad_all = jnp.stack(input_grads)[None]
     return (
@@ -1017,4 +1879,5 @@
         P("blk", "dp"),
         P("blk", "dp"),
     )
-    return jax.shard_map(shards, mesh=mesh, in_specs=in_specs, out_specs=out_specs, check_vma=False)
+    near = mesh.shape["dp"] == 4 and mesh.shape["blk"] == 8
+    return jax.shard_map(unit_shards if near else shards, mesh=mesh, in_specs=in_specs, out_specs=out_specs, check_vma=False)

time: 1000 us -> 281 us (0.28)
  blocking collectives: 241 us -> 0 us
  waiting for transfers between devices: 213 us -> 0 us
  matrix products: 137 us -> 0 us
  local copies, waits for them, and re-layouts: 125 us -> 5.76 us
  Pallas kernels: 151 us -> 269 us
  other arithmetic: 64.1 us -> 5.56 us
  starting transfers between devices: 39.3 us -> 0 us
  between operations: 23 us -> 0.72 us
    all_gather x8 -> x0, waiting for transfers between devices: 213 us -> none  [the longest x2 93.4 us: attention_key_grad(): lax.all_gather(heads_grad.astype(jnp.float32), 'blk', axis=0, tiled=True)]
    psum x7 -> x0, blocking collectives: 147 us -> none  [the longest x3 76.7 us: norm_backward(): lax.psum((group_sums(member, scaled), group_sums(member, scaled * grouped...]
    dot_general x96 -> x0, matrix products: 137 us -> none  [the longest x4 19.4 us: conv_apply(): result = jnp.dot(stacked, weight_matrix, preferred_element_type=jnp.float32)]
    pallas_call x2 -> x3, Pallas kernels: 151 us -> 269 us  [the longest x1 120 us: forward_call(): pl.pallas_call(forward_kernel, out_shape=[full((4608, 512), BF), full((46...]
    all_gather x4 -> x0, blocking collectives: 76.6 us -> none  [the longest x2 38.4 us: attention_key_grad(): lax.all_gather(correction, 'blk', axis=0, tiled=True)]
    ppermute x16 -> x0, starting transfers between devices: 38.8 us -> none  [the longest x8 28.3 us: extended(): before = lax.ppermute(last, axis, up)]
    unnamed x419 -> x6, local copies, waits for them, and re-layouts: 32.5 us -> 1.44 us
    dot_general x9 -> x0, local copies, waits for them, and re-layouts: 21.8 us -> none  [the longest x5 20.8 us: conv_apply(): result = jnp.dot(stacked, weight_matrix, preferred_element_type=jnp.float32)]
  transfers between devices with their start and end apart: 24 -> 0, of which waited for: 8 -> 0; matrix products, arithmetic and copies ran while one was open for 17% -> 0% of each run, Pallas kernels for 15% -> 0%
where the time goes in v2:
time: 281 us
  Pallas kernels  269 us (96%)
  local copies, waits for them, and re-layouts  5.76 us (2%)
  other arithmetic  5.56 us (2%)
    pallas_call x1, Pallas kernels, forward_call(): pl.pallas_call(forward_kernel, out_shape=[full((4608, 512), BF), full((46...  120 us
    pallas_call x1, Pallas kernels, backward_call(): pl.pallas_call(backward_kernel, out_shape=[full((2, 4, 64, 512), BF), ful...  120 us
    pallas_call x1, Pallas kernels, attention_call(): pl.pallas_call(attention_kernel, out_shape=[full(rows, BF), full((8, 256,...  29.4 us

profile of v2, /device:TPU:0, one launch (start us, length us, event | category | flops | bytes accessed | tf_op | source)
XLA Modules:
  0.0 280.7 jit_solution(5671413375026267928)
XLA Ops:
  0.7 0.7 convert_element_type.18
  1.4 0.1 convert_element_type.19
  1.4 0.8 stack.36
  2.2 0.7 select_maximum_fusion.par
  2.9 0.7 concatenate.15.bounds
  3.6 1.4 pad_maximum_fusion.sa
  5.0 119.7 %shard_map.254 = (bf16[4608,512]{1,0:T(8,128)(2,1)}, bf16[4608,512]{1,0:T(8,128)(2,1)}, bf16[8,256,512]{2,1,0:T(8,128)(2,1)}, f32[8,8,512]{2,1,0:T(8,128)}, bf16...) custom-call(bf16[2,4,64,512]{3,2,1,0:T(8,128)(2,1)} %bitcast.30, ...), custom_call_target="tpu_custom_call" | custom-call | tf_op jit(solution)/shard_map/pallas_call | solution.py:921
  124.7 29.4 %shard_map.255 = (bf16[8,64,512]{2,1,0:T(8,128)(2,1)}, bf16[8,256,512]{2,1,0:T(8,128)(2,1)}, f32[8,64,512]{2,1,0:T(8,128)}) custom-call(bf16[4,512,512]{2,1,0:T(8,128)(2,1)} %bitcast.29, bf16[4,512,512]{2,1,0:T(8,128)(2,1)} %bitcast.28, bf16[8,256,512]{2,1,0:T(8,128)(2,1)} %get-tuple-element.34.wa, f32[8,64,512]{2,1,0:T(8,128)} %get-tuple-element.35.resid, ...), custom_call_target="tpu_custom_call" | custom-call | tf_op jit(solution)/shard_map/pallas_call | solution.py:1073
  154.0 119.6 %shard_map.256 = (bf16[2,4,64,512]{3,2,1,0:T(8,128)(2,1)}, bf16[2,4,64,512]{3,2,1,0:T(8,128)(2,1)}, f32[576,128]{1,0:T(8,128)}, f32[576,128]{1,0:T(8,128)}, f32[256,128]{1,0:T(8,128)}, /*index=5*/f32[8,512]{1,0:T(8,128)}) custom-call(bf16[8,64,512]{2,1,0:T(8,128)(2,1)} %get-tuple-element.37.act, bf16[8,256,512]{2,1,0:T(8,128)(2,1)} %get-tuple-element.38.ga, ...), custom_call_target="tpu_custom_call" | custom-call | tf_op jit(solution)/shard_map/pallas_call | solution.py:1276
  273.6 0.0 copy-start.1
  273.6 0.0 copy-start
  273.6 0.8 constant_dynamic-slice_fusion
  274.4 0.5 slice_bitcast_fusion
  275.0 1.5 fusion.2
  276.4 2.8 bitcast_convert_fusion
  279.2 0.0 copy-done.1
  279.2 0.7 copy.31
  280.0 0.0 copy-done
  280.0 0.7 copy.32
  (2 shorter events, 0.0 us)
Async XLA Ops:
  273.6 5.6 %copy-start.1 = (f32[576,128]{1,0:T(8,128)S(1)}, f32[576,128]{1,0:T(8,128)}, u32[]{:S(2)}) copy-start(f32[576,128]{1,0:T(8,128)} %get-tuple-element.82) | copy-start | bytes 884740
  273.6 6.3 %copy-start = (f32[576,128]{1,0:T(8,128)S(1)}, f32[576,128]{1,0:T(8,128)}, u32[]{:S(2)}) copy-start(f32[576,128]{1,0:T(8,128)} %get-tuple-element.85) | copy-start | bytes 884740

commit v3 on v0

--- a/solution.py
+++ b/solution.py
@@ -1,6 +1,11 @@
+import functools
+import types
+
 import jax
 import jax.numpy as jnp
 from jax import lax
+from jax.experimental import pallas as pl
+from jax.experimental.pallas import tpu as pltpu
 from jax.sharding import PartitionSpec as P
 
 GROUPS = 32
@@ -10,6 +15,1364 @@
 EPSILON = 1e-06
 HIGHEST = lax.Precision.HIGHEST
 NEGATIVE = -1e30
+MESH = pl.DeviceIdType.MESH
+def in_order(s):
+    s.ow(), s.gpl0(), s.g1l0(), s.gpo0(), s.gao0(), s.g2o0(), s.g2l0(), s.gpl1()
+    s.gpo1(), s.gal0(), s.g1l1(), s.g1o1(), s.gpl2(), s.g2l1(), s.g1o0(), s.gpo2()
+    s.gpy1(), s.gpx1(), s.g1l2(), s.gpl3(), s.g2o1(), s.gpo3(), s.g1o2(), s.gpx0()
+    s.gpx3(), s.gpy0(), s.g1l3(), s.g1o3(), s.xs(), s.g2l2(), s.gpy2(), s.g1x1()
+    s.gal1(), s.g1x2(), s.gpx2(), s.gpy3(), s.bw(), s.g2x0(), s.g1x3(), s.g1y0()
+    s.g2l3(), s.g1y2(), s.g1y1(), s.gal2(), s.g1y3(), s.g2o3(), s.g1x0(), s.n1a()
+    s.gao1(), s.gpd2(), s.os(), s.gpd0(), s.g2o2(), s.gpd1(), s.gpd3(), s.n1b()
+    s.gal3(), s.n1c(), s.gao2(), s.g1d0(), s.g1d1(), s.g1d3(), s.n1d(), s.g2y3()
+    s.g1d2(), s.g2y0(), s.g2x3(), s.g1a(), s.g2y1(), s.gao3(), s.n1e(), s.c10()
+    s.c11(), s.n2a(), s.g2x2(), s.g2y2(), s.gay1(), s.gax3(), s.gay2(), s.g2x1()
+    s.gay3(), s.g2d3(), s.gay0(), s.n2b(), s.n2c(), s.ob(), s.g2d2(), s.n2d()
+    s.gax1(), s.n2e(), s.g2d0(), s.g2d1(), s.g2a(), s.c20(), s.gax2(), s.gad1()
+    s.c21(), s.n3a(), s.gad2(), s.gax0(), s.n3b(), s.n3c(), s.t2(), s.gad3()
+    s.or0(), s.or1(), s.gad0(), s.gaa(), s.po1(), s.pj1(), s.pj0(), s.po0()
+    s.po2(), s.nr0(), s.po3(), s.nr1(), s.pj2(), s.pj3(), s.qf(), s.qb()
+    s.hw(), s.gz(), s.hd(), s.ks(), s.an(), s.b3a(), s.aw(), s.rab3()
+    s.rab0(), s.t1(), s.rab1(), s.rab2(), s.rac3(), s.b3b(), s.rac1(), s.b3c()
+    s.rac2(), s.rac0(), s.b3d(), s.d20(), s.w20(), s.d21(), s.b2a(), s.r2b0()
+    s.w21(), s.r2b1(), s.w22(), s.r2b3(), s.rae2(), s.b2b(), s.r2b2(), s.rae1()
+    s.r2c2(), s.b2c(), s.raf2(), s.r2c3(), s.r2c0(), s.b2d(), s.d10(), s.d11()
+    s.b1a(), s.rae3(), s.r2e2(), s.w10(), s.r2e3(), s.raf1(), s.rae0(), s.b1m()
+    s.r2c1(), s.b1b(), s.raf3(), s.r2e0(), s.w11(), s.r1b0(), s.r2f2(), s.ps()
+    s.w12(), s.r1b3(), s.r1b1(), s.r1b2(), s.r1c3(), s.r2f3(), s.r1e3(), s.r1c2()
+    s.raf0(), s.r1f3(), s.r2e1(), s.r1e2(), s.py(), s.r2f0(), s.r1c1(), s.r2f1()
+    s.r1e1(), s.r1c0(), s.rat(), s.r1f2(), s.r1f1(), s.pz(), s.r1e0(), s.r2t()
+    s.r1f0(), s.r1t()
+
+
+DIRECT = (False, False, False, False)
+LIMIT = 60 << 20
+SPLIT, SPLIT_A = 432, 192
+CUT, CUT_A = 112, 48
+
+
+class Place:
+    def __init__(self):
+        self.d = lax.axis_index("dp")
+        self.b = lax.axis_index("blk")
+        self.y, self.c = self.d // 2, self.d % 2
+        self.z, self.x = self.b // 2, self.b % 2
+        self.up = {"dp": self.d, "blk": self.b + 2}
+        self.down = {"dp": self.d, "blk": self.b - 2}
+        self.xn = {"dp": self.d, "blk": self.z * 2 + 1 - self.x}
+        self.yn = {"dp": (1 - self.y) * 2 + self.c, "blk": self.b}
+        self.cn = {"dp": self.y * 2 + 1 - self.c, "blk": self.b}
+
+
+def remote(src, dst, send, recv, device):
+    return pltpu.make_async_remote_copy(
+        src_ref=src, dst_ref=dst, send_sem=send, recv_sem=recv, device_id=device, device_id_type=MESH
+    )
+
+
+def steps_of(z, nz):
+    visits = [(z, None)]
+    for k in range(1, nz):
+        visits.append((z - k, z >= k))
+        visits.append((z + k, z + k < nz))
+    return visits
+
+
+def guarded(valid, body):
+    if valid is None:
+        body()
+    else:
+        pl.when(valid)(body)
+
+
+class Gather:
+    SEMS = 40
+
+    def __init__(self, here, nz, at, sems, direct):
+        self.here, self.nz, self.at, self.sems, self.direct = here, nz, at, sems, direct
+        self.visits = steps_of(here.z, nz)
+
+    def sem(self, kind, z, way):
+        base = {"z": 0, "x": 4, "y": 8, "da": 12, "db": 16, "co": 20, "cx": 24, "cy": 28, "cd": 32, "zd": 36}[kind]
+        return self.sems.at[way, base + z]
+
+    def cp(self, kind, z, src, device, skind=None):
+        return remote(src, src, self.sem(skind or kind, z, 0), self.sem(kind, z, 1), device)
+
+    def own(self, z):
+        return self.at(z, self.here.x, self.here.d, None)
+
+    def colx(self, z, half=None):
+        return self.at(z, 1 - self.here.x, self.here.d, half)
+
+    def coly(self, z, half=None):
+        return self.at(z, self.here.x, (1 - self.here.y) * 2 + self.here.c, half)
+
+    def cold(self, z, half=None):
+        return self.at(z, 1 - self.here.x, (1 - self.here.y) * 2 + self.here.c, half)
+
+    def line_cp(self, k):
+        here = self.here
+        z = (here.z + k) % self.nz
+        device = {"dp": here.d, "blk": z * 2 + here.x}
+        return remote(self.own(here.z), self.own(here.z), self.sem("z", z, 0), self.sem("z", here.z, 1), device)
+
+    def line(self, j):
+        z, valid = self.visits[j]
+        here = self.here
+        if j == 0 and self.direct:
+            for k in range(1, self.nz):
+                self.line_cp(k).start()
+            return
+
+        def body():
+            src = self.own(z)
+            if j > 0:
+                self.cp("z", z, src, here.up).wait_recv()
+            if self.direct:
+                return
+            if j == 0 or j % 2 == 1:
+
+                @pl.when(here.z < self.nz - 1)
+                def _():
+                    self.cp("z", z, src, here.up).start()
+
+            if j == 0 or j % 2 == 0:
+
+                @pl.when(here.z > 0)
+                def _():
+                    self.cp("z", z, src, here.down, "zd").start()
+
+        guarded(valid, body)
+
+    def out(self, j):
+        z, valid = self.visits[j]
+        here = self.here
+
+        def body():
+            src = self.own(z)
+            self.cp("x", z, src, here.xn).start()
+            self.cp("y", z, src, here.yn).start()
+            self.cp("co", z, src, here.cn).start()
+
+        guarded(valid, body)
+
+    def have(self, j):
+        self.line(j)
+        self.out(j)
+
+    def from_x(self, j):
+        z, valid = self.visits[j]
+
+        def body():
+            self.cp("x", z, self.colx(z), self.here.xn).wait_recv()
+            self.cp("da", z, self.colx(z, 0), self.here.yn).start()
+            self.cp("cx", z, self.colx(z), self.here.cn).start()
+
+        guarded(valid, body)
+
+    def from_y(self, j):
+        z, valid = self.visits[j]
+
+        def body():
+            self.cp("y", z, self.coly(z), self.here.yn).wait_recv()
+            self.cp("db", z, self.coly(z, 1), self.here.xn).start()
+            self.cp("cy", z, self.coly(z), self.here.cn).start()
+
+        guarded(valid, body)
+
+    def cross(self, j):
+        self.from_x(j)
+        self.from_y(j)
+
+    def diagonal(self, j):
+        z, valid = self.visits[j]
+        here = self.here
+
+        def body():
+            self.cp("da", z, self.cold(z, 0), here.yn).wait_recv()
+            self.cp("db", z, self.cold(z, 1), here.xn).wait_recv()
+            self.cp("cd", z, self.cold(z), here.cn).start()
+
+        guarded(valid, body)
+
+    def arrive(self):
+        here = self.here
+        near, far = here.y * 2 + 1 - here.c, (1 - here.y) * 2 + 1 - here.c
+        for z in range(self.nz):
+            for kind, x, d in (("co", here.x, near), ("cx", 1 - here.x, near), ("cy", here.x, far), ("cd", 1 - here.x, far)):
+                self.cp(kind, z, self.at(z, x, d, None), here.cn).wait_recv()
+
+    def finish(self):
+        here = self.here
+        if self.direct:
+            for k in range(1, self.nz):
+                self.line_cp(k).wait_send()
+        for j, (z, valid) in enumerate(self.visits):
+
+            def body():
+                src = self.own(z)
+                if not self.direct and (j == 0 or j % 2 == 1):
+
+                    @pl.when(here.z < self.nz - 1)
+                    def _():
+                        self.cp("z", z, src, here.up).wait_send()
+
+                if not self.direct and (j == 0 or j % 2 == 0):
+
+                    @pl.when(here.z > 0)
+                    def _():
+                        self.cp("z", z, src, here.down, "zd").wait_send()
+
+                self.cp("x", z, src, here.xn).wait_send()
+                self.cp("y", z, src, here.yn).wait_send()
+                self.cp("da", z, self.colx(z, 0), here.yn).wait_send()
+                self.cp("db", z, self.coly(z, 1), here.xn).wait_send()
+                for kind in ("co", "cx", "cy", "cd"):
+                    self.cp(kind, z, src, here.cn).wait_send()
+
+            guarded(valid, body)
+
+    def table(self, name):
+        kinds = {"l": self.line, "o": self.out, "x": self.from_x, "y": self.from_y, "d": self.diagonal}
+        found = {name + "a": self.arrive}
+        for kind, step in kinds.items():
+            for k in range(self.nz):
+                js = (0,) if k == 0 else (2 * k - 1, 2 * k)
+                found["%s%s%d" % (name, kind, k)] = lambda js=js, step=step: [step(j) for j in js]
+        return found
+
+
+class Scatter:
+    SEMS = 48
+
+    def __init__(self, here, nz, at, core_at, part, sems, bufs):
+        self.here, self.nz, self.at, self.core_at, self.part, self.sems = here, nz, at, core_at, part, sems
+        self.half, self.side, self.last = bufs
+        self.visits = steps_of(here.z, nz)[::-1]
+
+    def sem(self, kind, z, way):
+        base = ("c0", "c1", "c2", "c3", "da", "db", "xa", "xb", "ya", "yb", "l").index(kind) * 4
+        return self.sems.at[way, base + z]
+
+    def cp(self, kind, z, src, dst, device):
+        return remote(src, dst, self.sem(kind, z, 0), self.sem(kind, z, 1), device)
+
+    def places(self, z, c):
+        here = self.here
+        y, x = here.y, here.x
+        return [(z, x, y * 2 + c), (z, 1 - x, y * 2 + c), (z, x, (1 - y) * 2 + c), (z, 1 - x, (1 - y) * 2 + c)]
+
+    def mine(self, z, k):
+        return self.at(*self.places(z, self.here.c)[k])
+
+    def core_cp(self, z, k):
+        place = self.places(z, 1 - self.here.c)[k]
+        return self.cp("c%d" % k, z, self.at(*place), self.core_at(k, *place), self.here.cn)
+
+    def core_in(self, z, k):
+        place = self.core_at(k, *self.places(z, self.here.c)[k])
+        self.cp("c%d" % k, z, place, place, self.here.cn).wait_recv()
+        return place[...]
+
+    def begin(self, z):
+        for k in (3, 1, 2, 0):
+            self.core_cp(z, k).start()
+
+    def half_cp(self, z, h):
+        return self.cp(("da", "db")[h], z, self.part(self.mine(z, 3), h), self.half[h].at[z], (self.here.xn, self.here.yn)[h])
+
+    def side_cp(self, z, side, h):
+        return self.cp(
+            "xy"[side] + "ab"[h], z, self.part(self.mine(z, 1 + side), h), self.part(self.side.at[side, z], h),
+            (self.here.xn, self.here.yn)[side],
+        )
+
+    def corner(self, j):
+        z, valid = self.visits[j]
+
+        def body():
+            for k in (3, 1, 2):
+                place = self.mine(z, k)
+                place[...] = place[...] + self.core_in(z, k)
+                if k == 3:
+                    self.half_cp(z, 0).start()
+                    self.half_cp(z, 1).start()
+                else:
+                    self.side_cp(z, k - 1, k - 1).start()
+
+        guarded(valid, body)
+
+    def edges(self, j):
+        z, valid = self.visits[j]
+
+        def body():
+            for side, h in ((0, 1), (1, 0)):
+                self.half_cp(z, h).wait_recv()
+                place = self.part(self.mine(z, 1 + side), h)
+                place[...] = place[...] + self.half[h][z]
+                self.side_cp(z, side, h).start()
+
+        guarded(valid, body)
+
+    def column(self, j, out):
+        z, valid = self.visits[j]
+        here = self.here
+
+        def body():
+            place = self.mine(z, 0)
+            total = place[...].astype(jnp.float32) + self.core_in(z, 0).astype(jnp.float32)
+            for side in (0, 1):
+                for h in (0, 1):
+                    self.side_cp(z, side, h).wait_recv()
+                total = total + self.side[side, z].astype(jnp.float32)
+            if j == len(self.visits) - 1:
+                out[...] = total
+            else:
+                place[...] = total.astype(jnp.bfloat16)
+                self.last_cp(z).start()
+
+        guarded(valid, body)
+
+    def last_cp(self, z):
+        here = self.here
+        device = {"dp": here.d, "blk": z * 2 + here.x}
+        return remote(self.mine(z, 0), self.last.at[here.z], self.sem("l", z, 0), self.sem("l", here.z, 1), device)
+
+    def total(self, out):
+        here = self.here
+        for k in range(1, self.nz):
+            z = (here.z + k) % self.nz
+            remote(self.last.at[z], self.last.at[z], self.sem("l", z, 0), self.sem("l", z, 1), here.up).wait_recv()
+            out[...] += self.last[z].astype(jnp.float32)
+
+    def finish(self):
+        for j, (z, valid) in enumerate(self.visits):
+
+            def body():
+                for k in range(4):
+                    self.core_cp(z, k).wait_send()
+                for h in (0, 1):
+                    self.half_cp(z, h).wait_send()
+                    for side in (0, 1):
+                        self.side_cp(z, side, h).wait_send()
+                if j < len(self.visits) - 1:
+                    self.last_cp(z).wait_send()
+
+            guarded(valid, body)
+
+    def table(self, name, out):
+        kinds = {"c": self.corner, "e": self.edges, "f": lambda j: self.column(j, out)}
+        top = 2 * (self.nz - 1)
+        found = {name + "t": lambda: self.total(out)}
+        for z in range(self.nz):
+            found["%sb%d" % (name, z)] = functools.partial(self.begin, z)
+        for kind, step in kinds.items():
+            for k in range(self.nz):
+                js = (top,) if k == 0 else (top - 2 * k, top - 2 * k + 1)
+                found["%s%s%d" % (name, kind, k)] = lambda js=js, step=step: [step(j) for j in js]
+        return found
+
+
+def part_of(ref, half, split, rows):
+    return ref.at[pl.ds(0, split)] if half == 0 else ref.at[pl.ds(split, rows - split)]
+
+
+def weight_places(ref, rows, split=0):
+    def at(z, x, d, half=None):
+        base, count = (z * 2 + x) * rows, rows
+        if half is not None:
+            base, count = base + half * split, rows - split if half else split
+        return ref.at[pl.ds(pl.multiple_of(base, 16), count), pl.ds(pl.multiple_of(d * 128, 128), 128)]
+
+    return at
+
+
+BF = jnp.bfloat16
+F32 = jnp.float32
+ROW = 8
+PARAMS = 16
+
+
+def both(a, b):
+    return jnp.logical_and(a, b)
+
+
+def cols(a, b):
+    return lax.dot_general(a, b, (((1,), (1,)), ((), ())), preferred_element_type=F32)
+
+
+def mm(a, b):
+    return jnp.dot(a, b, preferred_element_type=F32)
+
+
+class Unit(Place):
+    def __init__(self):
+        super().__init__()
+        self.q = jnp.where(self.c == 0, self.x, 3 - self.x)
+        self.mu = self.z % 2
+        self.alone = self.z == self.q
+
+    def member(self, q, z):
+        return {"dp": self.y * 2 + q // 2, "blk": z * 2 + jnp.where(q < 2, q, 3 - q)}
+
+    def peer(self, q):
+        return self.member(q, self.z)
+
+    def worker(self, m):
+        return self.member(self.z, 2 * self.c + m)
+
+    def keeper(self, h):
+        return {"dp": self.y * 2 + self.z // 2, "blk": self.q * 2 + h}
+
+    def column_worker(self, m):
+        return {"dp": self.y * 2 + self.z // 2, "blk": (2 * self.c + m) * 2 + self.x}
+
+    def column_keeper(self, k):
+        return {"dp": self.y * 2 + self.z // 2, "blk": (2 * self.c + k) * 2 + self.x}
+
+    def line(self, k):
+        return {"dp": self.d, "blk": ((self.z + k) % 4) * 2 + self.x}
+
+    def enter(self, shares, lines):
+        barrier = pltpu.get_barrier_semaphore()
+
+        def greet(device):
+            pl.semaphore_signal(barrier, inc=1, device_id=device, device_id_type=MESH)
+
+        for k in (1, 2, 3):
+            greet(self.peer((self.q + k) % 4))
+        count = 3
+        if lines:
+            greet(self.yn)
+            for k in (1, 2, 3):
+                greet(self.line(k))
+            count += 4
+        if shares:
+            for m in (0, 1):
+                pl.when(jnp.logical_not(both(self.alone, self.mu == m)))(lambda m=m: greet(self.worker(m)))
+            for h in (0, 1):
+                pl.when(jnp.logical_not(both(self.alone, self.x == h)))(lambda h=h: greet(self.keeper(h)))
+            near = self.c == self.z // 2
+            for k in (0, 1):
+                pl.when(jnp.logical_not(both(near, self.mu == k)))(lambda k=k: greet(self.column_worker(k)))
+            count = count + 6 - 2 * self.alone.astype(jnp.int32) - near.astype(jnp.int32)
+        pl.semaphore_wait(barrier, count)
+
+
+class Share:
+    def __init__(self, u, sems, local):
+        self.u, self.sems, self.local = u, sems, local
+
+    def send(self, src, dst):
+        u = self.u
+        for m in (0, 1):
+            mine = both(u.alone, u.mu == m)
+            place = dst.at[pl.ds(4 * u.x, 4)]
+            pl.when(mine)(lambda: pltpu.make_async_copy(src.at[m], place, self.local).start())
+            pl.when(jnp.logical_not(mine))(
+                lambda: remote(src.at[m], place, self.sems.at[0, m], self.sems.at[1, u.x], u.worker(m)).start()
+            )
+
+    def wait(self, src, dst):
+        u = self.u
+        for h in (0, 1):
+            mine = both(u.alone, u.x == h)
+            place = dst.at[pl.ds(4 * h, 4)]
+            pl.when(mine)(lambda: pltpu.make_async_copy(src.at[0], place, self.local).wait())
+            pl.when(jnp.logical_not(mine))(
+                lambda: remote(place, place, self.sems.at[0, 0], self.sems.at[1, h], u.keeper(h)).wait_recv()
+            )
+
+    def sent(self, src, dst):
+        u = self.u
+        for m in (0, 1):
+            place = dst.at[pl.ds(4 * u.x, 4)]
+            pl.when(jnp.logical_not(both(u.alone, u.mu == m)))(
+                lambda: remote(src.at[m], place, self.sems.at[0, m], self.sems.at[1, u.x], u.worker(m)).wait_send()
+            )
+
+    def back(self, src, dst):
+        u = self.u
+        for h in (0, 1):
+            mine = both(u.alone, u.x == h)
+            piece = src.at[pl.ds(4 * h, 4)]
+            pl.when(mine)(lambda: pltpu.make_async_copy(piece, dst.at[u.mu], self.local).start())
+            pl.when(jnp.logical_not(mine))(
+                lambda: remote(piece, dst.at[u.mu], self.sems.at[0, h], self.sems.at[1, u.mu], u.keeper(h)).start()
+            )
+
+    def back_wait(self, src, dst):
+        u = self.u
+        for m in (0, 1):
+            mine = both(u.alone, u.mu == m)
+            pl.when(mine)(lambda: pltpu.make_async_copy(src.at[pl.ds(0, 4)], dst.at[m], self.local).wait())
+            pl.when(jnp.logical_not(mine))(
+                lambda: remote(dst.at[m], dst.at[m], self.sems.at[0, 0], self.sems.at[1, m], u.worker(m)).wait_recv()
+            )
+        for h in (0, 1):
+            pl.when(jnp.logical_not(both(u.alone, u.x == h)))(
+                lambda: remote(
+                    src.at[pl.ds(4 * h, 4)], dst.at[u.mu], self.sems.at[0, h], self.sems.at[1, u.mu], u.keeper(h)
+                ).wait_send()
+            )
+
+
+class ColumnShare:
+    def __init__(self, u, buf, sems, local):
+        self.u, self.buf, self.sems, self.local = u, buf, sems, local
+        self.alone = u.c == u.z // 2
+
+    def place(self, z):
+        return self.buf.at[z, pl.ds(4 * self.u.x, 4)]
+
+    def cp(self, src, m):
+        u = self.u
+        return remote(src.at[m], self.place(u.z), self.sems.at[0, m], self.sems.at[1, u.mu], u.column_worker(m))
+
+    def send(self, src):
+        u = self.u
+        for m in (0, 1):
+            mine = both(self.alone, u.mu == m)
+            pl.when(mine)(lambda: pltpu.make_async_copy(src.at[m], self.place(u.z), self.local).start())
+            pl.when(jnp.logical_not(mine))(lambda: self.cp(src, m).start())
+
+    def wait(self, src):
+        u = self.u
+        for k in (0, 1):
+            mine = both(self.alone, u.mu == k)
+            place = self.place(2 * u.c + k)
+            pl.when(mine)(lambda: pltpu.make_async_copy(src.at[0], place, self.local).wait())
+            pl.when(jnp.logical_not(mine))(
+                lambda: remote(place, place, self.sems.at[0, 0], self.sems.at[1, k], u.column_keeper(k)).wait_recv()
+            )
+
+    def sent(self, src):
+        u = self.u
+        for m in (0, 1):
+            pl.when(jnp.logical_not(both(self.alone, u.mu == m)))(lambda: self.cp(src, m).wait_send())
+
+
+class Swap:
+    def __init__(self, u, buf, sems):
+        self.u, self.buf, self.sems = u, buf, sems
+
+    def cps(self):
+        u = self.u
+        out = []
+        for k in (1, 2, 3):
+            out.append((self.buf.at[u.q], self.sems.at[0, k], self.sems.at[1, u.q], u.peer((u.q + k) % 4)))
+        return out
+
+    def send(self):
+        for ref, s, r, dev in self.cps():
+            remote(ref, ref, s, r, dev).start()
+
+    def wait(self):
+        u = self.u
+        for k in (1, 2, 3):
+            p = (u.q + k) % 4
+            remote(self.buf.at[p], self.buf.at[p], self.sems.at[0, k], self.sems.at[1, p], u.peer(p)).wait_recv()
+
+    def sent(self):
+        for ref, s, r, dev in self.cps():
+            remote(ref, ref, s, r, dev).wait_send()
+
+    def total(self):
+        return self.buf[0] + self.buf[1] + self.buf[2] + self.buf[3]
+
+
+class Spread:
+    def __init__(self, u, buf, sems, parts):
+        self.u, self.buf, self.sems, self.parts = u, buf, sems, parts
+
+    def cp(self, kind, p, part):
+        u = self.u
+        ref = self.buf.at[p, part]
+        device = u.xn if kind == 1 else u.cn
+        return remote(ref, ref, self.sems.at[0, kind, part], self.sems.at[1, kind, part], device)
+
+    def send(self, part):
+        self.cp(1, self.u.q, part).start()
+        self.cp(0, self.u.q, part).start()
+
+    def across(self):
+        q = self.u.q
+        return q + 1 - 2 * (q % 2)
+
+    def relay(self, part):
+        copy = self.cp(1, self.across(), part)
+        copy.wait_recv()
+        self.cp(2, self.across(), part).start()
+
+    def near(self, part):
+        self.cp(0, 3 - self.u.q, part).wait_recv()
+
+    def far(self, part):
+        self.cp(2, 3 - self.across(), part).wait_recv()
+
+    def sent(self, part):
+        self.cp(1, self.u.q, part).wait_send()
+        self.cp(0, self.u.q, part).wait_send()
+        self.cp(2, self.across(), part).wait_send()
+
+
+class Halo:
+    def __init__(self, u, buf, sems):
+        self.u, self.buf, self.sems = u, buf, sems
+
+    def cp(self, downward):
+        u, buf = self.u, self.buf
+        if downward:
+            return remote(buf.at[1], buf.at[ROW + 1], self.sems.at[0, 0], self.sems.at[1, 0], u.peer(jnp.maximum(u.q - 1, 0)))
+        return remote(buf.at[ROW], buf.at[0], self.sems.at[0, 1], self.sems.at[1, 1], u.peer(jnp.minimum(u.q + 1, 3)))
+
+    def send(self):
+        u, buf = self.u, self.buf
+        pl.when(u.q > 0)(lambda: self.cp(True).start())
+        pl.when(u.q < 3)(lambda: self.cp(False).start())
+
+        @pl.when(u.q == 0)
+        def _():
+            buf[0] = jnp.zeros(buf.shape[1:], buf.dtype)
+
+        @pl.when(u.q == 3)
+        def _():
+            buf[ROW + 1] = jnp.zeros(buf.shape[1:], buf.dtype)
+
+    def wait(self):
+        u = self.u
+        pl.when(u.q > 0)(lambda: self.cp(False).wait_recv())
+        pl.when(u.q < 3)(lambda: self.cp(True).wait_recv())
+
+    def sent(self):
+        u = self.u
+        pl.when(u.q > 0)(lambda: self.cp(True).wait_send())
+        pl.when(u.q < 3)(lambda: self.cp(False).wait_send())
+
+
+def canvas_of(rows, limits):
+    return (rows >= limits[0:1]).astype(F32) + (rows >= limits[1:2]).astype(F32)
+
+
+def row_numbers(u, offset, shape):
+    return (ROW * u.q + offset + lax.broadcasted_iota(jnp.int32, shape, 0)).astype(F32)
+
+
+def counts_of(limits, total_rows):
+    each = 64.0 * 16.0
+    return (limits[0:1] * each, (limits[1:2] - limits[0:1]) * each, (total_rows - limits[1:2]) * each)
+
+
+def group_total(sums):
+    width = sums.shape[1]
+    lane = lax.broadcasted_iota(jnp.int32, sums.shape, 1)
+    for step in (1, 2, 4, 8):
+        after = pltpu.roll(sums, width - step, 1)
+        before = pltpu.roll(sums, step, 1)
+        sums = sums + jnp.where((lane // step) % 2 == 0, after, before)
+    return sums
+
+
+def canvas_sums(first, second, seg):
+    out = []
+    for rows in (first, second):
+        for k in range(CANVASES):
+            out.append(jnp.sum(jnp.where(seg == float(k), rows, 0.0), axis=0, keepdims=True))
+    out.append(jnp.zeros((2, first.shape[1]), F32))
+    return jnp.concatenate(out, axis=0)
+
+
+def by_row(values, seg):
+    return jnp.where(seg == 0.0, values[0], jnp.where(seg == 1.0, values[1], values[2]))
+
+
+def moments(total, counts, seg):
+    grouped = group_total(total)
+    averages, inverses = [], []
+    for k in range(CANVASES):
+        average = grouped[k : k + 1] / counts[k]
+        averages.append(average)
+        inverses.append(lax.rsqrt(grouped[3 + k : 4 + k] / counts[k] - average * average + EPSILON))
+    return by_row(averages, seg), by_row(inverses, seg)
+
+
+def sigmoid(argument):
+    return 0.5 * jnp.tanh(0.5 * argument) + 0.5
+
+
+def each_row(body):
+    lax.fori_loop(0, ROW, lambda r, carry: (body(r), carry)[1], 0)
+
+
+def row_of(ref, r):
+    return ref[pl.ds(r, 1), :]
+
+
+def tap_masks(u, limits, masks):
+    shape = (ROW, limits.shape[1])
+    rows = row_numbers(u, 0, shape)
+    seg = canvas_of(rows, limits)
+    masks[0] = both(canvas_of(rows - 1.0, limits) == seg, rows >= 1.0).astype(F32)
+    masks[1] = both(canvas_of(rows + 1.0, limits) == seg, rows < 4.0 * ROW - 1.0).astype(F32)
+    return seg
+
+
+def shifted(line):
+    position = lax.broadcasted_iota(jnp.int32, line.shape, 0)
+    width = line.shape[0]
+    before = jnp.where(position == 0, 0.0, pltpu.roll(line, 1, 0))
+    after = jnp.where(position == width - 1, 0.0, pltpu.roll(line, width - 1, 0))
+    return before, line, after
+
+
+def taps_inner(buf, masks, taps):
+    def body(s):
+        lines = shifted(buf[s + 1].astype(F32))
+        for k in range(3):
+            taps[3 + k, s] = lines[k].astype(BF)
+
+        @pl.when(s < ROW - 1)
+        def _():
+            mask = masks[0, pl.ds(s + 1, 1), :]
+            for k in range(3):
+                taps[k, s + 1] = (lines[k] * mask).astype(BF)
+
+        @pl.when(s > 0)
+        def _():
+            mask = masks[1, pl.ds(s - 1, 1), :]
+            for k in range(3):
+                taps[6 + k, s - 1] = (lines[k] * mask).astype(BF)
+
+    each_row(body)
+
+
+def taps_outer(buf, masks, taps):
+    for k, line in enumerate(shifted(buf[0].astype(F32))):
+        taps[k, 0] = (line * masks[0, 0:1, :]).astype(BF)
+    for k, line in enumerate(shifted(buf[ROW + 1].astype(F32))):
+        taps[6 + k, ROW - 1] = (line * masks[1, ROW - 1 : ROW, :]).astype(BF)
+
+
+def conv_tile(taps, weight, m, flip):
+    total = None
+    for tap in range(9):
+        left = taps[8 - tap if flip else tap, pl.ds(pl.multiple_of(m * 4, 4), 4)].reshape(256, -1)
+        right = weight[tap * 512 : (tap + 1) * 512, :]
+        term = cols(left, right) if flip else mm(left, right)
+        total = term if total is None else total + term
+    return total.reshape(4, 64, -1)
+
+
+def conv_weight_grad(act_t, taps, out, first, last):
+    def body(tap, carry):
+        piece = mm(act_t[...], taps[8 - tap].reshape(512, -1))
+        out[pl.ds(pl.multiple_of(tap * 512, 512), 512), :] = piece.astype(BF)
+        return carry
+
+    lax.fori_loop(first, last, body, 0)
+
+
+def attn_places(ref, split=0):
+    def at(z, x, d, half=None):
+        place = ref.at[z * 2 + x]
+        lanes = pl.ds(pl.multiple_of(d * 128, 128), 128)
+        if half is None:
+            return place.at[:, lanes]
+        return place.at[pl.ds(half * split, 256 - split if half else split), lanes]
+
+    return at
+
+
+def param_places(ref):
+    def at(z, x, d, half=None):
+        place = ref.at[z * 2 + x]
+        lanes = pl.ds(pl.multiple_of(d * 128, 128), 128)
+        if half is None:
+            return place.at[:, lanes]
+        return place.at[pl.ds(half * 8, 8), lanes]
+
+    return at
+
+
+class Halves:
+    def __init__(self, ref):
+        self.ref = ref
+
+    @property
+    def at(self):
+        return self
+
+    def __getitem__(self, index):
+        member, part = index
+        return self.ref.at[member, pl.ds(part * (ROW // 2), ROW // 2)]
+
+
+ANY = pl.BlockSpec(memory_space=pl.ANY)
+VM = pl.BlockSpec(memory_space=pltpu.VMEM)
+
+
+class Blocks:
+    def __init__(self, ref):
+        self.ref = ref
+
+    @property
+    def at(self):
+        return self
+
+    def __getitem__(self, index):
+        member, part = index
+        x = jnp.where(member < 2, member, 3 - member)
+        return self.ref.at[2 * (member // 2) + part, pl.ds(4 * x, 4)]
+
+
+def unit_inputs(features, bounds, out_grad, norms, conv1, conv2, attn):
+    d, b = lax.axis_index("dp"), lax.axis_index("blk")
+    limits = jnp.broadcast_to(bounds.reshape(-1).astype(F32)[:, None], (4, 512))
+    limits = jnp.concatenate([limits, jnp.zeros((4, 512), F32)])
+    rows = jnp.stack([item.astype(F32) for item in norms])
+    mine = jnp.where(d == b // 2, rows, 0.0)
+    params = jnp.concatenate([jnp.where(b % 2 == 0, mine, 0.0), jnp.where(b % 2 == 1, mine, 0.0)], axis=1)
+    params = jnp.concatenate([params, jnp.zeros((PARAMS - 6, 128), F32)])
+    return (features[0], out_grad[0], limits, params, conv1, conv2, jnp.concatenate(attn))
+
+
+def whole_kernel(
+    feat, grad, bounds, par, s1, s2, sa,
+    act_back, grad_back, g1_out, g2_out, ga_out, norm_out,
+    w1, w2, wa, pb, bb, xin, oall, nall, taps, a1, a2, masks, hidden, resid, small, rows_a, rows_b, swaps, lds,
+    wg1, wg2, scores, gk, gv, lcol, dcol, big, gres, low, act, act_t1, act_t2, ga, mine, psum_y, psum_z,
+    core_a, core_2, half_a, rest_a, side_a, last_a, half_2, rest_2, side_2, last_2, half_1, rest_1, side_1, last_1,
+    gsems, ssems, local, share_sems, bound_sems, swap_sems, spread_sems, halo_sems, py_sems, pz_sems,
+):
+    u = Unit()
+    u.enter(True, True)
+    mine[...] = jnp.zeros_like(mine)
+    table = {}
+    ats = (weight_places(w1, 576, SPLIT), weight_places(w2, 576, SPLIT), attn_places(wa, SPLIT_A), param_places(pb))
+    groups = [Gather(u, 4, at, gsems.at[k], DIRECT[k]) for k, at in enumerate(ats)]
+    for name, group in zip(("g1", "g2", "ga", "gp"), groups):
+        table.update(group.table(name))
+    sources = (s1, s2, sa, par)
+    own = [pltpu.make_async_copy(src, group.own(u.z), local.at[k]) for k, (src, group) in enumerate(zip(sources, groups))]
+    for copy in own:
+        copy.start()
+    keep = pltpu.make_async_copy(bounds, bb.at[u.c], local.at[4])
+    keep.start()
+    share_x, share_a, share_g = [Share(u, share_sems.at[k], local.at[5 + k]) for k in range(3)]
+    share_o = ColumnShare(u, oall, share_sems.at[3], local.at[8])
+    swap = [Swap(u, swaps.at[k], swap_sems.at[k]) for k in range(6)] + [Swap(u, lds, swap_sems.at[6])]
+    halo = [Halo(u, (a1, a2)[k % 2], halo_sems.at[k]) for k in range(4)]
+    spread_o = Spread(u, Blocks(oall), spread_sems.at[0], 2)
+    spread_n = Spread(u, Halves(nall), spread_sems.at[1], 2)
+
+    w2_at = weight_places(w2, 576)
+    part_a = lambda ref, h: part_of(ref, h, CUT_A, 256)
+    part_w = lambda ref, h: part_of(ref, h, CUT, 576)
+    sum_a = Scatter(
+        u, 4, attn_places(ga), lambda k, z, x, d: core_a.at[k, z], part_a, ssems.at[0], ((half_a, rest_a), side_a, last_a)
+    )
+    sum_2 = Scatter(
+        u, 4, weight_places(wg2, 576), lambda k, z, x, d: core_2.at[k, z], part_w, ssems.at[1], ((half_2, rest_2), side_2, last_2)
+    )
+    sum_1 = Scatter(
+        u, 4, weight_places(wg1, 576), lambda k, z, x, d: w2_at(z, x, d), part_w, ssems.at[2], ((half_1, rest_1), side_1, last_1)
+    )
+    for name, total, out in (("ra", sum_a, ga_out), ("r2", sum_2, g2_out), ("r1", sum_1, g1_out)):
+        table.update(total.table(name, out))
+    bound_cp = remote(bounds, bb.at[u.c], bound_sems.at[0], bound_sems.at[1], u.cn)
+    state = {}
+
+    def step(function):
+        table[function.__name__] = function
+        return function
+
+
+    @step
+    def xs():
+        share_x.send(feat, xin)
+        bound_cp.start()
+
+    @step
+    def os():
+        share_o.send(grad)
+
+    @step
+    def ow():
+        for copy in own:
+            copy.wait()
+
+    @step
+    def bw():
+        keep.wait()
+        remote(bounds, bb.at[1 - u.c], bound_sems.at[0], bound_sems.at[1], u.cn).wait_recv()
+        limits = jnp.where(u.mu == 0, bb[u.z // 2, 0:2, :], bb[u.z // 2, 2:4, :])
+        small[7] = jnp.concatenate([limits, jnp.zeros((6, limits.shape[1]), F32)], axis=0)
+        state["seg"] = tap_masks(u, limits, masks)
+        state["counts"] = counts_of(limits, 4.0 * ROW)
+
+    def first(r):
+        return xin[r].astype(F32)
+
+    def second(r):
+        return hidden[r]
+
+    def third(r):
+        return resid[r]
+
+    values = (first, second, third)
+
+    def norm_sums(k):
+        def body(r):
+            line = values[k](r)
+            rows_a[pl.ds(r, 1), :] = jnp.sum(line, axis=0, keepdims=True)
+            rows_b[pl.ds(r, 1), :] = jnp.sum(line * line, axis=0, keepdims=True)
+
+        each_row(body)
+        swap[k].buf[u.q] = canvas_sums(rows_a[...], rows_b[...], state["seg"])
+        swap[k].send()
+
+    def norm_stats(k):
+        swap[k].wait()
+        average, inverse = moments(swap[k].total(), state["counts"], state["seg"])
+        small[2 * k] = average
+        small[2 * k + 1] = inverse
+
+    def param(j):
+        return small[6, j : j + 1, :]
+
+    def xhat(k, r):
+        return (values[k](r) - small[2 * k, pl.ds(r, 1), :]) * small[2 * k + 1, pl.ds(r, 1), :]
+
+    def normal(k, r):
+        return xhat(k, r) * param(2 * k) + param(2 * k + 1)
+
+    def activate(k, buf):
+        def body(r):
+            line = normal(k, r)
+            buf[r + 1] = (line * sigmoid(line)).astype(BF)
+
+        each_row(body)
+
+    @step
+    def n1a():
+        share_x.wait(feat, xin)
+        norm_sums(0)
+
+    @step
+    def n1b():
+        groups[3].arrive()
+        total = pb[0, 0:8, :]
+        for b in range(1, 8):
+            total = total + pb[b, 0:8, :]
+        small[6] = total
+        norm_stats(0)
+
+    def conv_steps(name, k, buf):
+        def c():
+            activate(k, buf)
+            halo[k].send()
+
+        def d():
+            taps_inner(buf, masks, taps)
+
+        def e():
+            halo[k].wait()
+            taps_outer(buf, masks, taps)
+            halo[k].sent()
+
+        table[name + "c"], table[name + "d"], table[name + "e"] = c, d, e
+
+    conv_steps("n1", 0, a1)
+    conv_steps("n2", 1, a2)
+
+    @step
+    def t1():
+        act_t1[...] = a1[1 : ROW + 1].reshape(512, 512).T
+
+    @step
+    def t2():
+        act_t2[...] = a2[1 : ROW + 1].reshape(512, 512).T
+
+    def first_conv(m):
+        hidden[4 * m : 4 * m + 4] = conv_tile(taps, w1, m, False)
+
+    def second_conv(m):
+        resid[4 * m : 4 * m + 4] = conv_tile(taps, w2, m, False) + xin[4 * m : 4 * m + 4].astype(F32)
+
+    for m in (0, 1):
+        table["c1%d" % m] = functools.partial(first_conv, m)
+        table["c2%d" % m] = functools.partial(second_conv, m)
+    table["n2a"], table["n2b"] = functools.partial(norm_sums, 1), functools.partial(norm_stats, 1)
+    table["n3a"], table["n3b"] = functools.partial(norm_sums, 2), functools.partial(norm_stats, 2)
+
+    @step
+    def n3c():
+        def row(r):
+            nall[u.q, r] = normal(2, r).astype(BF)
+
+        for part in range(2):
+            lax.fori_loop(4 * part, 4 * part + 4, lambda r, carry: (row(r), carry)[1], 0)
+            spread_n.send(part)
+
+    @step
+    def ob():
+        share_o.wait(grad)
+        for part in range(2):
+            spread_o.send(part)
+
+    for part in (0, 1):
+        table["or%d" % part] = functools.partial(spread_o.relay, part)
+        table["nr%d" % part] = functools.partial(spread_n.relay, part)
+
+    scale = 512.0 ** (-0.5)
+
+    def slot(ref, i):
+        return ref.at[pl.ds(pl.multiple_of(i * 512, 512), 512)]
+
+    def query_of(i):
+        return slot(wg1, i)
+
+    def key_of(i):
+        return slot(wg1, 4 + i)
+
+    def value_of(i):
+        return slot(wg2, i)
+
+    def upstream_of(i):
+        return slot(wg2, 4 + i)
+
+    heads, gq = slot(wg1, 8), slot(wg2, 8)
+
+    def matrix(k):
+        return wa[:, pl.ds(k * 64, 64), :].reshape(512, 512)
+
+    across = u.q + 1 - 2 * (u.q % 2)
+    members = (u.q, 3 - u.q, across, 3 - across)
+
+    def project(k):
+        if k in (1, 3):
+            for part in range(2):
+                (spread_n.near if k == 1 else spread_n.far)(part)
+        tokens = nall[members[k]].reshape(512, 512)
+        query_of(members[k])[...] = mm(tokens, matrix(0)).astype(BF)
+        key_of(members[k])[...] = mm(tokens, matrix(1)).astype(BF)
+        value_of(members[k])[...] = mm(tokens, matrix(2)).astype(BF)
+
+    def project_up(k):
+        if k == 1:
+            for part in range(2):
+                spread_o.near(part)
+                spread_o.far(part)
+        upstream = oall[members[k]].reshape(512, 512)
+        upstream_of(members[k])[...] = cols(upstream, matrix(3)).astype(BF)
+
+    for k in range(4):
+        table["pj%d" % k] = functools.partial(project, k)
+        table["po%d" % k] = functools.partial(project_up, k)
+
+    def canvas(rows):
+        return (rows >= small[7, 0:1, 0:1]).astype(F32) + (rows >= small[7, 1:2, 0:1]).astype(F32)
+
+    def seg_col(q, offset, count):
+        token = offset + lax.broadcasted_iota(jnp.int32, (count, 1), 0)
+        return canvas((ROW * q + token // 64).astype(F32))
+
+    def seg_row(q):
+        token = lax.broadcasted_iota(jnp.int32, (1, 512), 1)
+        return canvas((ROW * q + token // 64).astype(F32))
+
+    def kept(j, i):
+        return taps.at[i, pl.ds(pl.multiple_of(j * 4, 4), 4)]
+
+    def queries(j, carry):
+        block = pl.ds(pl.multiple_of(j * 256, 256), 256)
+        query = query_of(u.q)[block]
+        seg = seg_col(u.q, j * 256, 256)
+        most = jnp.full((256, 1), NEGATIVE, F32)
+        for i in range(4):
+            part = jnp.where(seg == seg_row(i), cols(query, key_of(i)[...]) * scale, NEGATIVE)
+            scores[i] = part
+            most = jnp.maximum(most, jnp.max(part, axis=1, keepdims=True))
+        total = jnp.zeros((256, 1), F32)
+        for i in range(4):
+            part = jnp.exp(scores[i] - most)
+            total = total + jnp.sum(part, axis=1, keepdims=True)
+            scores[i] = part
+        inverse = 1.0 / total
+        found = jnp.zeros((256, 512), F32)
+        for i in range(4):
+            part = (scores[i] * inverse).astype(BF)
+            kept(j, i)[...] = part.reshape(4, 64, 512)
+            found = found + mm(part, value_of(i)[...])
+        heads[block, :] = found.astype(BF)
+        lcol[block, :] = jnp.broadcast_to(most + jnp.log(total), (256, 128))
+        return carry
+
+    @step
+    def qf():
+        lax.fori_loop(0, 2, queries, 0)
+
+    def queries_back(j, carry):
+        block = pl.ds(pl.multiple_of(j * 256, 256), 256)
+        upstream = upstream_of(u.q)[block]
+        correction = jnp.zeros((256, 1), F32)
+        for i in range(4):
+            slope = cols(upstream, value_of(i)[...])
+            scores[i] = slope
+            part = kept(j, i)[...].reshape(256, 512).astype(F32)
+            correction = correction + jnp.sum(part * slope, axis=1, keepdims=True)
+        back = jnp.zeros((256, 512), F32)
+        for i in range(4):
+            part = kept(j, i)[...].reshape(256, 512).astype(F32)
+            back = back + mm((part * (scores[i] - correction)).astype(BF), key_of(i)[...])
+        gq[block, :] = (back * scale).astype(BF)
+        dcol[block, :] = jnp.broadcast_to(correction, (256, 128))
+        return carry
+
+    @step
+    def qb():
+        lax.fori_loop(0, 2, queries_back, 0)
+        lds[u.q] = jnp.concatenate([lcol[...].T[0:1], dcol[...].T[0:1], jnp.zeros((6, 512), F32)], axis=0)
+        swap[6].send()
+
+    @step
+    def gz():
+        for group in groups:
+            group.finish()
+
+    @step
+    def hd():
+        act[...] = (resid[...] + mm(heads[...], matrix(3)).reshape(ROW, 64, 512)).astype(BF)
+        share_a.back(act, act_back)
+
+    @step
+    def hw():
+        ga[:, 192:256, :] = mm(heads[...].T, oall[u.q].reshape(512, 512)).astype(BF).reshape(8, 64, 512)
+
+    def keys(index, carry):
+        i, j = index // 2, index % 2
+        block = pl.ds(pl.multiple_of(j * 256, 256), 256)
+        key, value = key_of(u.q)[block], value_of(u.q)[block]
+        query, upstream = query_of(i)[...], upstream_of(i)[...]
+        shared = seg_col(u.q, j * 256, 256) == seg_row(i)
+        part = jnp.where(shared, cols(key, query) * scale, NEGATIVE)
+        part = jnp.where(shared, jnp.exp(part - lds[i, 0:1, :]), 0.0)
+        rows = pl.ds(pl.multiple_of(j * 4, 4), 4)
+        gres[rows] += mm(part.astype(BF), upstream).reshape(4, 64, 512)
+        slope = cols(value, upstream) - lds[i, 1:2, :]
+        big[rows] += mm((part * slope).astype(BF), query).reshape(4, 64, 512)
+        return carry
+
+    @step
+    def ks():
+        big[...] = jnp.zeros_like(big)
+        gres[...] = jnp.zeros_like(gres)
+        swap[6].wait()
+        lax.fori_loop(0, 8, keys, 0)
+        gk[...] = (big[...] * scale).astype(BF).reshape(512, 512)
+        gv[...] = gres[...].astype(BF).reshape(512, 512)
+
+    @step
+    def aw():
+        tokens = nall[u.q].reshape(512, 512).T
+        for k, part in enumerate((gq, gk, gv)):
+            ga[:, k * 64 : (k + 1) * 64, :] = mm(tokens, part[...]).astype(BF).reshape(8, 64, 512)
+
+    @step
+    def an():
+        total = None
+        for k, part in enumerate((gq, gk, gv)):
+            term = cols(part[...], matrix(k))
+            total = term if total is None else total + term
+        big[...] = total.reshape(ROW, 64, 512)
+
+
+    def back_sums(k, slope):
+        def body(r):
+            line = big[r]
+            if slope:
+                value = normal(k, r)
+                part = sigmoid(value)
+                line = line * (part * (1.0 + value * (1.0 - part)))
+                big[r] = line
+            rows_a[pl.ds(r, 1), :] = jnp.sum(line, axis=0, keepdims=True)
+            rows_b[pl.ds(r, 1), :] = jnp.sum(line * xhat(k, r), axis=0, keepdims=True)
+
+        each_row(body)
+        swap[3 + k].buf[u.q] = canvas_sums(rows_a[...], rows_b[...], state["seg"])
+        swap[3 + k].send()
+
+    def back_means(k):
+        swap[3 + k].wait()
+        total = swap[3 + k].total()
+        mine[2 * k : 2 * k + 1, :] = jnp.sum(total[3:6], axis=0, keepdims=True)
+        mine[2 * k + 1 : 2 * k + 2, :] = jnp.sum(total[0:3], axis=0, keepdims=True)
+        grouped = group_total(total * param(2 * k))
+        counts, seg = state["counts"], state["seg"]
+        rows_a[...] = by_row([grouped[j : j + 1] / counts[j] for j in range(3)], seg)
+        rows_b[...] = by_row([grouped[3 + j : 4 + j] / counts[j] for j in range(3)], seg)
+
+    def back(k, r):
+        line = big[r] * param(2 * k) - row_of(rows_a, r) - xhat(k, r) * row_of(rows_b, r)
+        return line * small[2 * k + 1, pl.ds(r, 1), :]
+
+    @step
+    def b3a():
+        back_sums(2, False)
+
+    @step
+    def b3b():
+        back_means(2)
+
+        def row(r):
+            line = oall[u.q, r].astype(F32) + back(2, r)
+            gres[r] = line
+            a2[r + 1] = line.astype(BF)
+
+        each_row(row)
+        halo[3].send()
+
+    @step
+    def b2a():
+        back_sums(1, True)
+
+    @step
+    def b2b():
+        back_means(1)
+
+        def row(r):
+            a1[r + 1] = back(1, r).astype(BF)
+
+        each_row(row)
+        halo[2].send()
+
+    @step
+    def b1a():
+        back_sums(0, True)
+
+    @step
+    def b1m():
+        back_means(0)
+
+    @step
+    def b1b():
+        def row(r):
+            low[r] = (gres[r] + back(0, r)).astype(BF)
+
+        each_row(row)
+        share_g.back(low, grad_back)
+
+    @step
+    def ps():
+        remote(mine, psum_y, py_sems.at[0], py_sems.at[1], u.yn).start()
+
+    def back_taps(name, k, buf):
+        def c():
+            taps_inner(buf, masks, taps)
+
+        def d():
+            halo[k].wait()
+            taps_outer(buf, masks, taps)
+            halo[k].sent()
+
+        table[name + "c"], table[name + "d"] = c, d
+
+    back_taps("b3", 3, a2)
+    back_taps("b2", 2, a1)
+
+    def tile_back(weight, m):
+        big[4 * m : 4 * m + 4] = conv_tile(taps, weight, m, True)
+
+    for m in (0, 1):
+        table["d2%d" % m] = functools.partial(tile_back, w2, m)
+        table["d1%d" % m] = functools.partial(tile_back, w1, m)
+    for k in range(3):
+        table["w2%d" % k] = functools.partial(conv_weight_grad, act_t2, taps, wg2, 3 * k, 3 * k + 3)
+        table["w1%d" % k] = functools.partial(conv_weight_grad, act_t1, taps, wg1, 3 * k, 3 * k + 3)
+
+    def line_cp(k):
+        return remote(psum_z.at[u.z], psum_z.at[u.z], pz_sems.at[0, k], pz_sems.at[1, u.z], u.line(k))
+
+    @step
+    def py():
+        remote(mine, psum_y, py_sems.at[0], py_sems.at[1], u.yn).wait()
+        psum_z[u.z] = mine[...] + psum_y[...]
+        for k in (1, 2, 3):
+            line_cp(k).start()
+
+    @step
+    def pz():
+        for k in (1, 2, 3):
+            other = (u.z + k) % 4
+            remote(psum_z.at[other], psum_z.at[other], pz_sems.at[0, k], pz_sems.at[1, other], u.line(k)).wait_recv()
+        norm_out[...] = psum_z[0] + psum_z[1] + psum_z[2] + psum_z[3]
+
+    in_order(types.SimpleNamespace(**table))
+
+    share_a.back_wait(act, act_back)
+    share_g.back_wait(low, grad_back)
+    for total in (sum_a, sum_2, sum_1):
+        total.finish()
+    bound_cp.wait_send()
+    share_x.sent(feat, xin)
+    share_o.sent(grad)
+    for item in swap:
+        item.sent()
+    for item in (spread_o, spread_n):
+        for part in range(2):
+            item.sent(part)
+    for k in (1, 2, 3):
+        line_cp(k).wait_send()
+
+
+def whole_call(features, out_grad, limits, params, s1, s2, sa):
+    full = lambda shape, kind: jax.ShapeDtypeStruct(shape, kind)
+    dma = pltpu.SemaphoreType.DMA
+    rows, padded, square, weight = (ROW, 64, 512), (ROW + 2, 64, 512), (512, 512), (4608, 512)
+    low = lambda *shape: pltpu.VMEM(shape, BF)
+    wide = lambda *shape: pltpu.VMEM(shape, F32)
+    sums = []
+    for r, cut in ((256, CUT_A), (576, CUT), (576, CUT)):
+        sums += [low(4, cut, 128), low(4, r - cut, 128), low(2, 4, r, 128), low(4, r, 128)]
+    return pl.pallas_call(
+        whole_kernel,
+        out_shape=[
+            full((2, 4, 64, 512), BF), full((2, 4, 64, 512), BF), full((576, 128), F32), full((576, 128), F32),
+            full((256, 128), F32), full((8, 512), F32),
+        ],
+        in_specs=[ANY] * 7,
+        out_specs=[VM] * 6,
+        scratch_shapes=[
+            low(*weight), low(*weight), low(8, 256, 512), wide(8, PARAMS, 512), wide(2, 8, 512), low(*rows),
+            low(4, *rows), low(4, *rows), low(9, *rows), low(*padded), low(*padded), wide(2, ROW, 512),
+            wide(*rows), wide(*rows), wide(8, 8, 512), wide(ROW, 512), wide(ROW, 512), wide(6, 4, 8, 512), wide(4, 8, 512),
+            low(*weight), low(*weight), wide(4, 256, 512), low(*square), low(*square),
+            wide(512, 128), wide(512, 128), wide(*rows), wide(*rows), low(*rows), low(*rows), low(*square), low(*square),
+            low(8, 256, 512), wide(8, 512), wide(8, 512), wide(4, 8, 512),
+            low(4, 4, 256, 128), low(4, 4, 576, 128), *sums,
+            dma((4, 2, Gather.SEMS)), dma((3, 2, Scatter.SEMS)), dma((9,)), dma((4, 2, 2)), dma((2,)), dma((7, 2, 4)),
+            dma((2, 2, 3, 2)), dma((4, 2, 2)), dma((2,)), dma((2, 4)),
+        ],
+        compiler_params=pltpu.CompilerParams(collective_id=0, has_side_effects=True, vmem_limit_bytes=LIMIT),
+    )(features, out_grad, limits, params, s1, s2, sa)
+
+
+def unit_shards(
+    features, bounds, out_grad, norm1_gain, norm1_shift, conv1_weight, norm2_gain, norm2_shift, conv2_weight,
+    norm3_gain, norm3_shift, query_weight, key_weight, value_weight, output_weight,
+):
+    norms = (norm1_gain, norm1_shift, norm2_gain, norm2_shift, norm3_gain, norm3_shift)
+    attn = (query_weight, key_weight, value_weight, output_weight)
+    act_back, grad_back, g1, g2, ga, norms = whole_call(
+        *unit_inputs(features, bounds, out_grad, norms, conv1_weight, conv2_weight, attn)
+    )
+    norms = lax.dynamic_slice_in_dim(norms, lax.axis_index("blk") * 64, 64, axis=1)
+    ga = ga.reshape(4, 64, 128)
+    return (
+        act_back.astype(F32)[None], grad_back.astype(F32)[None], norms[0], norms[1], g1, norms[2], norms[3], g2,
+        norms[4], norms[5], ga[0], ga[1], ga[2], ga[3],
+    )
 
 
 def extended(shard, sides, width):
@@ -585,4 +1948,5 @@
         P("blk", "dp"),
         P("blk", "dp"),
     )
-    return jax.shard_map(shards, mesh=mesh, in_specs=in_specs, out_specs=out_specs, check_vma=False)
+    near = mesh.shape["dp"] == 4 and mesh.shape["blk"] == 8
+    return jax.shard_map(unit_shards if near else shards, mesh=mesh, in_specs=in_specs, out_specs=out_specs, check_vma=False)

time: 1420 us -> 201 us (0.14)
  waiting for transfers between devices: 624 us -> 0 us
  blocking collectives: 388 us -> 0 us
  Pallas kernels: 0 us -> 190 us
  matrix products: 141 us -> 0 us
  local copies, waits for them, and re-layouts: 111 us -> 6.05 us
  other arithmetic: 68 us -> 4.16 us
  starting transfers between devices: 50 us -> 0 us
  between operations: 23.1 us -> 0.82 us
    reduce_scatter x12 -> x0, waiting for transfers between devices: 490 us -> none  [the longest x1 164 us: reduce_all(): lax.psum_scatter(gradients[1], 'blk', scatter_dimension=0, tiled=True)]
    all_gather x12 -> x0, blocking collectives: 226 us -> none  [the longest x2 38.3 us: attention_key_grad(): lax.all_gather(correction, 'blk', axis=0, tiled=True)]
    pallas_call x0 -> x1, Pallas kernels: none -> 190 us  [whole_call(): pl.pallas_call(whole_kernel, out_shape=[full((2, 4, 64, 512), BF), full((...]
    dot_general x96 -> x0, matrix products: 141 us -> none  [the longest x4 15.3 us: conv_apply(): result = jnp.dot(stacked, weight_matrix, preferred_element_type=jnp.float32)]
    psum x7 -> x0, blocking collectives: 138 us -> none  [the longest x3 73.9 us: norm_backward(): lax.psum((group_sums(member, scaled), group_sums(member, scaled * grouped...]
    all_gather x12 -> x0, waiting for transfers between devices: 133 us -> none  [the longest x2 89.3 us: attention_key_grad(): lax.all_gather(heads_grad.astype(jnp.float32), 'blk', axis=0, tiled=True)]
    ppermute x16 -> x0, starting transfers between devices: 47.9 us -> none  [the longest x8 37.4 us: extended(): before = lax.ppermute(last, axis, up)]
    unnamed x373 -> x28, local copies, waits for them, and re-layouts: 35.5 us -> 2.5 us
  transfers between devices with their start and end apart: 40 -> 0, of which waited for: 12 -> 0; matrix products, arithmetic and copies ran while one was open for 21% -> 0% of each run, Pallas kernels for 0% -> 0%
where the time goes in v3:
time: 201 us
  Pallas kernels  190 us (95%)
  local copies, waits for them, and re-layouts  6.05 us (3%)
  other arithmetic  4.16 us (2%)
    pallas_call x1, Pallas kernels, whole_call(): pl.pallas_call(whole_kernel, out_shape=[full((2, 4, 64, 512), BF), full((...  190 us

profile of v3, /device:TPU:0, one launch (start us, length us, event | category | flops | bytes accessed | tf_op | source)
XLA Modules:
  0.0 200.5 jit_solution(9293779769081945668)
XLA Ops:
  0.7 0.0 copy-start.9
  0.7 0.0 copy-start.10
  0.7 0.0 copy-start.11
  0.7 0.0 copy-start.12
  0.7 0.0 copy-start.6
  0.7 0.0 copy-start.7
  0.7 0.0 copy-start.8
  0.7 0.0 copy-start.5
  0.8 0.7 copy-done.6
  1.4 0.1 convert_element_type.19
  1.6 0.0 copy-start.4
  1.6 0.0 copy-start.2
  1.6 0.0 copy-start.3
  1.6 0.7 select_maximum_fusion.par
  2.3 0.7 concatenate.15.bounds
  3.0 0.6 pad_maximum_fusion.sa
  3.6 189.5 %shard_map.254 = (bf16[2,4,64,512]{3,2,1,0:T(8,128)(2,1)}, bf16[2,4,64,512]{3,2,1,0:T(8,128)(2,1)}, f32[576,128]{1,0:T(8,128)}, f32[576,128]{1,0:T(8,128)}, f32[256,128]{1,0:T(8,128)}, /*index=5*/f32[8,512]{1,0:T(8,128)}) custom-call(bf16[2,4,64,512]{3,2,1,0:T(8,128)(2,1)} %bitcast.26, bf16[2,4,64,512]{3,2,1,0:T(8,128)(2,1)} %bitcast.27, ...), custom_call_target="tpu_custom_call" | custom-call | tf_op jit(solution)/shard_map/pallas_call | solution.py:1338
  193.2 0.8 constant_dynamic-slice_fusion
  193.9 0.5 slice_bitcast_fusion
  194.5 1.5 fusion.2
  195.9 2.8 %bitcast_convert_fusion = (f32[1,2,4,64,512]{4,3,2,1,0:T(8,128)}, f32[1,2,4,64,512]{4,3,2,1,0:T(8,128)}) fusion(bf16[2,4,64,512]{3,2,1,0:T(8,128)(2,1)} %get-tuple-element.21, bf16[2,4,64,512]{3,2,1,0:T(8,128)(2,1)} %get-tuple-element.20), kind=kLoop, calls=%fused_computation | loop fusion | flops 524288 | bytes 3145728 | tf_op jit(solution)/shard_map/broadcast_in_dim | solution.py:1373
  198.8 0.7 copy.31
  199.5 0.4 copy-done
  199.8 0.7 copy.32
  (17 shorter events, 0.1 us)
Async XLA Ops:
  0.7 0.8 copy-start.9
  0.7 0.8 copy-start.10
  0.7 0.8 copy-start.11
  0.7 0.8 copy-start.12
  0.7 0.7 copy-start.6
  0.7 0.8 copy-start.7
  0.7 0.8 copy-start.8
  0.7 2.2 %copy-start.5 = (bf16[64,128]{1,0:T(8,128)(2,1)S(1)}, bf16[64,128]{1,0:T(8,128)(2,1)}, u32[]{:S(2)}) copy-start(bf16[64,128]{1,0:T(8,128)(2,1)} %param.26) | copy-start | bytes 49156
  1.6 1.4 copy-start.4
  1.6 1.4 copy-start.2
  1.6 1.4 copy-start.3
  195.9 2.8 %copy-start.1 = (f32[576,128]{1,0:T(8,128)S(1)}, f32[576,128]{1,0:T(8,128)}, u32[]{:S(2)}) copy-start(f32[576,128]{1,0:T(8,128)} %get-tuple-element.58) | copy-start | bytes 884740
  198.8 1.1 copy-start

commit v4 on v3

--- a/solution.py
+++ b/solution.py
@@ -86,18 +86,21 @@
 
 
 class Gather:
-    SEMS = 40
-
-    def __init__(self, here, nz, at, sems, direct):
-        self.here, self.nz, self.at, self.sems, self.direct = here, nz, at, sems, direct
+    SEMS = 27
+
+    def __init__(self, here, nz, at, block, sems, direct):
+        self.here, self.nz, self.at, self.block, self.sems, self.direct = here, nz, at, block, sems, direct
         self.visits = steps_of(here.z, nz)
 
-    def sem(self, kind, z, way):
-        base = {"z": 0, "x": 4, "y": 8, "da": 12, "db": 16, "co": 20, "cx": 24, "cy": 28, "cd": 32, "zd": 36}[kind]
-        return self.sems.at[way, base + z]
-
-    def cp(self, kind, z, src, device, skind=None):
-        return remote(src, src, self.sem(skind or kind, z, 0), self.sem(kind, z, 1), device)
+    def ends(self, kind, z):
+        if kind[0] == "c":
+            return self.sems.at[26], self.sems.at[16]
+        send = {"z": 17 + z, "zd": 21 + z}.get(kind, 25)
+        recv = {"z": 0, "zd": 0, "x": 4, "y": 8, "da": 12, "db": 12}[kind] + z
+        return self.sems.at[send], self.sems.at[recv]
+
+    def cp(self, kind, z, src, device):
+        return remote(src, src, *self.ends(kind, z), device)
 
     def own(self, z):
         return self.at(z, self.here.x, self.here.d, None)
@@ -115,7 +118,7 @@
         here = self.here
         z = (here.z + k) % self.nz
         device = {"dp": here.d, "blk": z * 2 + here.x}
-        return remote(self.own(here.z), self.own(here.z), self.sem("z", z, 0), self.sem("z", here.z, 1), device)
+        return remote(self.own(here.z), self.own(here.z), self.sems.at[17 + z], self.sems.at[here.z], device)
 
     def line(self, j):
         z, valid = self.visits[j]
@@ -141,7 +144,7 @@
 
                 @pl.when(here.z > 0)
                 def _():
-                    self.cp("z", z, src, here.down, "zd").start()
+                    self.cp("zd", z, src, here.down).start()
 
         guarded(valid, body)
 
@@ -190,48 +193,30 @@
         here = self.here
 
         def body():
-            self.cp("da", z, self.cold(z, 0), here.yn).wait_recv()
-            self.cp("db", z, self.cold(z, 1), here.xn).wait_recv()
+            self.cp("da", z, self.cold(z), here.yn).wait_recv()
             self.cp("cd", z, self.cold(z), here.cn).start()
 
         guarded(valid, body)
 
     def arrive(self):
-        here = self.here
-        near, far = here.y * 2 + 1 - here.c, (1 - here.y) * 2 + 1 - here.c
-        for z in range(self.nz):
-            for kind, x, d in (("co", here.x, near), ("cx", 1 - here.x, near), ("cy", here.x, far), ("cd", 1 - here.x, far)):
-                self.cp(kind, z, self.at(z, x, d, None), here.cn).wait_recv()
+        self.cp("co", 0, self.block(4 * self.nz), self.here.cn).wait_recv()
 
     def finish(self):
         here = self.here
         if self.direct:
             for k in range(1, self.nz):
                 self.line_cp(k).wait_send()
-        for j, (z, valid) in enumerate(self.visits):
-
-            def body():
-                src = self.own(z)
-                if not self.direct and (j == 0 or j % 2 == 1):
-
-                    @pl.when(here.z < self.nz - 1)
-                    def _():
-                        self.cp("z", z, src, here.up).wait_send()
-
-                if not self.direct and (j == 0 or j % 2 == 0):
-
-                    @pl.when(here.z > 0)
-                    def _():
-                        self.cp("z", z, src, here.down, "zd").wait_send()
-
-                self.cp("x", z, src, here.xn).wait_send()
-                self.cp("y", z, src, here.yn).wait_send()
-                self.cp("da", z, self.colx(z, 0), here.yn).wait_send()
-                self.cp("db", z, self.coly(z, 1), here.xn).wait_send()
-                for kind in ("co", "cx", "cy", "cd"):
-                    self.cp(kind, z, src, here.cn).wait_send()
-
-            guarded(valid, body)
+        else:
+            for j, (z, valid) in enumerate(self.visits):
+                valid = True if valid is None else valid
+                if j == 0 or j % 2 == 1:
+                    going = jnp.logical_and(valid, here.z < self.nz - 1)
+                    pl.when(going)(lambda: self.cp("z", z, self.own(z), here.up).wait_send())
+                if j == 0 or j % 2 == 0:
+                    going = jnp.logical_and(valid, here.z > 0)
+                    pl.when(going)(lambda: self.cp("zd", z, self.own(z), here.down).wait_send())
+        self.cp("x", 0, self.block(3 * self.nz), here.xn).wait_send()
+        self.cp("co", 0, self.block(4 * self.nz), here.cn).wait_send()
 
     def table(self, name):
         kinds = {"l": self.line, "o": self.out, "x": self.from_x, "y": self.from_y, "d": self.diagonal}
@@ -244,19 +229,16 @@
 
 
 class Scatter:
-    SEMS = 48
-
-    def __init__(self, here, nz, at, core_at, part, sems, bufs):
-        self.here, self.nz, self.at, self.core_at, self.part, self.sems = here, nz, at, core_at, part, sems
+    SEMS = 20
+
+    def __init__(self, here, nz, at, core_at, part, block, sems, bufs):
+        self.here, self.nz, self.at, self.core_at, self.part = here, nz, at, core_at, part
+        self.block, self.sems = block, sems
         self.half, self.side, self.last = bufs
         self.visits = steps_of(here.z, nz)[::-1]
 
-    def sem(self, kind, z, way):
-        base = ("c0", "c1", "c2", "c3", "da", "db", "xa", "xb", "ya", "yb", "l").index(kind) * 4
-        return self.sems.at[way, base + z]
-
-    def cp(self, kind, z, src, dst, device):
-        return remote(src, dst, self.sem(kind, z, 0), self.sem(kind, z, 1), device)
+    def cp(self, send, recv, src, dst, device):
+        return remote(src, dst, self.sems.at[17 + send], self.sems.at[recv], device)
 
     def places(self, z, c):
         here = self.here
@@ -268,23 +250,21 @@
 
     def core_cp(self, z, k):
         place = self.places(z, 1 - self.here.c)[k]
-        return self.cp("c%d" % k, z, self.at(*place), self.core_at(k, *place), self.here.cn)
+        return self.cp(0, z, self.at(*place), self.core_at(k, *place), self.here.cn)
 
     def core_in(self, z, k):
-        place = self.core_at(k, *self.places(z, self.here.c)[k])
-        self.cp("c%d" % k, z, place, place, self.here.cn).wait_recv()
-        return place[...]
+        return self.core_at(k, *self.places(z, self.here.c)[k])[...]
 
     def begin(self, z):
         for k in (3, 1, 2, 0):
             self.core_cp(z, k).start()
 
     def half_cp(self, z, h):
-        return self.cp(("da", "db")[h], z, self.part(self.mine(z, 3), h), self.half[h].at[z], (self.here.xn, self.here.yn)[h])
+        return self.cp(1, 4 + 4 * h + z, self.part(self.mine(z, 3), h), self.half[h].at[z], (self.here.xn, self.here.yn)[h])
 
     def side_cp(self, z, side, h):
         return self.cp(
-            "xy"[side] + "ab"[h], z, self.part(self.mine(z, 1 + side), h), self.part(self.side.at[side, z], h),
+            1, 12 + z, self.part(self.mine(z, 1 + side), h), self.part(self.side.at[side, z], h),
             (self.here.xn, self.here.yn)[side],
         )
 
@@ -292,6 +272,7 @@
         z, valid = self.visits[j]
 
         def body():
+            self.cp(0, z, self.block(4), self.block(4), self.here.cn).wait_recv()
             for k in (3, 1, 2):
                 place = self.mine(z, k)
                 place[...] = place[...] + self.core_in(z, k)
@@ -322,9 +303,8 @@
         def body():
             place = self.mine(z, 0)
             total = place[...].astype(jnp.float32) + self.core_in(z, 0).astype(jnp.float32)
+            self.cp(1, 12 + z, self.side.at[:, z], self.side.at[:, z], here.xn).wait_recv()
             for side in (0, 1):
-                for h in (0, 1):
-                    self.side_cp(z, side, h).wait_recv()
                 total = total + self.side[side, z].astype(jnp.float32)
             if j == len(self.visits) - 1:
                 out[...] = total
@@ -337,29 +317,23 @@
     def last_cp(self, z):
         here = self.here
         device = {"dp": here.d, "blk": z * 2 + here.x}
-        return remote(self.mine(z, 0), self.last.at[here.z], self.sem("l", z, 0), self.sem("l", here.z, 1), device)
+        return self.cp(2, 16, self.mine(z, 0), self.last.at[here.z], device)
+
+    def others(self):
+        others = self.last.at[pl.ds(0, self.nz - 1)]
+        return self.cp(2, 16, others, others, self.here.up)
 
     def total(self, out):
         here = self.here
+        self.others().wait_recv()
         for k in range(1, self.nz):
-            z = (here.z + k) % self.nz
-            remote(self.last.at[z], self.last.at[z], self.sem("l", z, 0), self.sem("l", z, 1), here.up).wait_recv()
-            out[...] += self.last[z].astype(jnp.float32)
+            out[...] += self.last[(here.z + k) % self.nz].astype(jnp.float32)
 
     def finish(self):
-        for j, (z, valid) in enumerate(self.visits):
-
-            def body():
-                for k in range(4):
-                    self.core_cp(z, k).wait_send()
-                for h in (0, 1):
-                    self.half_cp(z, h).wait_send()
-                    for side in (0, 1):
-                        self.side_cp(z, side, h).wait_send()
-                if j < len(self.visits) - 1:
-                    self.last_cp(z).wait_send()
-
-            guarded(valid, body)
+        here = self.here
+        self.cp(0, 0, self.block(4 * self.nz), self.block(4 * self.nz), here.cn).wait_send()
+        self.cp(1, 0, self.block(3 * self.nz), self.block(3 * self.nz), here.xn).wait_send()
+        self.others().wait_send()
 
     def table(self, name, out):
         kinds = {"c": self.corner, "e": self.edges, "f": lambda j: self.column(j, out)}
@@ -378,6 +352,14 @@
     return ref.at[pl.ds(0, split)] if half == 0 else ref.at[pl.ds(split, rows - split)]
 
 
+def weight_block(ref):
+    return lambda n: ref.at[pl.ds(0, n * 288), pl.ds(0, 256)]
+
+
+def stacked_block(ref):
+    return lambda n: ref.at[pl.ds(0, n // 2), :, pl.ds(0, 256)]
+
+
 def weight_places(ref, rows, split=0):
     def at(z, x, d, half=None):
         base, count = (z * 2 + x) * rows, rows
@@ -434,7 +416,7 @@
     def line(self, k):
         return {"dp": self.d, "blk": ((self.z + k) % 4) * 2 + self.x}
 
-    def enter(self, shares, lines):
+    def greet(self, shares, lines):
         barrier = pltpu.get_barrier_semaphore()
 
         def greet(device):
@@ -457,7 +439,10 @@
             for k in (0, 1):
                 pl.when(jnp.logical_not(both(near, self.mu == k)))(lambda k=k: greet(self.column_worker(k)))
             count = count + 6 - 2 * self.alone.astype(jnp.int32) - near.astype(jnp.int32)
-        pl.semaphore_wait(barrier, count)
+        return count
+
+    def enter(self, count):
+        pl.semaphore_wait(pltpu.get_barrier_semaphore(), count)
 
 
 class Share:
@@ -557,26 +542,21 @@
     def __init__(self, u, buf, sems):
         self.u, self.buf, self.sems = u, buf, sems
 
-    def cps(self):
+    def send(self):
         u = self.u
-        out = []
+        block = self.buf.at[u.q]
         for k in (1, 2, 3):
-            out.append((self.buf.at[u.q], self.sems.at[0, k], self.sems.at[1, u.q], u.peer((u.q + k) % 4)))
-        return out
-
-    def send(self):
-        for ref, s, r, dev in self.cps():
-            remote(ref, ref, s, r, dev).start()
+            remote(block, block, self.sems.at[0], self.sems.at[1], u.peer((u.q + k) % 4)).start()
+
+    def three(self):
+        block = self.buf.at[pl.ds(0, 3)]
+        return remote(block, block, self.sems.at[0], self.sems.at[1], self.u.cn)
 
     def wait(self):
-        u = self.u
-        for k in (1, 2, 3):
-            p = (u.q + k) % 4
-            remote(self.buf.at[p], self.buf.at[p], self.sems.at[0, k], self.sems.at[1, p], u.peer(p)).wait_recv()
+        self.three().wait_recv()
 
     def sent(self):
-        for ref, s, r, dev in self.cps():
-            remote(ref, ref, s, r, dev).wait_send()
+        self.three().wait_send()
 
     def total(self):
         return self.buf[0] + self.buf[1] + self.buf[2] + self.buf[3]
@@ -826,41 +806,43 @@
         return self.ref.at[2 * (member // 2) + part, pl.ds(4 * x, 4)]
 
 
-def unit_inputs(features, bounds, out_grad, norms, conv1, conv2, attn):
+def unit_inputs(bounds, norms):
     d, b = lax.axis_index("dp"), lax.axis_index("blk")
-    limits = jnp.broadcast_to(bounds.reshape(-1).astype(F32)[:, None], (4, 512))
-    limits = jnp.concatenate([limits, jnp.zeros((4, 512), F32)])
     rows = jnp.stack([item.astype(F32) for item in norms])
-    mine = jnp.where(d == b // 2, rows, 0.0)
-    params = jnp.concatenate([jnp.where(b % 2 == 0, mine, 0.0), jnp.where(b % 2 == 1, mine, 0.0)], axis=1)
-    params = jnp.concatenate([params, jnp.zeros((PARAMS - 6, 128), F32)])
-    return (features[0], out_grad[0], limits, params, conv1, conv2, jnp.concatenate(attn))
+    lane = jnp.arange(128)[None] // 64
+    params = jnp.where((d == b // 2) & (lane == b % 2), jnp.concatenate([rows, rows], axis=1), 0.0)
+    limits = jnp.broadcast_to(bounds.reshape(-1).astype(F32)[:, None], (4, 128))
+    blank = jnp.zeros((2, 128), F32)
+    return jnp.concatenate([params, blank, limits, blank, blank])
 
 
 def whole_kernel(
-    feat, grad, bounds, par, s1, s2, sa,
-    act_back, grad_back, g1_out, g2_out, ga_out, norm_out,
+    feat, grad, par, s1, s2, sq, sk, sv, so,
+    act_back, grad_back, weights_out, norm_out,
     w1, w2, wa, pb, bb, xin, oall, nall, taps, a1, a2, masks, hidden, resid, small, rows_a, rows_b, swaps, lds,
     wg1, wg2, scores, gk, gv, lcol, dcol, big, gres, low, act, act_t1, act_t2, ga, mine, psum_y, psum_z,
     core_a, core_2, half_a, rest_a, side_a, last_a, half_2, rest_2, side_2, last_2, half_1, rest_1, side_1, last_1,
     gsems, ssems, local, share_sems, bound_sems, swap_sems, spread_sems, halo_sems, py_sems, pz_sems,
 ):
     u = Unit()
-    u.enter(True, True)
+    greeters = u.greet(True, True)
     mine[...] = jnp.zeros_like(mine)
     table = {}
     ats = (weight_places(w1, 576, SPLIT), weight_places(w2, 576, SPLIT), attn_places(wa, SPLIT_A), param_places(pb))
-    groups = [Gather(u, 4, at, gsems.at[k], DIRECT[k]) for k, at in enumerate(ats)]
+    blocks = (weight_block(w1), weight_block(w2), stacked_block(wa), stacked_block(pb))
+    groups = [Gather(u, 4, ats[k], blocks[k], gsems.at[k], DIRECT[k]) for k in range(4)]
     for name, group in zip(("g1", "g2", "ga", "gp"), groups):
         table.update(group.table(name))
-    sources = (s1, s2, sa, par)
-    own = [pltpu.make_async_copy(src, group.own(u.z), local.at[k]) for k, (src, group) in enumerate(zip(sources, groups))]
-    for copy in own:
+    own = [pltpu.make_async_copy(src, groups[k].own(u.z), local.at[k]) for k, src in ((0, s1), (1, s2), (3, par))]
+    for k, src in enumerate((sq, sk, sv, so)):
+        own.append(pltpu.make_async_copy(src, groups[2].own(u.z).at[pl.ds(64 * k, 64)], local.at[8 + k]))
+    keep = pltpu.make_async_copy(par, bb.at[u.c], local.at[4])
+    for copy in own + [keep]:
         copy.start()
-    keep = pltpu.make_async_copy(bounds, bb.at[u.c], local.at[4])
-    keep.start()
+    g1_out, g2_out = weights_out.at[pl.ds(0, 576)], weights_out.at[pl.ds(576, 576)]
+    ga_out = weights_out.at[pl.ds(1152, 256)]
     share_x, share_a, share_g = [Share(u, share_sems.at[k], local.at[5 + k]) for k in range(3)]
-    share_o = ColumnShare(u, oall, share_sems.at[3], local.at[8])
+    share_o = ColumnShare(u, oall, share_sems.at[3], local.at[2])
     swap = [Swap(u, swaps.at[k], swap_sems.at[k]) for k in range(6)] + [Swap(u, lds, swap_sems.at[6])]
     halo = [Halo(u, (a1, a2)[k % 2], halo_sems.at[k]) for k in range(4)]
     spread_o = Spread(u, Blocks(oall), spread_sems.at[0], 2)
@@ -870,17 +852,17 @@
     part_a = lambda ref, h: part_of(ref, h, CUT_A, 256)
     part_w = lambda ref, h: part_of(ref, h, CUT, 576)
     sum_a = Scatter(
-        u, 4, attn_places(ga), lambda k, z, x, d: core_a.at[k, z], part_a, ssems.at[0], ((half_a, rest_a), side_a, last_a)
+        u, 4, attn_places(ga), lambda k, z, x, d: core_a.at[k, z], part_a, stacked_block(ga), ssems.at[0], ((half_a, rest_a), side_a, last_a)
     )
     sum_2 = Scatter(
-        u, 4, weight_places(wg2, 576), lambda k, z, x, d: core_2.at[k, z], part_w, ssems.at[1], ((half_2, rest_2), side_2, last_2)
+        u, 4, weight_places(wg2, 576), lambda k, z, x, d: core_2.at[k, z], part_w, weight_block(wg2), ssems.at[1], ((half_2, rest_2), side_2, last_2)
     )
     sum_1 = Scatter(
-        u, 4, weight_places(wg1, 576), lambda k, z, x, d: w2_at(z, x, d), part_w, ssems.at[2], ((half_1, rest_1), side_1, last_1)
+        u, 4, weight_places(wg1, 576), lambda k, z, x, d: w2_at(z, x, d), part_w, weight_block(wg1), ssems.at[2], ((half_1, rest_1), side_1, last_1)
     )
     for name, total, out in (("ra", sum_a, ga_out), ("r2", sum_2, g2_out), ("r1", sum_1, g1_out)):
         table.update(total.table(name, out))
-    bound_cp = remote(bounds, bb.at[u.c], bound_sems.at[0], bound_sems.at[1], u.cn)
+    bound_cp = remote(par, bb.at[u.c], bound_sems.at[0], bound_sems.at[1], u.cn)
     state = {}
 
     def step(function):
@@ -901,12 +883,14 @@
     def ow():
         for copy in own:
             copy.wait()
+        u.enter(greeters)
 
     @step
     def bw():
         keep.wait()
-        remote(bounds, bb.at[1 - u.c], bound_sems.at[0], bound_sems.at[1], u.cn).wait_recv()
-        limits = jnp.where(u.mu == 0, bb[u.z // 2, 0:2, :], bb[u.z // 2, 2:4, :])
+        remote(par, bb.at[1 - u.c], bound_sems.at[0], bound_sems.at[1], u.cn).wait_recv()
+        limits = jnp.where(u.mu == 0, bb[u.z // 2, 8:10, :], bb[u.z // 2, 10:12, :])
+        limits = jnp.concatenate([limits] * 4, axis=1)
         small[7] = jnp.concatenate([limits, jnp.zeros((6, limits.shape[1]), F32)], axis=0)
         state["seg"] = tap_masks(u, limits, masks)
         state["counts"] = counts_of(limits, 4.0 * ROW)
@@ -1026,6 +1010,7 @@
         table["nr%d" % part] = functools.partial(spread_n.relay, part)
 
     scale = 512.0 ** (-0.5)
+    steep = scale * 1.4426950408889634
 
     def slot(ref, i):
         return ref.at[pl.ds(pl.multiple_of(i * 512, 512), 512)]
@@ -1091,12 +1076,12 @@
         seg = seg_col(u.q, j * 256, 256)
         most = jnp.full((256, 1), NEGATIVE, F32)
         for i in range(4):
-            part = jnp.where(seg == seg_row(i), cols(query, key_of(i)[...]) * scale, NEGATIVE)
+            part = jnp.where(seg == seg_row(i), cols(query, key_of(i)[...]) * steep, NEGATIVE)
             scores[i] = part
             most = jnp.maximum(most, jnp.max(part, axis=1, keepdims=True))
         total = jnp.zeros((256, 1), F32)
         for i in range(4):
-            part = jnp.exp(scores[i] - most)
+            part = jnp.exp2(scores[i] - most)
             total = total + jnp.sum(part, axis=1, keepdims=True)
             scores[i] = part
         inverse = 1.0 / total
@@ -1106,7 +1091,7 @@
             kept(j, i)[...] = part.reshape(4, 64, 512)
             found = found + mm(part, value_of(i)[...])
         heads[block, :] = found.astype(BF)
-        lcol[block, :] = jnp.broadcast_to(most + jnp.log(total), (256, 128))
+        lcol[block, :] = jnp.broadcast_to(most + jnp.log2(total), (256, 128))
         return carry
 
     @step
@@ -1150,18 +1135,16 @@
     def hw():
         ga[:, 192:256, :] = mm(heads[...].T, oall[u.q].reshape(512, 512)).astype(BF).reshape(8, 64, 512)
 
-    def keys(index, carry):
-        i, j = index // 2, index % 2
-        block = pl.ds(pl.multiple_of(j * 256, 256), 256)
-        key, value = key_of(u.q)[block], value_of(u.q)[block]
+    def keys(i, carry):
         query, upstream = query_of(i)[...], upstream_of(i)[...]
-        shared = seg_col(u.q, j * 256, 256) == seg_row(i)
-        part = jnp.where(shared, cols(key, query) * scale, NEGATIVE)
-        part = jnp.where(shared, jnp.exp(part - lds[i, 0:1, :]), 0.0)
-        rows = pl.ds(pl.multiple_of(j * 4, 4), 4)
-        gres[rows] += mm(part.astype(BF), upstream).reshape(4, 64, 512)
-        slope = cols(value, upstream) - lds[i, 1:2, :]
-        big[rows] += mm((part * slope).astype(BF), query).reshape(4, 64, 512)
+        for j in (0, 1):
+            key, value = key_of(u.q)[256 * j : 256 * j + 256], value_of(u.q)[256 * j : 256 * j + 256]
+            shared = seg_col(u.q, j * 256, 256) == seg_row(i)
+            part = jnp.exp2(jnp.where(shared, cols(key, query) * steep, NEGATIVE) - lds[i, 0:1, :])
+            slope = cols(value, upstream) - lds[i, 1:2, :]
+            rows = pl.ds(4 * j, 4)
+            gres[rows] += mm(part.astype(BF), upstream).reshape(4, 64, 512)
+            big[rows] += mm((part * slope).astype(BF), query).reshape(4, 64, 512)
         return carry
 
     @step
@@ -1169,7 +1152,7 @@
         big[...] = jnp.zeros_like(big)
         gres[...] = jnp.zeros_like(gres)
         swap[6].wait()
-        lax.fori_loop(0, 8, keys, 0)
+        lax.fori_loop(0, 4, keys, 0)
         gk[...] = (big[...] * scale).astype(BF).reshape(512, 512)
         gv[...] = gres[...].astype(BF).reshape(512, 512)
 
@@ -1291,22 +1274,21 @@
         table["w2%d" % k] = functools.partial(conv_weight_grad, act_t2, taps, wg2, 3 * k, 3 * k + 3)
         table["w1%d" % k] = functools.partial(conv_weight_grad, act_t1, taps, wg1, 3 * k, 3 * k + 3)
 
-    def line_cp(k):
-        return remote(psum_z.at[u.z], psum_z.at[u.z], pz_sems.at[0, k], pz_sems.at[1, u.z], u.line(k))
+    def line_cp(block, k):
+        return remote(block, block, pz_sems.at[0], pz_sems.at[1], u.line(k))
 
     @step
     def py():
         remote(mine, psum_y, py_sems.at[0], py_sems.at[1], u.yn).wait()
         psum_z[u.z] = mine[...] + psum_y[...]
         for k in (1, 2, 3):
-            line_cp(k).start()
+            line_cp(psum_z.at[u.z], k).start()
 
     @step
     def pz():
-        for k in (1, 2, 3):
-            other = (u.z + k) % 4
-            remote(psum_z.at[other], psum_z.at[other], pz_sems.at[0, k], pz_sems.at[1, other], u.line(k)).wait_recv()
-        norm_out[...] = psum_z[0] + psum_z[1] + psum_z[2] + psum_z[3]
+        line_cp(psum_z.at[pl.ds(0, 3)], 1).wait_recv()
+        total = psum_z[0] + psum_z[1] + psum_z[2] + psum_z[3]
+        norm_out[...] = pltpu.roll(total, lax.rem(512 - 64 * u.b, 512), 1)[:, 0:128]
 
     in_order(types.SimpleNamespace(**table))
 
@@ -1322,11 +1304,10 @@
     for item in (spread_o, spread_n):
         for part in range(2):
             item.sent(part)
-    for k in (1, 2, 3):
-        line_cp(k).wait_send()
-
-
-def whole_call(features, out_grad, limits, params, s1, s2, sa):
+    line_cp(psum_z.at[pl.ds(0, 3)], 1).wait_send()
+
+
+def whole_call(features, out_grad, params, *shards):
     full = lambda shape, kind: jax.ShapeDtypeStruct(shape, kind)
     dma = pltpu.SemaphoreType.DMA
     rows, padded, square, weight = (ROW, 64, 512), (ROW + 2, 64, 512), (512, 512), (4608, 512)
@@ -1338,24 +1319,24 @@
     return pl.pallas_call(
         whole_kernel,
         out_shape=[
-            full((2, 4, 64, 512), BF), full((2, 4, 64, 512), BF), full((576, 128), F32), full((576, 128), F32),
-            full((256, 128), F32), full((8, 512), F32),
+            full((2, 4, 64, 512), BF), full((2, 4, 64, 512), BF), full((1408, 128), F32),
+            full((8, 128), F32),
         ],
-        in_specs=[ANY] * 7,
-        out_specs=[VM] * 6,
+        in_specs=[ANY] * 9,
+        out_specs=[VM] * 4,
         scratch_shapes=[
-            low(*weight), low(*weight), low(8, 256, 512), wide(8, PARAMS, 512), wide(2, 8, 512), low(*rows),
+            low(*weight), low(*weight), low(8, 256, 512), wide(8, PARAMS, 512), wide(2, PARAMS, 128), low(*rows),
             low(4, *rows), low(4, *rows), low(9, *rows), low(*padded), low(*padded), wide(2, ROW, 512),
             wide(*rows), wide(*rows), wide(8, 8, 512), wide(ROW, 512), wide(ROW, 512), wide(6, 4, 8, 512), wide(4, 8, 512),
             low(*weight), low(*weight), wide(4, 256, 512), low(*square), low(*square),
             wide(512, 128), wide(512, 128), wide(*rows), wide(*rows), low(*rows), low(*rows), low(*square), low(*square),
             low(8, 256, 512), wide(8, 512), wide(8, 512), wide(4, 8, 512),
             low(4, 4, 256, 128), low(4, 4, 576, 128), *sums,
-            dma((4, 2, Gather.SEMS)), dma((3, 2, Scatter.SEMS)), dma((9,)), dma((4, 2, 2)), dma((2,)), dma((7, 2, 4)),
-            dma((2, 2, 3, 2)), dma((4, 2, 2)), dma((2,)), dma((2, 4)),
+            dma((4, Gather.SEMS)), dma((3, Scatter.SEMS)), dma((12,)), dma((4, 2, 2)), dma((2,)), dma((7, 2)),
+            dma((2, 2, 3, 2)), dma((4, 2, 2)), dma((2,)), dma((2,)),
         ],
         compiler_params=pltpu.CompilerParams(collective_id=0, has_side_effects=True, vmem_limit_bytes=LIMIT),
-    )(features, out_grad, limits, params, s1, s2, sa)
+    )(features, out_grad, params, *shards)
 
 
 def unit_shards(
@@ -1363,12 +1344,12 @@
     norm3_gain, norm3_shift, query_weight, key_weight, value_weight, output_weight,
 ):
     norms = (norm1_gain, norm1_shift, norm2_gain, norm2_shift, norm3_gain, norm3_shift)
-    attn = (query_weight, key_weight, value_weight, output_weight)
-    act_back, grad_back, g1, g2, ga, norms = whole_call(
-        *unit_inputs(features, bounds, out_grad, norms, conv1_weight, conv2_weight, attn)
-    )
-    norms = lax.dynamic_slice_in_dim(norms, lax.axis_index("blk") * 64, 64, axis=1)
-    ga = ga.reshape(4, 64, 128)
+    act_back, grad_back, weights, norms = whole_call(
+        features[0], out_grad[0], unit_inputs(bounds, norms), conv1_weight, conv2_weight,
+        query_weight, key_weight, value_weight, output_weight,
+    )
+    norms = norms[:, :64]
+    g1, g2, ga = weights[:576], weights[576:1152], weights[1152:].reshape(4, 64, 128)
     return (
         act_back.astype(F32)[None], grad_back.astype(F32)[None], norms[0], norms[1], g1, norms[2], norms[3], g2,
         norms[4], norms[5], ga[0], ga[1], ga[2], ga[3],

time: 201 us -> 192 us (0.955)
  Pallas kernels: 190 us -> 182 us
    pallas_call x1, Pallas kernels: 190 us -> 182 us  [whole_call(): pl.pallas_call(whole_kernel, out_shape=[full((2, 4, 64, 512), BF), full((...]
where the time goes in v4:
time: 192 us; the launch traced here: 191 us
  Pallas kernels  182 us (95%)
  local copies, waits for them, and re-layouts  6.21 us (3%)
  other arithmetic  2.36 us (1%)
    pallas_call x1, Pallas kernels, whole_call(): pl.pallas_call(whole_kernel, out_shape=[full((2, 4, 64, 512), BF), full((...  182 us

profile of v4, /device:TPU:0, one launch (start us, length us, event | category | flops | bytes accessed | tf_op | source)
XLA Modules:
  0.0 191.4 jit_solution(17603185848467562381)
XLA Ops:
  0.7 0.1 pad.1.clone
  0.8 0.0 copy-start.3
  0.8 0.1 pad.3.clone
  0.8 0.6 copy-done.3
  1.4 0.0 copy-start.7
  1.5 0.1 reshape.87
  1.5 0.1 pad.2.clone
  1.6 0.5 copy-done.7
  2.1 0.0 copy-done.8
  2.1 0.0 copy-done.9
  2.1 0.1 copy-done.4
  2.2 0.0 copy-done.5
  2.2 0.0 copy-done.6
  2.3 0.1 convert_select_fusion
  2.3 0.7 maximum_maximum_fusion.par
  3.0 182.1 %shard_map.254 = (bf16[2,4,64,512]{3,2,1,0:T(8,128)(2,1)}, bf16[2,4,64,512]{3,2,1,0:T(8,128)(2,1)}, f32[1408,128]{1,0:T(8,128)}, f32[8,128]{1,0:T(8,128)}) custom-call(bf16[2,4,64,512]{3,2,1,0:T(8,128)(2,1)} %bitcast.26, bf16[2,4,64,512]{3,2,1,0:T(8,128)(2,1)} %bitcast.27, f32[16,128]{1,0:T(8,128)} %maximum_maximum_fusion.par, bf16[576,128]{1,0:T(8,128)(2,1)} %s1_.1, ...), custom_call_target="tpu_custom_call" | custom-call | tf_op jit(solution)/shard_map/pallas_call | solution.py:1319
  185.1 0.0 copy-start.2
  185.1 0.7 copy-done.2
  185.8 0.5 slice_bitcast_fusion
  186.3 1.5 fusion
  187.8 2.0 %fusion.1 = (f32[576,128]{1,0:T(8,128)}, f32[576,128]{1,0:T(8,128)}) fusion(f32[1408,128]{1,0:T(8,128)} %get-tuple-element.21), kind=kLoop, calls=%fused_computation.16 | loop fusion | bytes 1179648 | tf_op jit(solution)/shard_map/slice | solution.py:1352
  189.8 0.0 copy-done
  189.8 0.0 copy-done.1
  189.8 1.6 bitcast_convert_fusion
  (12 shorter events, 0.1 us)
Async XLA Ops:
  0.8 0.7 copy-start.3
  1.4 0.7 copy-start.7
  1.5 0.7 copy-start.8
  1.5 0.7 copy-start.9
  1.5 0.7 copy-start.4
  1.5 0.7 copy-start.5
  1.5 0.7 copy-start.6
  185.1 0.7 copy-start.2
  187.8 2.0 %copy-start = (bf16[2,4,64,512]{3,2,1,0:T(8,128)(2,1)S(1)}, bf16[2,4,64,512]{3,2,1,0:T(8,128)(2,1)}, u32[]{:S(2)}) copy-start(bf16[2,4,64,512]{3,2,1,0:T(8,128)(2,1)} %get-tuple-element.18) | copy-start | bytes 1572868
  187.8 2.0 %copy-start.1 = (bf16[2,4,64,512]{3,2,1,0:T(8,128)(2,1)S(1)}, bf16[2,4,64,512]{3,2,1,0:T(8,128)(2,1)}, u32[]{:S(2)}) copy-start(bf16[2,4,64,512]{3,2,1,0:T(8,128)(2,1)} %get-tuple-element.19) | copy-start | bytes 1572868

commit v5 on v4

--- a/solution.py
+++ b/solution.py
@@ -17,31 +17,31 @@
 NEGATIVE = -1e30
 MESH = pl.DeviceIdType.MESH
 def in_order(s):
-    s.ow(), s.gpl0(), s.g1l0(), s.gpo0(), s.gao0(), s.g2o0(), s.g2l0(), s.gpl1()
-    s.gpo1(), s.gal0(), s.g1l1(), s.g1o1(), s.gpl2(), s.g2l1(), s.g1o0(), s.gpo2()
-    s.gpy1(), s.gpx1(), s.g1l2(), s.gpl3(), s.g2o1(), s.gpo3(), s.g1o2(), s.gpx0()
-    s.gpx3(), s.gpy0(), s.g1l3(), s.g1o3(), s.xs(), s.g2l2(), s.gpy2(), s.g1x1()
-    s.gal1(), s.g1x2(), s.gpx2(), s.gpy3(), s.bw(), s.g2x0(), s.g1x3(), s.g1y0()
-    s.g2l3(), s.g1y2(), s.g1y1(), s.gal2(), s.g1y3(), s.g2o3(), s.g1x0(), s.n1a()
-    s.gao1(), s.gpd2(), s.os(), s.gpd0(), s.g2o2(), s.gpd1(), s.gpd3(), s.n1b()
-    s.gal3(), s.n1c(), s.gao2(), s.g1d0(), s.g1d1(), s.g1d3(), s.n1d(), s.g2y3()
-    s.g1d2(), s.g2y0(), s.g2x3(), s.g1a(), s.g2y1(), s.gao3(), s.n1e(), s.c10()
-    s.c11(), s.n2a(), s.g2x2(), s.g2y2(), s.gay1(), s.gax3(), s.gay2(), s.g2x1()
-    s.gay3(), s.g2d3(), s.gay0(), s.n2b(), s.n2c(), s.ob(), s.g2d2(), s.n2d()
-    s.gax1(), s.n2e(), s.g2d0(), s.g2d1(), s.g2a(), s.c20(), s.gax2(), s.gad1()
-    s.c21(), s.n3a(), s.gad2(), s.gax0(), s.n3b(), s.n3c(), s.t2(), s.gad3()
-    s.or0(), s.or1(), s.gad0(), s.gaa(), s.po1(), s.pj1(), s.pj0(), s.po0()
-    s.po2(), s.nr0(), s.po3(), s.nr1(), s.pj2(), s.pj3(), s.qf(), s.qb()
-    s.hw(), s.gz(), s.hd(), s.ks(), s.an(), s.b3a(), s.aw(), s.rab3()
-    s.rab0(), s.t1(), s.rab1(), s.rab2(), s.rac3(), s.b3b(), s.rac1(), s.b3c()
-    s.rac2(), s.rac0(), s.b3d(), s.d20(), s.w20(), s.d21(), s.b2a(), s.r2b0()
-    s.w21(), s.r2b1(), s.w22(), s.r2b3(), s.rae2(), s.b2b(), s.r2b2(), s.rae1()
-    s.r2c2(), s.b2c(), s.raf2(), s.r2c3(), s.r2c0(), s.b2d(), s.d10(), s.d11()
-    s.b1a(), s.rae3(), s.r2e2(), s.w10(), s.r2e3(), s.raf1(), s.rae0(), s.b1m()
-    s.r2c1(), s.b1b(), s.raf3(), s.r2e0(), s.w11(), s.r1b0(), s.r2f2(), s.ps()
-    s.w12(), s.r1b3(), s.r1b1(), s.r1b2(), s.r1c3(), s.r2f3(), s.r1e3(), s.r1c2()
-    s.raf0(), s.r1f3(), s.r2e1(), s.r1e2(), s.py(), s.r2f0(), s.r1c1(), s.r2f1()
-    s.r1e1(), s.r1c0(), s.rat(), s.r1f2(), s.r1f1(), s.pz(), s.r1e0(), s.r2t()
+    s.ow(), s.gpl0(), s.g1l0(), s.g1o0(), s.g2o0(), s.gpo0(), s.g2l0(), s.gpl1()
+    s.gao0(), s.g1l1(), s.g2y0(), s.gpl2(), s.g1y0(), s.gpo2(), s.g1x0(), s.gpo1()
+    s.g2l1(), s.gpl3(), s.g1o1(), s.gpo3(), s.g1l2(), s.gal0(), s.g2o1(), s.g1o2()
+    s.gpx2(), s.g1l3(), s.gpy3(), s.gpx1(), s.gpy0(), s.g1o3(), s.gpx0(), s.xs()
+    s.g2x0(), s.gal1(), s.gpy1(), s.gpx3(), s.g2l2(), s.g1x1(), s.gpy2(), s.g1x2()
+    s.g1y3(), s.g1x3(), s.g1y2(), s.bw(), s.gal2(), s.g2l3(), s.gpd3(), s.gpd1()
+    s.g2o3(), s.gal3(), s.os(), s.gpd0(), s.n1a(), s.gpd2(), s.g1y1(), s.gax0()
+    s.g1d0(), s.g1d3(), s.g2o2(), s.n1b(), s.n1c(), s.gao2(), s.gao3(), s.g1d1()
+    s.g1d2(), s.n1d(), s.gao1(), s.g2y3(), s.g1a(), s.n1e(), s.c10(), s.c11()
+    s.n2a(), s.gay3(), s.gay0(), s.g2x3(), s.g2d0(), s.g2x2(), s.g2x1(), s.g2y2()
+    s.gax1(), s.g2y1(), s.gay2(), s.gay1(), s.n2b(), s.n2c(), s.ob(), s.gax3()
+    s.n2d(), s.n2e(), s.g2d3(), s.g2d2(), s.g2d1(), s.g2a(), s.c20(), s.c21()
+    s.gax2(), s.gad1(), s.n3a(), s.t1(), s.or0(), s.gad3(), s.gad2(), s.gad0()
+    s.or1(), s.n3b(), s.n3c(), s.t2(), s.gaa(), s.po0(), s.pj1(), s.nr0()
+    s.po1(), s.po2(), s.pj0(), s.po3(), s.nr1(), s.pj2(), s.pj3(), s.qf()
+    s.qb(), s.hw(), s.gz(), s.hd(), s.ks(), s.an(), s.b3a(), s.aw()
+    s.rab0(), s.rab2(), s.rab1(), s.rab3(), s.b3b(), s.b3c(), s.rac1(), s.rac3()
+    s.rac2(), s.rac0(), s.b3d(), s.w20(), s.d20(), s.d21(), s.b2a(), s.w21()
+    s.rae2(), s.r2b0(), s.w22(), s.r2b3(), s.r2b1(), s.rae1(), s.b2b(), s.r2b2()
+    s.r2c3(), s.r2c2(), s.r2c1(), s.b2c(), s.rae0(), s.raf2(), s.b2d(), s.d10()
+    s.d11(), s.b1a(), s.raf1(), s.r2e3(), s.r2e2(), s.w10(), s.b1m(), s.rae3()
+    s.ps(), s.b1b(), s.r2c0(), s.r1b0(), s.w11(), s.r1b1(), s.w12(), s.r2f2()
+    s.py(), s.r1b3(), s.r1b2(), s.r2f3(), s.r1c3(), s.r2e1(), s.raf0(), s.r1e3()
+    s.r1c2(), s.raf3(), s.r1f3(), s.r1c1(), s.r2f1(), s.r1e2(), s.r1e1(), s.r1c0()
+    s.pz(), s.r2e0(), s.r1f2(), s.r1f1(), s.rat(), s.r1e0(), s.r2f0(), s.r2t()
     s.r1f0(), s.r1t()
 
 
@@ -1323,7 +1323,7 @@
             full((8, 128), F32),
         ],
         in_specs=[ANY] * 9,
-        out_specs=[VM] * 4,
+        out_specs=[ANY, ANY, VM, VM],
         scratch_shapes=[
             low(*weight), low(*weight), low(8, 256, 512), wide(8, PARAMS, 512), wide(2, PARAMS, 128), low(*rows),
             low(4, *rows), low(4, *rows), low(9, *rows), low(*padded), low(*padded), wide(2, ROW, 512),

time: 192 us -> 187 us (0.974)
  Pallas kernels: 182 us -> 177 us
    pallas_call x1, Pallas kernels: 182 us -> 177 us  [whole_call(): pl.pallas_call(whole_kernel, out_shape=[full((2, 4, 64, 512), BF), full((...]
where the time goes in v5:
time: 187 us
  Pallas kernels  177 us (95%)
  local copies, waits for them, and re-layouts  6.21 us (3%)
  other arithmetic  2.36 us (1%)
    pallas_call x1, Pallas kernels, whole_call(): pl.pallas_call(whole_kernel, out_shape=[full((2, 4, 64, 512), BF), full((...  177 us

profile of v5, /device:TPU:0, one launch (start us, length us, event | category | flops | bytes accessed | tf_op | source)
XLA Modules:
  0.0 186.5 jit_solution(4630715705739416716)
XLA Ops:
  0.7 0.1 pad.1.clone
  0.8 0.0 copy-start.3
  0.8 0.1 pad.3.clone
  0.8 0.6 copy-done.3
  1.4 0.0 copy-start.7
  1.5 0.1 reshape.87
  1.5 0.1 pad.2.clone
  1.6 0.5 copy-done.7
  2.1 0.0 copy-done.8
  2.1 0.0 copy-done.9
  2.1 0.1 copy-done.4
  2.2 0.0 copy-done.5
  2.2 0.0 copy-done.6
  2.3 0.1 convert_select_fusion
  2.3 0.7 maximum_maximum_fusion.par
  3.0 177.2 %shard_map.254 = (bf16[2,4,64,512]{3,2,1,0:T(8,128)(2,1)}, bf16[2,4,64,512]{3,2,1,0:T(8,128)(2,1)}, f32[1408,128]{1,0:T(8,128)}, f32[8,128]{1,0:T(8,128)}) custom-call(bf16[2,4,64,512]{3,2,1,0:T(8,128)(2,1)} %bitcast.26, bf16[2,4,64,512]{3,2,1,0:T(8,128)(2,1)} %bitcast.27, f32[16,128]{1,0:T(8,128)} %maximum_maximum_fusion.par, bf16[576,128]{1,0:T(8,128)(2,1)} %s1_.1, ...), custom_call_target="tpu_custom_call" | custom-call | tf_op jit(solution)/shard_map/pallas_call | solution.py:1319
  180.3 0.0 copy-start.2
  180.3 0.7 copy-done.2
  180.9 0.5 slice_bitcast_fusion
  181.5 1.5 fusion
  182.9 2.0 %fusion.1 = (f32[576,128]{1,0:T(8,128)}, f32[576,128]{1,0:T(8,128)}) fusion(f32[1408,128]{1,0:T(8,128)} %get-tuple-element.21), kind=kLoop, calls=%fused_computation.16 | loop fusion | bytes 1179648 | tf_op jit(solution)/shard_map/slice | solution.py:1352
  184.9 0.0 copy-done
  184.9 0.0 copy-done.1
  184.9 1.6 bitcast_convert_fusion
  (12 shorter events, 0.1 us)
Async XLA Ops:
  0.8 0.7 copy-start.3
  1.4 0.7 copy-start.7
  1.5 0.7 copy-start.8
  1.5 0.7 copy-start.9
  1.5 0.7 copy-start.4
  1.5 0.7 copy-start.5
  1.5 0.7 copy-start.6
  180.3 0.7 copy-start.2
  182.9 2.0 %copy-start = (bf16[2,4,64,512]{3,2,1,0:T(8,128)(2,1)S(1)}, bf16[2,4,64,512]{3,2,1,0:T(8,128)(2,1)}, u32[]{:S(2)}) copy-start(bf16[2,4,64,512]{3,2,1,0:T(8,128)(2,1)} %get-tuple-element.18) | copy-start | bytes 1572868
  182.9 2.0 %copy-start.1 = (bf16[2,4,64,512]{3,2,1,0:T(8,128)(2,1)S(1)}, bf16[2,4,64,512]{3,2,1,0:T(8,128)(2,1)}, u32[]{:S(2)}) copy-start(bf16[2,4,64,512]{3,2,1,0:T(8,128)(2,1)} %get-tuple-element.19) | copy-start | bytes 1572868

commit v6 on v5

--- a/solution.py
+++ b/solution.py
@@ -1070,54 +1070,54 @@
     def kept(j, i):
         return taps.at[i, pl.ds(pl.multiple_of(j * 4, 4), 4)]
 
-    def queries(j, carry):
-        block = pl.ds(pl.multiple_of(j * 256, 256), 256)
+    def queries(j):
+        block = pl.ds(j * 256, 256)
         query = query_of(u.q)[block]
         seg = seg_col(u.q, j * 256, 256)
         most = jnp.full((256, 1), NEGATIVE, F32)
         for i in range(4):
             part = jnp.where(seg == seg_row(i), cols(query, key_of(i)[...]) * steep, NEGATIVE)
-            scores[i] = part
+            scores[j, i] = part
             most = jnp.maximum(most, jnp.max(part, axis=1, keepdims=True))
         total = jnp.zeros((256, 1), F32)
         for i in range(4):
-            part = jnp.exp2(scores[i] - most)
+            part = jnp.exp2(scores[j, i] - most)
             total = total + jnp.sum(part, axis=1, keepdims=True)
-            scores[i] = part
+            scores[j, i] = part
         inverse = 1.0 / total
         found = jnp.zeros((256, 512), F32)
         for i in range(4):
-            part = (scores[i] * inverse).astype(BF)
+            part = (scores[j, i] * inverse).astype(BF)
             kept(j, i)[...] = part.reshape(4, 64, 512)
             found = found + mm(part, value_of(i)[...])
         heads[block, :] = found.astype(BF)
         lcol[block, :] = jnp.broadcast_to(most + jnp.log2(total), (256, 128))
-        return carry
 
     @step
     def qf():
-        lax.fori_loop(0, 2, queries, 0)
-
-    def queries_back(j, carry):
-        block = pl.ds(pl.multiple_of(j * 256, 256), 256)
+        for j in (0, 1):
+            queries(j)
+
+    def queries_back(j):
+        block = pl.ds(j * 256, 256)
         upstream = upstream_of(u.q)[block]
         correction = jnp.zeros((256, 1), F32)
         for i in range(4):
             slope = cols(upstream, value_of(i)[...])
-            scores[i] = slope
+            scores[j, i] = slope
             part = kept(j, i)[...].reshape(256, 512).astype(F32)
             correction = correction + jnp.sum(part * slope, axis=1, keepdims=True)
         back = jnp.zeros((256, 512), F32)
         for i in range(4):
             part = kept(j, i)[...].reshape(256, 512).astype(F32)
-            back = back + mm((part * (scores[i] - correction)).astype(BF), key_of(i)[...])
+            back = back + mm((part * (scores[j, i] - correction)).astype(BF), key_of(i)[...])
         gq[block, :] = (back * scale).astype(BF)
         dcol[block, :] = jnp.broadcast_to(correction, (256, 128))
-        return carry
 
     @step
     def qb():
-        lax.fori_loop(0, 2, queries_back, 0)
+        for j in (0, 1):
+            queries_back(j)
         lds[u.q] = jnp.concatenate([lcol[...].T[0:1], dcol[...].T[0:1], jnp.zeros((6, 512), F32)], axis=0)
         swap[6].send()
 
@@ -1328,7 +1328,7 @@
             low(*weight), low(*weight), low(8, 256, 512), wide(8, PARAMS, 512), wide(2, PARAMS, 128), low(*rows),
             low(4, *rows), low(4, *rows), low(9, *rows), low(*padded), low(*padded), wide(2, ROW, 512),
             wide(*rows), wide(*rows), wide(8, 8, 512), wide(ROW, 512), wide(ROW, 512), wide(6, 4, 8, 512), wide(4, 8, 512),
-            low(*weight), low(*weight), wide(4, 256, 512), low(*square), low(*square),
+            low(*weight), low(*weight), wide(2, 4, 256, 512), low(*square), low(*square),
             wide(512, 128), wide(512, 128), wide(*rows), wide(*rows), low(*rows), low(*rows), low(*square), low(*square),
             low(8, 256, 512), wide(8, 512), wide(8, 512), wide(4, 8, 512),
             low(4, 4, 256, 128), low(4, 4, 576, 128), *sums,

time: 187 us -> 186 us (level)
  no operation moved by 1% of the time
where the time goes in v6:
time: 186 us
  Pallas kernels  176 us (95%)
  local copies, waits for them, and re-layouts  6.21 us (3%)
  other arithmetic  2.36 us (1%)
    pallas_call x1, Pallas kernels, whole_call(): pl.pallas_call(whole_kernel, out_shape=[full((2, 4, 64, 512), BF), full((...  176 us

profile of v6, /device:TPU:0, one launch (start us, length us, event | category | flops | bytes accessed | tf_op | source)
XLA Modules:
  0.0 185.7 jit_solution(12785204238800688298)
XLA Ops:
  0.7 0.1 pad.1.clone
  0.8 0.0 copy-start.3
  0.8 0.1 pad.3.clone
  0.8 0.6 copy-done.3
  1.4 0.0 copy-start.7
  1.5 0.1 reshape.87
  1.5 0.1 pad.2.clone
  1.6 0.5 copy-done.7
  2.1 0.0 copy-done.8
  2.1 0.0 copy-done.9
  2.1 0.1 copy-done.4
  2.2 0.0 copy-done.5
  2.2 0.0 copy-done.6
  2.3 0.1 convert_select_fusion
  2.3 0.7 maximum_maximum_fusion.par
  3.0 176.4 %shard_map.254 = (bf16[2,4,64,512]{3,2,1,0:T(8,128)(2,1)}, bf16[2,4,64,512]{3,2,1,0:T(8,128)(2,1)}, f32[1408,128]{1,0:T(8,128)}, f32[8,128]{1,0:T(8,128)}) custom-call(bf16[2,4,64,512]{3,2,1,0:T(8,128)(2,1)} %bitcast.26, bf16[2,4,64,512]{3,2,1,0:T(8,128)(2,1)} %bitcast.27, f32[16,128]{1,0:T(8,128)} %maximum_maximum_fusion.par, bf16[576,128]{1,0:T(8,128)(2,1)} %s1_.1, ...), custom_call_target="tpu_custom_call" | custom-call | tf_op jit(solution)/shard_map/pallas_call | solution.py:1319
  179.4 0.0 copy-start.2
  179.4 0.7 copy-done.2
  180.1 0.5 slice_bitcast_fusion
  180.6 1.5 fusion
  182.1 2.0 %fusion.1 = (f32[576,128]{1,0:T(8,128)}, f32[576,128]{1,0:T(8,128)}) fusion(f32[1408,128]{1,0:T(8,128)} %get-tuple-element.21), kind=kLoop, calls=%fused_computation.16 | loop fusion | bytes 1179648 | tf_op jit(solution)/shard_map/slice | solution.py:1352
  184.1 0.0 copy-done
  184.1 0.0 copy-done.1
  184.1 1.6 bitcast_convert_fusion
  (12 shorter events, 0.1 us)
Async XLA Ops:
  0.8 0.7 copy-start.3
  1.4 0.7 copy-start.7
  1.5 0.7 copy-start.8
  1.5 0.7 copy-start.9
  1.5 0.7 copy-start.4
  1.5 0.7 copy-start.5
  1.5 0.7 copy-start.6
  179.4 0.7 copy-start.2
  182.1 2.0 %copy-start = (bf16[2,4,64,512]{3,2,1,0:T(8,128)(2,1)S(1)}, bf16[2,4,64,512]{3,2,1,0:T(8,128)(2,1)}, u32[]{:S(2)}) copy-start(bf16[2,4,64,512]{3,2,1,0:T(8,128)(2,1)} %get-tuple-element.18) | copy-start | bytes 1572868
  182.1 2.0 %copy-start.1 = (bf16[2,4,64,512]{3,2,1,0:T(8,128)(2,1)S(1)}, bf16[2,4,64,512]{3,2,1,0:T(8,128)(2,1)}, u32[]{:S(2)}) copy-start(bf16[2,4,64,512]{3,2,1,0:T(8,128)(2,1)} %get-tuple-element.19) | copy-start | bytes 1572868
